TPU v7x, 128 devices: a whole 4x4x4 slice. The times are simulated.
128 devices in a mesh: row: 16 (over y, x), col: 8 (over z, core).
Axes of the slice: x: 4, y: 4, z: 4, core: 2. Of those that a mesh axis runs over, the one named last changes fastest.
Arguments:
- offsets: float32 [3, 131072], P(None, ('row', 'col')), may hold values from 0 to 31.5
- measured: float32 [3, 131072], P(None, ('row', 'col')), may hold values from -6 to 6
- block_brick: int32 [1024], P(('row', 'col')), may hold values from 0 to 127
- block_count: int32 [1024], P(('row', 'col')), may hold values from 32 to 128, as said below
Outputs:
- vort_spec: float32 [2, 3, 32, 1024, 1024], P(None, None, 'col', 'row')
- residual: float32 [3, 131072], P(None, ('row', 'col'))
Inputs may be any that keep to these rules, and one draw needn't show every extreme that they name: `block_brick`: brick of each block inside the x slab of the block's device row, numbered bx * 32 * 2 + by * 2 + bz. `block_count`: live slots are the first ones of a block; some block is full.
All inputs are finite; a program needn't handle non-finite values.
Results may differ from a plain program's by a relative error of at most 0.0003.
Values sent between devices are 32-bit elements; how exact they have to be, the bound alone decides.
No kernel may reach another device: no remote copies, remote signals or barrier semaphores. Data moves between devices by JAX's collectives and lax.ppermute only.
A program may use at most 192 MiB of HBM per device.

v0:
```python
import math

import jax
import jax.numpy as jnp
from jax import lax
from jax.sharding import PartitionSpec as P

NX = 1024
NY = 1024
NZ = 64
BRICK = 32


TWO_PI = 2.0 * math.pi
HIGHEST = lax.Precision.HIGHEST


def shifted(value, axis, steps):
    count = lax.axis_size(axis)
    pairs = [(source, (source + steps) % count) for source in range(count)]
    return lax.ppermute(value, axis, pairs)


def phase_table(first_index, second_index, modulus):
    angle = TWO_PI * (first_index * second_index % modulus).astype(jnp.float32) / modulus
    return (jnp.cos(angle), jnp.sin(angle))


def complex_block(cosine, sine):
    return jnp.stack([jnp.stack([cosine, sine], 1), jnp.stack([-sine, cosine], 1)], 0)


def rotate(middle, cosine, sine):
    return jnp.stack([middle[0] * cosine - middle[1] * sine, middle[0] * sine + middle[1] * cosine])


def forward_last(field):
    length = field.shape[-1]
    outer = length // 128
    inner = 128
    shape = field.shape
    parts = field.reshape(shape[:-1] + (outer, inner))
    outer_ids = jnp.arange(outer, dtype=jnp.int32)
    inner_ids = jnp.arange(inner, dtype=jnp.int32)
    cosine, sine = phase_table(outer_ids[:, None], outer_ids[None, :], outer)
    middle = jnp.einsum(
        "r...an,rasb->s...bn", parts, complex_block(cosine, -sine), precision=HIGHEST
    )
    cosine, sine = phase_table(outer_ids[:, None], inner_ids[None, :], length)
    middle = rotate(middle, cosine, -sine)
    cosine, sine = phase_table(inner_ids[:, None], inner_ids[None, :], inner)
    result = jnp.einsum(
        "r...bn,rnsm->s...bm", middle, complex_block(cosine, -sine), precision=HIGHEST
    )
    return result.reshape(shape)


def inverse_last(spectrum):
    length = spectrum.shape[-1]
    outer = length // 128
    inner = 128
    shape = spectrum.shape
    parts = spectrum.reshape(shape[:-1] + (outer, inner))
    outer_ids = jnp.arange(outer, dtype=jnp.int32)
    inner_ids = jnp.arange(inner, dtype=jnp.int32)
    cosine, sine = phase_table(inner_ids[:, None], inner_ids[None, :], inner)
    middle = jnp.einsum(
        "r...bm,rmsn->s...bn", parts, complex_block(cosine, sine), precision=HIGHEST
    )
    cosine, sine = phase_table(outer_ids[:, None], inner_ids[None, :], length)
    middle = rotate(middle, cosine, sine)
    cosine, sine = phase_table(outer_ids[:, None], outer_ids[None, :], outer)
    result = jnp.einsum(
        "r...bn,rbsa->s...an", middle, complex_block(cosine, sine), precision=HIGHEST
    )
    return result.reshape(shape)


def frequency(position, length):
    return position % 128 * (length // 128) + position // 128


def wavenumber(index, length):
    signed = jnp.where(index < length // 2, index, index - length)
    return TWO_PI * signed.astype(jnp.float32) / length


def biot_savart(spectrum, row_index, col_index):
    modes_z, rows_y, length_x = spectrum.shape[2:]
    index_z = col_index * modes_z + jnp.arange(modes_z, dtype=jnp.int32)
    index_y = frequency(row_index * rows_y + jnp.arange(rows_y, dtype=jnp.int32), NY)
    index_x = frequency(jnp.arange(length_x, dtype=jnp.int32), NX)
    wave_z = (TWO_PI * index_z.astype(jnp.float32) / NZ)[:, None, None]
    wave_y = wavenumber(index_y, NY)[None, :, None]
    wave_x = wavenumber(index_x, NX)[None, None, :]
    valid = (index_y != NY // 2)[None, :, None] & (index_x != NX // 2)[None, None, :]
    anchor = (
        (index_z == 0)[:, None, None]
        & (index_y == 0)[None, :, None]
        & (index_x == 0)[None, None, :]
    )
    valid = valid & jnp.logical_not(anchor)
    squared = wave_x * wave_x + wave_y * wave_y + wave_z * wave_z
    inverse = jnp.where(valid, 1.0 / jnp.where(valid, squared, 1.0), 0.0)

    def crossed(vector):
        return [
            wave_y * vector[2] - wave_z * vector[1],
            wave_z * vector[0] - wave_x * vector[2],
            wave_x * vector[1] - wave_y * vector[0],
        ]

    real_part = jnp.stack([-value * inverse for value in crossed(spectrum[1])])
    imag_part = jnp.stack([value * inverse for value in crossed(spectrum[0])])
    return jnp.stack([real_part, imag_part])


def spectral_norm(spectrum, col_index):
    modes_z = spectrum.shape[2]
    index_z = col_index * modes_z + jnp.arange(modes_z, dtype=jnp.int32)
    weight = jnp.where(index_z == 0, 1.0, 2.0) / float(NX * NY * NZ)
    return jnp.sum(weight[:, None, None] * jnp.sum(spectrum * spectrum, axis=(0, 1)))


def total(value):
    return lax.psum(value, ("row", "col"))


def point_geometry(offsets_all, bricks_all, counts_all):
    slot_count = offsets_all.shape[1]
    slot_index = jnp.arange(slot_count, dtype=jnp.int32)
    brick = jnp.repeat(bricks_all, 128)
    count = jnp.repeat(counts_all, 128)
    live = (slot_index % 128 < count).astype(jnp.float32)
    bricks_y = NY // BRICK
    bricks_z = NZ // BRICK
    brick_x = brick // (bricks_y * bricks_z)
    brick_y = brick // bricks_z % bricks_y
    brick_z = brick % bricks_z
    lower = jnp.floor(offsets_all)
    fraction = offsets_all - lower
    cell = lower.astype(jnp.int32)
    cell_x = BRICK * brick_x + cell[0]
    cell_y = (BRICK * brick_y + cell[1]) % NY
    next_y = (cell_y + 1) % NY
    cell_z = (BRICK * brick_z + cell[2]) % NZ
    next_z = (cell_z + 1) % NZ
    columns = jnp.concatenate(
        [
            cell_x * NY + cell_y,
            cell_x * NY + next_y,
            (cell_x + 1) * NY + cell_y,
            (cell_x + 1) * NY + next_y,
        ]
    )
    across = jnp.concatenate(
        [
            (1.0 - fraction[0]) * (1.0 - fraction[1]),
            (1.0 - fraction[0]) * fraction[1],
            fraction[0] * (1.0 - fraction[1]),
            fraction[0] * fraction[1],
        ]
    )
    return (live, columns, across, cell_z, next_z, 1.0 - fraction[2], fraction[2])


def depth_factors(cell_z, next_z, lower_weight, upper_weight, col_index, modes_z):
    index_z = col_index * modes_z + jnp.arange(modes_z, dtype=jnp.int32)
    near_cos, near_sin = phase_table(index_z[:, None], cell_z[None, :], NZ)
    far_cos, far_sin = phase_table(index_z[:, None], next_z[None, :], NZ)
    cos_sum = lower_weight[None] * near_cos + upper_weight[None] * far_cos
    sin_sum = lower_weight[None] * near_sin + upper_weight[None] * far_sin
    scale = (jnp.where(index_z == 0, 1.0, 2.0) / float(NX * NY * NZ))[:, None]
    return (scale * cos_sum, scale * sin_sum, cos_sum, -sin_sum)


def interpolate(field, columns, across, factor_real, factor_imag):
    channels = field.shape[0] * field.shape[1] * field.shape[2]
    following = shifted(field[:, :, :, 0:1, :], "row", -1)
    extended = jnp.concatenate([field, following], 3).reshape(channels, -1)
    picked = extended[:, columns] * across[None]
    gathered = jnp.sum(picked.reshape(channels, 4, -1), axis=1)
    gathered = gathered.reshape(field.shape[:3] + (-1,))
    return jnp.sum(gathered[0] * factor_real[None] - gathered[1] * factor_imag[None], axis=1)


def spread(values, columns, across, spread_real, spread_imag, planes):
    modes_z = spread_real.shape[0]
    channels = 6 * modes_z
    source = jnp.stack(
        [values[:, None, :] * spread_real[None], values[:, None, :] * spread_imag[None]]
    )
    source = source.reshape(channels, -1)
    weighted = jnp.concatenate([source, source, source, source], 1) * across[None]
    flat = jnp.zeros((channels, (planes + 1) * NY), jnp.float32).at[:, columns].add(weighted)
    field = flat.reshape((2, 3, modes_z, planes + 1, NY))
    spill = shifted(field[:, :, :, planes:, :], "row", 1)
    field = field[:, :, :, :planes, :]
    return field.at[:, :, :, 0:1, :].add(spill)


def forward(field):
    swapped = jnp.swapaxes(forward_last(field), 3, 4)
    return forward_last(lax.all_to_all(swapped, "row", split_axis=3, concat_axis=4, tiled=True))


def backward(spectrum):
    swapped = jnp.swapaxes(inverse_last(spectrum), 3, 4)
    return inverse_last(lax.all_to_all(swapped, "row", split_axis=3, concat_axis=4, tiled=True))


def body(offsets, measured, block_brick, block_count):
    row_index = lax.axis_index("row")
    col_index = lax.axis_index("col")
    col_count = lax.axis_size("col")
    row_count = lax.axis_size("row")
    slot_count = offsets.shape[1]
    modes_z = NZ // 2 // col_count
    planes = NX // row_count
    offsets_all, measured_all = (
        lax.all_gather(offsets, "col", axis=1, tiled=True),
        lax.all_gather(measured, "col", axis=1, tiled=True),
    )
    bricks_all, counts_all = (
        lax.all_gather(block_brick, "col", axis=0, tiled=True),
        lax.all_gather(block_count, "col", axis=0, tiled=True),
    )
    live, columns, across, cell_z, next_z, lower_weight, upper_weight = point_geometry(
        offsets_all, bricks_all, counts_all
    )
    factor_real, factor_imag, spread_real, spread_imag = depth_factors(
        cell_z, next_z, lower_weight, upper_weight, col_index, modes_z
    )
    own_live = lax.dynamic_slice_in_dim(live, col_index * slot_count, slot_count, 0)
    residual_all = measured_all * live[None]
    residual_own = lax.dynamic_slice_in_dim(residual_all, col_index * slot_count, slot_count, 1)
    gradient = biot_savart(
        forward(spread(residual_all, columns, across, spread_real, spread_imag, planes)),
        row_index,
        col_index,
    )
    gamma = total(spectral_norm(gradient, col_index))
    field = backward(biot_savart(gradient, row_index, col_index))
    partial_velocity = interpolate(field, columns, across, factor_real, factor_imag)
    velocity_all = lax.psum(partial_velocity, "col")
    velocity_own = lax.dynamic_slice_in_dim(velocity_all, col_index * slot_count, slot_count, 1)
    curvature = total(jnp.sum(velocity_own * velocity_own * own_live[None]))
    step_length = gamma / curvature
    vorticity = step_length * gradient
    residual_own = residual_own - step_length * velocity_own * own_live[None]
    return (vorticity * (1.0 / math.sqrt(float(NX * NY * NZ))), residual_own)


def solution(mesh):
    in_specs = (
        P(None, ("row", "col")),
        P(None, ("row", "col")),
        P(("row", "col")),
        P(("row", "col")),
    )
    out_specs = (P(None, None, "col", "row", None), P(None, ("row", "col")))
    return jax.shard_map(body, mesh=mesh, in_specs=in_specs, out_specs=out_specs, check_vma=False)
```

profile of v0, /device:TPU:1, one launch (start us, length us, event | category | flops | bytes accessed | tf_op | source)
XLA Modules:
  0.0 1084.4 jit_solution(18302114396789419576)
XLA Ops:
  10.8 9.8 all-reduce.2
  20.7 15.0 %all_gather.13 = f32[3,8192]{1,0:T(4,128)S(1)} all-gather(f32[3,1024]{1,0:T(4,128)} %param.6), channel_id=1, replica_groups=mesh['row'=16,'col'=8] {'col'}, dimensions={1}, use_global_device_ids=true | all-gather | bytes 110592 | tf_op jit(solution)/shard_map/all_gather | solution.py:221
  35.7 12.9 %all_gather.14 = f32[3,8192]{1,0:T(4,128)S(1)} all-gather(f32[3,1024]{1,0:T(4,128)} %param.7), channel_id=1, replica_groups=mesh['row'=16,'col'=8] {'col'}, dimensions={1}, use_global_device_ids=true | all-gather | bytes 110592 | tf_op jit(solution)/shard_map/all_gather | solution.py:222
  57.5 8.9 copy.155
  66.6 188.0 %scatter_custom_fusion = f32[24,66560]{0,1:T(8,128)} fusion(s32[32768]{0:T(1024)S(1)} %bitcast.273, f32[32768,24]{1,0:T(8,128)} %copy.155, f32[]{:T(128)} %constant.327.clone.1), kind=kCustom, calls=%fused_computation.2 | custom fusion | flops 786432 | bytes 6390272 | tf_op jit(solution)/shard_map/scatter-add | solution.py:195
  254.5 20.3 %copy.156 = f32[24,66560]{1,0:T(8,128)} copy(f32[24,66560]{0,1:T(8,128)} %scatter_custom_fusion) | data formatting | bytes 12779520 | tf_op jit(solution)/shard_map/scatter-add | solution.py:195
  274.8 7.1 reshape.1593
  285.0 6.6 slice.186
  297.4 4.3 copy.218
  301.7 6.0 fusion.22
  309.2 5.8 fusion.25
  318.6 12.2 %copy.160 = f32[2,3,4,1024,64]{4,2,1,0,3:T(4,128)} copy(f32[2,3,4,1024,64]{3,4,2,1,0:T(8,128)} %bitcast.263) | data formatting | bytes 12582912 | tf_op jit(solution)/shard_map/transpose | solution.py:203
  330.8 17.9 %reshape.1651 = f32[16,1,98304]{2,1,0:T(1,128)} reshape(f32[1024,2,3,4,64]{4,3,2,1,0:T(4,128)} %bitcast.253) | data formatting | bytes 12582912
  348.7 6.5 all-to-all-start
  355.9 92.4 %all-to-all-done = f32[16,1,98304]{2,1,0:T(1,128)} async-done(((f32[16,1,98304]{2,1,0:T(1,128)}), f32[16,1,98304]{2,1,0:T(1,128)}, u32[]{:S(2)}, u32[]{:S(2)}) %all-to-all-start) | async-done | bytes 6291488 | tf_op jit(solution)/shard_map/all_to_all | solution.py:204
  448.8 19.5 %reduce.2 = f32[16,98304]{1,0:T(8,128)} reduce(f32[16,1,98304]{2,1,0:T(1,128)} %all-to-all-done, f32[]{:T(128)} %broadcast.3757), dimensions={1}, to_apply=%all_to_all.22.reduce_sub_computation | reduce | bytes 12582916 | tf_op jit(solution)/shard_map/all_to_all | solution.py:204
  468.3 17.8 %reshape.1652 = f32[1024,2,3,4,64]{4,3,2,1,0:T(4,128)} reshape(f32[16,98304]{1,0:T(8,128)} %reduce.2) | data formatting | bytes 12582912
  486.1 16.4 %copy.266 = f32[2,3,4,16,64,64]{5,3,0,4,2,1:T(8,128)} copy(f32[2,3,4,16,64,64]{5,2,1,0,4,3:T(4,128)} %bitcast.254) | data formatting | bytes 12582912 | tf_op jit(solution)/shard_map/all_to_all | solution.py:204
  502.5 11.1 %reshape.1633 = f32[2,3,4,64,8,128,1]{5,4,0,3,2,1,6:T(8,128)} reshape(f32[2,3,4,64,16,64]{5,4,0,3,2,1:T(8,128)} %bitcast.255) | data formatting | bytes 12582912 | tf_op jit(solution)/shard_map/reshape | solution.py:42
  513.6 8.1 convolution_bitcast_fusion
  523.2 5.6 fusion.28
  534.2 8.4 fusion.31
  543.4 7.8 fusion.34
  551.2 10.1 copy.211
  561.3 17.9 %reshape.1653 = f32[16,1,98304]{2,1,0:T(1,128)} reshape(f32[1024,2,3,4,64]{4,3,2,1,0:T(4,128)} %bitcast.256) | data formatting | bytes 12582912
  579.2 5.2 all-to-all-start.1
  593.4 4.6 negate_multiply_fusion.8
  598.0 7.3 subtract_multiply_fusion.7
  605.3 4.2 maximum_bitcast_fusion.2
  609.5 4.2 maximum_bitcast_fusion.1
  613.7 61.7 %all-to-all-done.1 = f32[16,1,98304]{2,1,0:T(1,128)} async-done(((f32[16,1,98304]{2,1,0:T(1,128)}), f32[16,1,98304]{2,1,0:T(1,128)}, u32[]{:S(2)}, u32[]{:S(2)}) %all-to-all-start.1) | async-done | bytes 6291488 | tf_op jit(solution)/shard_map/all_to_all | solution.py:209
  675.4 19.5 %reduce.3 = f32[16,98304]{1,0:T(8,128)} reduce(f32[16,1,98304]{2,1,0:T(1,128)} %all-to-all-done.1, f32[]{:T(128)} %broadcast.3757), dimensions={1}, to_apply=%all_to_all.25.reduce_sub_computation | reduce | bytes 12582916 | tf_op jit(solution)/shard_map/all_to_all | solution.py:209
  694.8 17.8 %reshape.1654 = f32[1024,2,3,4,64]{4,3,2,1,0:T(4,128)} reshape(f32[16,98304]{1,0:T(8,128)} %reduce.3) | data formatting | bytes 12582912
  712.6 16.4 %copy.265 = f32[2,3,4,16,64,64]{5,3,4,2,1,0:T(8,128)} copy(f32[2,3,4,16,64,64]{5,2,1,0,4,3:T(4,128)} %bitcast.257) | data formatting | bytes 12582912 | tf_op jit(solution)/shard_map/all_to_all | solution.py:209
  729.0 11.2 %reshape.1598 = f32[2,3,4,64,8,128]{5,4,3,2,1,0:T(8,128)} reshape(f32[2,3,4,64,16,64]{5,4,3,2,1,0:T(8,128)} %bitcast.258) | data formatting | bytes 12582912 | tf_op jit(solution)/shard_map/reshape | solution.py:63
  740.2 8.7 fusion.37
  749.8 8.0 fusion.40
  757.7 7.1 reshape.1599
  767.9 6.2 multiply_reduce_fusion.1
  775.5 6.3 copy.219
  781.9 17.7 %copy.183 = f32[24,66560]{0,1:T(8,128)} copy(f32[24,66560]{1,0:T(8,128)} %bitcast.260) | data formatting | bytes 12779520 | tf_op jit(solution)/shard_map/reshape | solution.py:180
  799.6 118.9 %gather_fusion = f32[32768,24]{1,0:T(8,128)} fusion(f32[24,66560]{0,1:T(8,128)} %copy.183, s32[32768]{0:T(1024)S(1)} %broadcast_clamp_fusion), kind=kCustom, calls=%fused_computation | custom fusion | bytes 6422528 | tf_op jit(solution)/shard_map/gather | solution.py:181
  918.5 7.8 multiply_reduce_fusion
  926.4 4.7 fusion.154
  939.1 55.1 %all-reduce.6.cloned.1.call-done = f32[3,8192]{1,0:T(4,128)} async-done(((f32[3,8192]{1,0:T(4,128)}), f32[3,8192]{1,0:T(4,128)}) %all-reduce.6.cloned.1.call-update) | async-done | bytes 98320 | tf_op jit(solution)/shard_map/psum | solution.py:245
  995.5 67.3 %all-reduce.3 = (f32[]{:T(128)}, f32[]{:T(128)}) all-reduce(f32[]{:T(128)} %multiply_reduce_fusion.2, f32[]{:T(128)} %multiply_reduce_fusion.3), channel_id=1, replica_groups=mesh['row'=16,'col'=8] {'row','col'}, use_global_device_ids=true, to_apply=%region_3.4 | all-reduce | flops 2 | bytes 16 | tf_op jit(solution)/shard_map/psum | solution.py:126
  1064.1 5.2 multiply_multiply_fusion
  1069.4 6.3 copy.186
  (154 shorter events, 59.3 us)
Async XLA Ops:
  7.2 59.2 %copy-start.26 = (f32[4]{0:T(128)}, f32[4]{0:T(128)S(1)}, u32[]{:S(2)}) copy-start(f32[4]{0:T(128)S(1)} %get-tuple-element.101) | copy-start | bytes 52
  7.2 523.3 %copy-start.18 = (f32[4]{0:T(128)}, f32[4]{0:T(128)S(1)}, u32[]{:S(2)}) copy-start(f32[4]{0:T(128)S(1)} %get-tuple-element.100) | copy-start | bytes 52
  20.7 31.8 %copy-start.10 = (f32[8192]{0:T(1024)}, f32[8192]{0:T(1024)S(1)}, u32[]{:S(2)}) copy-start(f32[8192]{0:T(1024)S(1)} %fusion.93) | copy-start | bytes 98308
  49.5 3.1 copy-start.5
  54.0 0.6 copy-start.3
  66.5 188.0 %copy-start.8 = (s32[32768,1]{0,1:T(1,128)}, s32[32768,1]{0,1:T(1,128)S(1)}, u32[]{:S(2)}) copy-start(s32[32768,1]{0,1:T(1,128)S(1)} %compare_select_fusion) | copy-start | bytes 393220
  283.1 9.5 collective-permute-start
  348.7 99.6 %all-to-all-start = ((f32[16,1,98304]{2,1,0:T(1,128)}), f32[16,1,98304]{2,1,0:T(1,128)}, u32[]{:S(2)}, u32[]{:S(2)}) async-start(f32[16,1,98304]{2,1,0:T(1,128)} %reshape.1651), calls=%async_computation | async-start | bytes 12582912 | tf_op jit(solution)/shard_map/all_to_all | solution.py:204
  355.3 188.1 %copy-start.15 = (f32[1,8,2,8]{1,3,0,2:T(8,128)}, f32[1,8,2,8]{1,3,0,2:T(8,128)S(1)}, u32[]{:S(2)}) copy-start(f32[1,8,2,8]{1,3,0,2:T(8,128)S(1)} %copy.171) | copy-start | bytes 1540
  355.4 175.2 %copy-start.22 = (f32[4]{0:T(128)}, f32[4]{0:T(128)S(1)}, u32[]{:S(2)}) copy-start(f32[4]{0:T(128)S(1)} %fusion.151) | copy-start | bytes 52
  355.4 112.8 %copy-start.28 = (f32[64]{0:T(128)}, f32[64]{0:T(128)S(1)}, u32[]{:S(2)}) copy-start(f32[64]{0:T(128)S(1)} %get-tuple-element.97) | copy-start | bytes 772
  355.4 175.1 %copy-start.20 = (f32[64]{0:T(128)}, f32[64]{0:T(128)S(1)}, u32[]{:S(2)}) copy-start(f32[64]{0:T(128)S(1)} %get-tuple-element.96) | copy-start | bytes 772
  355.5 112.8 %copy-start.29 = (pred[64]{0:T(512)(128)(4,1)}, pred[64]{0:T(512)(128)(4,1)S(1)}, u32[]{:S(2)}) copy-start(pred[64]{0:T(512)(128)(4,1)S(1)} %get-tuple-element.98) | copy-start | bytes 196
  355.7 174.9 %copy-start.24 = (pred[4,64]{1,0:T(4,128)(4,1)}, pred[4,64]{1,0:T(4,128)(4,1)S(1)}, u32[]{:S(2)}) copy-start(pred[4,64]{1,0:T(4,128)(4,1)S(1)} %broadcast_and_fusion.2) | copy-start | bytes 772
  528.8 4.3 copy-start
  533.1 1.0 copy-start.11
  533.1 1.0 copy-start.13
  579.2 5.8 copy-start.4
  579.2 8.6 copy-start.9
  579.2 96.2 %all-to-all-start.1 = ((f32[16,1,98304]{2,1,0:T(1,128)}), f32[16,1,98304]{2,1,0:T(1,128)}, u32[]{:S(2)}, u32[]{:S(2)}) async-start(f32[16,1,98304]{2,1,0:T(1,128)} %reshape.1653), calls=%async_computation.1 | async-start | bytes 12582912 | tf_op jit(solution)/shard_map/all_to_all | solution.py:209
  584.3 409.9 %all-reduce.6.cloned.1.call-start = ((), (), s32[]{:S(2)}) async-start(), calls=%async_computation.2 | async-start | bytes 262144 | tf_op jit(solution)/shard_map/psum | solution.py:245
  587.8 4.3 copy-start.2
  589.6 3.8 copy-start.19
  589.6 3.8 copy-start.21
  589.6 3.8 copy-start.23
  589.6 3.8 copy-start.25
  589.6 3.8 copy-start.30
  729.0 11.2 %copy-start.12 = (f32[1,128,2,128]{3,1,2,0:T(8,128)S(1)}, f32[1,128,2,128]{3,1,2,0:T(8,128)}, u32[]{:S(2)}) copy-start(f32[1,128,2,128]{3,1,2,0:T(8,128)} %get-tuple-element.67) | copy-start | bytes 393220
  729.0 11.2 %copy-start.14 = (f32[1,128,2,128]{3,1,2,0:T(8,128)S(1)}, f32[1,128,2,128]{3,1,2,0:T(8,128)}, u32[]{:S(2)}) copy-start(f32[1,128,2,128]{3,1,2,0:T(8,128)} %get-tuple-element.85) | copy-start | bytes 393220
  748.9 0.9 copy-start.16
  764.8 9.3 copy-start.1
  766.2 8.0 collective-permute-start.1
  931.1 6.0 copy-start.6
  931.1 6.0 copy-start.7
  931.1 7.1 copy-start.27
  931.1 63.1 %copy-start.17 = (f32[1024]{0:T(1024)S(1)}, f32[1024]{0:T(1024)}, u32[]{:S(2)}) copy-start(f32[1024]{0:T(1024)} %dynamic_slice.10) | copy-start | bytes 12292
Sparse Core Ops, SparseCore 0:
  938.3 55.8 all-reduce.5
where the time goes:
time: 1100 us; the launch traced here: 1080 us
  local copies, waits for them, and re-layouts  385 us (35%)
  other arithmetic  295 us (27%)
  waiting for transfers between devices  209 us (19%)
  blocking collectives  105 us (10%)
  matrix products  58.3 us (5%)
  between operations  17.3 us (2%)
  starting transfers between devices  14.7 us (1%)
    scatter-add x1, other arithmetic, spread(): jnp.zeros((channels, (planes + 1) * NY), jnp.float32).at[:, columns]  188 us
    gather x1, local copies, waits for them, and re-layouts, interpolate(): picked = extended[:, columns] * across[None]  119 us
    all_to_all x1, waiting for transfers between devices, forward(): lax.all_to_all(swapped, 'row', split_axis=3, concat_axis=4, tiled=True)  92.4 us
    unnamed x72, local copies, waits for them, and re-layouts  92.1 us
    psum x1, blocking collectives, total(): return lax.psum(value, ('row', 'col'))  67.3 us
    all_to_all x1, waiting for transfers between devices, backward(): lax.all_to_all(swapped, 'row', split_axis=3, concat_axis=4, tiled=True)  61.7 us
    psum x1, waiting for transfers between devices, body(): velocity_all = lax.psum(partial_velocity, 'col')  55.1 us
  transfers between devices with their start and end apart: 5, of which 3 were waited for; matrix products, arithmetic and copies ran while one was open for 4% of the time, Pallas kernels for 0%

commit v1 on v0

v1 whole, which is shorter than its diff:
```python
import math

import jax
import jax.numpy as jnp
import ml_dtypes
import numpy as np
from jax import lax
from jax.experimental import pallas as pl
from jax.experimental.pallas import tpu as pltpu
from jax.sharding import PartitionSpec as P

NX = 1024
NY = 1024
NZ = 64
CELLS = float(NX * NY * NZ)
TWO_PI = 2.0 * math.pi
F32 = jnp.float32
BF16 = jnp.bfloat16
VMEM_LIMIT = 56 * 1024 * 1024
VMEM = pl.BlockSpec(memory_space=pltpu.VMEM)
SMEM = pl.BlockSpec(memory_space=pltpu.SMEM)


def halves(table):
    table = table.astype(np.float32)
    high = table.astype(ml_dtypes.bfloat16)
    low = (table - high.astype(np.float32)).astype(ml_dtypes.bfloat16)
    return np.stack([high, low])


def table_y():
    first = np.arange(8)[:, None, None]
    angle = TWO_PI * ((np.arange(128)[None, :, None] * 8 + first) * np.arange(128)[None, None, :] % 1024) / 1024
    cosine, sine = np.cos(angle), np.sin(angle)
    return np.concatenate([np.concatenate([cosine, sine], 2), np.concatenate([-sine, cosine], 2)], 1)


def table_x():
    result = np.zeros((8, 2, 2, 64, 2, 64, 2))
    inner = np.arange(64)
    for first in range(8):
        for upper in range(2):
            wave = 16 * np.arange(64) + first + 8 * upper
            angle = TWO_PI * (inner[:, None] * wave[None, :] % 1024) / 1024
            result[first, upper, 0, :, 0, :, upper] = np.cos(angle)
            result[first, upper, 1, :, 0, :, upper] = np.sin(angle)
            result[first, upper, 0, :, 1, :, upper] = -np.sin(angle)
            result[first, upper, 1, :, 1, :, upper] = np.cos(angle)
    return result.reshape(8, 256, 256)


def split(value):
    high = value.astype(BF16)
    return high, (value - high.astype(F32)).astype(BF16)


def mul(left, right):
    return jnp.dot(left, right, preferred_element_type=F32)


def mul_t(left, right):
    return lax.dot_general(left, right, (((1,), (1,)), ((), ())), preferred_element_type=F32)


def small_dft(values, sign):
    count = len(values)
    if count == 1:
        return values
    even = small_dft(values[0::2], sign)
    odd = small_dft(values[1::2], sign)
    low, high = [], []
    for k in range(count // 2):
        real, imag = odd[k]
        if k > 0:
            if 4 * k == count:
                real, imag = (-imag, real) if sign > 0 else (imag, -real)
            elif 8 * k == count:
                root = math.sqrt(0.5)
                if sign > 0:
                    real, imag = (real - imag) * root, (real + imag) * root
                else:
                    real, imag = (real + imag) * root, (imag - real) * root
            elif 8 * k == 3 * count:
                root = math.sqrt(0.5)
                if sign > 0:
                    real, imag = (real + imag) * -root, (real - imag) * root
                else:
                    real, imag = (imag - real) * root, (real + imag) * -root
            else:
                cosine = math.cos(TWO_PI * k / count)
                sine = sign * math.sin(TWO_PI * k / count)
                real, imag = real * cosine - imag * sine, real * sine + imag * cosine
        low.append((even[k][0] + real, even[k][1] + imag))
        high.append((even[k][0] - real, even[k][1] - imag))
    return low + high


def hat(distance):
    return jnp.maximum(1.0 - jnp.abs(distance), 0.0)


def ramp(shape, axis):
    return lax.broadcasted_iota(jnp.int32, shape, axis).astype(F32)


def brick_place(brick):
    return brick // 64, brick // 2 % 32, brick % 2


def block_points(points, block):
    lane = pl.multiple_of(block % 8 * 128, 128)
    return points[block // 8, :, pl.ds(lane, 128)]


def depth_wave(points, meta, depth):
    index = lax.broadcasted_iota(jnp.int32, (8, 128), 0)
    mode = 4 * meta[65] + 2 * (index // 4) + index % 2
    turn = 16 * (index // 2 % 2)

    def wave(cell):
        angle = (mode * cell + turn) & 63
        value = (jnp.abs(angle - 32) - 16).astype(F32) * (math.pi / 32.0)
        square = value * value
        total = -1.0 / 39916800.0
        for factor in (1.0 / 362880.0, -1.0 / 5040.0, 1.0 / 120.0, -1.0 / 6.0, 1.0):
            total = total * square + factor
        return total * value

    def step(block, carry):
        height = block_points(points, block)[2:3]
        lower = jnp.floor(height)
        part = height - lower
        cell = lower.astype(jnp.int32) + 32 * (meta[block] % 2)
        depth[block] = (1.0 - part) * wave(cell) + part * wave(cell + 1)
        return carry

    lax.fori_loop(0, 64, step, 0, unroll=4)


def edge_kernel(meta, points, depth, edge):
    depth_wave(points, meta, depth)
    edge[...] = jnp.zeros_like(edge)
    cells = ramp((256, 128), 0)

    def step(block, carry):
        place_x, place_y, _ = brick_place(meta[block])

        @pl.when(place_x == 1)
        def _():
            point = block_points(points, block)
            across = jnp.maximum(point[0:1] - 31.0, 0.0)
            waves = depth[block] * across
            source = jnp.concatenate([waves * point[3 + c : 4 + c] for c in range(3)], 0)
            weight = hat(cells - (32 * (place_y % 4)).astype(F32) - point[1:2])
            source_high, source_low = split(source)
            weight_high, weight_low = split(weight)
            value = (
                mul_t(source_high, weight_high) + mul_t(source_low, weight_high) + mul_t(source_high, weight_low)
            )
            lane = pl.multiple_of(place_y // 4 * 128, 128)
            edge[:, pl.ds(lane, 256)] += value

        return carry

    lax.fori_loop(0, 64, step, 0)
    edge[:, 0:128] += edge[:, 1024:1152]


def slab_weights(point, waves, place_x):
    across = hat(ramp((64, 128), 0) - (32 * place_x).astype(F32) - point[0:1])
    return jnp.concatenate([waves[i : i + 1] * across for i in range(8)], 0)


def spread_kernel(meta, points, depth, edge, table, out, field, parts):
    field[...] = jnp.zeros_like(field)

    def step(block, carry):
        place_x, place_y, _ = brick_place(meta[block])
        point = block_points(points, block)
        weight_high, weight_low = split(slab_weights(point, depth[block], place_x))
        along = hat(ramp((40, 128), 0) - point[1:2])
        source = jnp.concatenate([along * point[3 + c : 4 + c] for c in range(3)], 0)
        source_high, source_low = split(source)
        both = mul_t(jnp.concatenate([source_high, source_low], 0), weight_high)
        value = both[:120] + both[120:] + mul_t(source_high, weight_low)
        row = pl.multiple_of(place_y * 32, 32)
        for c in range(3):
            field[c, pl.ds(row, 40), :] += value[40 * c : 40 * c + 40]
        return carry

    lax.fori_loop(0, 64, step, 0, unroll=2)
    lane = lax.broadcasted_iota(jnp.int32, (16, 512), 1)
    place = (lane == 64 * (lax.broadcasted_iota(jnp.int32, (16, 512), 0) % 8)).astype(BF16)
    for c in range(3):
        field[c, 0:1, :] += field[c, 1024:1025, :]
        high, low = split(edge[8 * c : 8 * c + 8, :])
        columns = jnp.concatenate([high.astype(F32), low.astype(F32)], 0).T.astype(BF16)
        field[c, 0:1024, :] += mul(columns, place)

    def outer(tile, carry):
        row = pl.multiple_of(tile * 8, 8)
        for c in range(3):
            for p in range(2):
                lane = 256 * p
                values = [
                    (
                        field[c, pl.ds(128 * a + row, 8), lane : lane + 128],
                        field[c, pl.ds(128 * a + row, 8), lane + 128 : lane + 256],
                    )
                    for a in range(8)
                ]
                for k, (real, imag) in enumerate(small_dft(values, -1)):
                    at = 128 * (2 * c + p)
                    parts[k, pl.ds(row, 8), at : at + 128] = real
                    parts[k, pl.ds(128 + row, 8), at : at + 128] = imag
        return carry

    lax.fori_loop(0, 16, outer, 0)

    def inner(k, carry):
        high, low = split(parts[k])
        value = mul(table[0, k], high) + mul(table[1, k], high) + mul(table[0, k], low)
        for half in range(2):
            for p in range(2):
                for c in range(3):
                    for part in range(2):
                        row = 128 * part + 64 * half
                        at = 128 * (2 * c + p)
                        out[2 * k + half, p, c, part] = value[row : row + 64, at : at + 128]
        return carry

    lax.fori_loop(0, 8, inner, 0)


def spectrum_kernel(meta, received, table, table_back, spectrum, out, norm, parts, back):
    pair = pl.program_id(0)
    row = meta[64]
    lane = lax.broadcasted_iota(jnp.int32, (8, 128), 1)
    lower = lane < 64

    def turned(value):
        return pltpu.roll(value, 64, 1)

    def outer(tile, carry):
        at = pl.multiple_of(tile * 8, 8)
        for c in range(3):
            values = [
                (received[s, 0, c, 0, pl.ds(at, 8), :], received[s, 0, c, 1, pl.ds(at, 8), :]) for s in range(16)
            ]
            for k, (real, imag) in enumerate(small_dft(values, -1)):
                to = 128 * (k // 8)
                parts[k % 8, pl.ds(128 * c + at, 8), to : to + 128] = jnp.where(lower, real, turned(imag))
                parts[k % 8, pl.ds(128 * c + 64 + at, 8), to : to + 128] = jnp.where(lower, turned(real), imag)
        return carry

    lax.fori_loop(0, 8, outer, 0)

    index_y = 8 * (64 * (row % 2) + lax.broadcasted_iota(jnp.int32, (64, 128), 0)) + row // 2
    lane_x = lax.broadcasted_iota(jnp.int32, (64, 128), 1)
    wave_y = jnp.where(index_y < NY // 2, index_y, index_y - NY).astype(F32) * (TWO_PI / NY)

    def inner(k, total):
        high, low = split(parts[k])
        value = mul(high, table[0, k]) + mul(low, table[0, k]) + mul(high, table[1, k])
        index_x = 8 * lane_x + k
        wave_x = jnp.where(index_x < NX // 2, index_x, index_x - NX).astype(F32) * (TWO_PI / NX)
        flat = wave_x * wave_x + wave_y * wave_y
        valid = (index_y != NY // 2) & (index_x != NX // 2)
        to = pl.multiple_of(k * 128, 128)
        rows = [[None, None] for _ in range(3)]
        for h in range(2):
            index_z = 4 * meta[65] + 2 * pair + h
            wave_z = index_z.astype(F32) * (TWO_PI / NZ)
            weight = jnp.where(index_z == 0, 1.0, 2.0).astype(F32) / CELLS
            squared = flat + wave_z * wave_z
            keep = valid & (squared > 0.0)
            inverse = jnp.where(keep, 1.0 / jnp.where(keep, squared, 1.0), 0.0)

            def crossed(vector, scale):
                return [
                    (wave_y * vector[2] - wave_z * vector[1]) * scale,
                    (wave_z * vector[0] - wave_x * vector[2]) * scale,
                    (wave_x * vector[1] - wave_y * vector[0]) * scale,
                ]

            start = [128 * c + 64 * h for c in range(3)]
            real = [value[s : s + 64, 0:128] for s in start]
            imag = [value[s : s + 64, 128:256] for s in start]
            grad_real = crossed(imag, -inverse)
            grad_imag = crossed(real, inverse)
            square = 0.0
            for c in range(3):
                spectrum[0, c, h, :, pl.ds(to, 128)] = grad_real[c]
                spectrum[1, c, h, :, pl.ds(to, 128)] = grad_imag[c]
                square = square + grad_real[c] * grad_real[c] + grad_imag[c] * grad_imag[c]
            total = total + weight * square
            scale = inverse * weight
            back_real = crossed(grad_imag, -scale)
            back_imag = crossed(grad_real, scale)
            for c in range(3):
                rows[c][h] = jnp.concatenate([back_real[c], back_imag[c]], 1)
        high, low = split(jnp.concatenate([rows[c][h] for c in range(3) for h in range(2)], 0))
        back[k] = mul(high, table_back[0, k]) + mul(low, table_back[0, k]) + mul(high, table_back[1, k])
        return total

    total = lax.fori_loop(0, 8, inner, jnp.zeros((64, 128), F32))
    norm[0] = jnp.sum(total.reshape(8, 8, 128), axis=0)

    def last(tile, carry):
        at = pl.multiple_of(tile * 8, 8)
        for c in range(3):
            values = []
            for k in range(16):
                to = 128 * (k // 8)
                first = back[k % 8, pl.ds(128 * c + at, 8), to : to + 128]
                second = back[k % 8, pl.ds(128 * c + 64 + at, 8), to : to + 128]
                values.append((jnp.where(lower, first, turned(second)), jnp.where(lower, turned(first), second)))
            for s, (real, imag) in enumerate(small_dft(values, 1)):
                out[s, 0, c, 0, pl.ds(at, 8), :] = real
                out[s, 0, c, 1, pl.ds(at, 8), :] = imag
        return carry

    lax.fori_loop(0, 8, last, 0)


def gather_kernel(meta, points, depth, received, table, out, edge, field_high, field_low, parts):
    def inner(k, carry):
        columns = []
        for c in range(3):
            for p in range(2):
                columns.append(
                    jnp.concatenate(
                        [received[2 * k + half, p, c, part] for part in range(2) for half in range(2)], 0
                    )
                )
        high, low = split(jnp.concatenate(columns, 1))
        parts[k] = mul(table[0, k], high) + mul(table[1, k], high) + mul(table[0, k], low)
        return carry

    lax.fori_loop(0, 8, inner, 0)

    def outer(tile, carry):
        row = pl.multiple_of(tile * 16, 16)
        for c in range(3):
            for p in range(2):
                at = 128 * (2 * c + p)
                values = [
                    (parts[k, pl.ds(row, 16), at : at + 128], parts[k, pl.ds(128 + row, 16), at : at + 128])
                    for k in range(8)
                ]
                for a, pieces in enumerate(small_dft(values, 1)):
                    for part in range(2):
                        high, low = split(pieces[part])
                        lane = 256 * p + 128 * part
                        field_high[c, pl.ds(128 * a + row, 16), lane : lane + 128] = high
                        field_low[c, pl.ds(128 * a + row, 16), lane : lane + 128] = low
        return carry

    lax.fori_loop(0, 8, outer, 0)
    lane = lax.broadcasted_iota(jnp.int32, (16, 512), 1)
    place = (lane == 64 * lax.broadcasted_iota(jnp.int32, (16, 512), 0)).astype(BF16)
    for c in range(3):
        value = mul_t(place, field_high[c, 0:1024, :]) + mul_t(place, field_low[c, 0:1024, :])
        edge[8 * c : 8 * c + 8, :] = value[0:8]
        field_high[c, 1024:1040, :] = field_high[c, 0:16, :]
        field_low[c, 1024:1040, :] = field_low[c, 0:16, :]

    def step(block, carry):
        place_x, place_y, _ = brick_place(meta[block])
        point = block_points(points, block)
        weight_high, weight_low = split(slab_weights(point, depth[block], place_x))
        weights = jnp.concatenate([weight_high, weight_low], 1)
        along = hat(ramp((48, 128), 0) - point[1:2])
        row = pl.multiple_of(place_y * 32, 32)
        high = jnp.concatenate([field_high[c, pl.ds(row, 48), :] for c in range(3)], 0)
        low = jnp.concatenate([field_low[c, pl.ds(row, 48), :] for c in range(3)], 0)
        both = mul(high, weights)
        value = both[:, :128] + both[:, 128:] + mul(low, weight_high)
        for c in range(3):
            velocity = jnp.sum(along * value[48 * c : 48 * c + 48], axis=0, keepdims=True)
            out[block // 8, pl.ds(8 * c + block % 8, 1), :] = velocity
        return carry

    lax.fori_loop(0, 64, step, 0, unroll=2)


def border_kernel(meta, points, depth, edge, velocity, out, wide):
    out[...] = velocity[...]
    wide[:, 0:1024] = edge[...]
    wide[:, 1024:1152] = edge[:, 0:128]
    cells = ramp((256, 128), 0)

    def step(block, carry):
        place_x, place_y, _ = brick_place(meta[block])

        @pl.when(place_x == 1)
        def _():
            point = block_points(points, block)
            waves = depth[block] * jnp.maximum(point[0:1] - 31.0, 0.0)
            weight_high, weight_low = split(hat(cells - (32 * (place_y % 4)).astype(F32) - point[1:2]))
            lane = pl.multiple_of(place_y // 4 * 128, 128)
            high, low = split(wide[:, pl.ds(lane, 256)])
            value = mul(high, weight_high) + mul(low, weight_high) + mul(high, weight_low)
            for c in range(3):
                more = jnp.sum(waves * value[8 * c : 8 * c + 8], axis=0, keepdims=True)
                out[block // 8, pl.ds(8 * c + block % 8, 1), :] += more

        return carry

    lax.fori_loop(0, 64, step, 0)


def call(kernel, outs, specs, scratch=(), flops=0, traffic=0, **extra):
    return pl.pallas_call(
        kernel,
        out_shape=outs,
        in_specs=specs,
        scratch_shapes=list(scratch),
        cost_estimate=pl.CostEstimate(flops=flops, bytes_accessed=traffic, transcendentals=0),
        compiler_params=pltpu.CompilerParams(vmem_limit_bytes=VMEM_LIMIT),
        **extra,
    )


def shape(*dims):
    return jax.ShapeDtypeStruct(dims, F32)


def shifted(value, axis, steps):
    count = lax.axis_size(axis)
    return lax.ppermute(value, axis, [(source, (source + steps) % count) for source in range(count)])


def spread_out(value, axis):
    count = lax.axis_size(axis)
    return lax.all_to_all(jnp.broadcast_to(value[None], (count,) + value.shape), axis, 0, 0, tiled=True)


def exchange(value):
    return lax.all_to_all(value, "row", 0, 0, tiled=True)


def body(offsets, measured, block_brick, block_count):
    row = lax.axis_index("row")
    col = lax.axis_index("col")
    slot = jnp.arange(1024, dtype=jnp.int32) % 128
    live = (slot < jnp.repeat(block_count, 128)).astype(F32)
    residual = measured * live[None]
    bricks = jnp.repeat(block_brick, 128).astype(F32)[None]
    points = spread_out(jnp.concatenate([offsets, residual, bricks, bricks], 0), "col")
    bricks = points[:, 6, ::128].reshape(64).astype(jnp.int32)
    meta = jnp.concatenate([bricks, jnp.stack([row, col]).astype(jnp.int32)])
    y_table = table_y()
    x_table = table_x()
    forward_y = jnp.asarray(halves(y_table))
    inverse_y = jnp.asarray(halves(y_table.transpose(0, 2, 1)))
    forward_x = jnp.asarray(halves(x_table))
    inverse_x = jnp.asarray(halves(x_table.transpose(0, 2, 1)))

    depth, edge = call(edge_kernel, (shape(64, 8, 128), shape(24, 1152)), [SMEM, VMEM])(meta, points)
    edge = shifted(edge[:, :1024], "row", 1)
    sent = call(
        spread_kernel,
        shape(16, 2, 3, 2, 64, 128),
        [SMEM, VMEM, VMEM, VMEM, VMEM],
        [pltpu.VMEM((3, 1032, 512), F32), pltpu.VMEM((8, 256, 768), F32)],
    )(meta, points, depth, edge, forward_y)
    received = exchange(sent)
    block = (16, 1, 3, 2, 64, 128)
    spectrum, sent, norm = pl.pallas_call(
        spectrum_kernel,
        grid=(2,),
        out_shape=(shape(2, 3, 4, 64, 1024), shape(16, 2, 3, 2, 64, 128), shape(2, 8, 128)),
        in_specs=[
            SMEM,
            pl.BlockSpec(block, lambda i: (0, i, 0, 0, 0, 0)),
            VMEM,
            VMEM,
        ],
        out_specs=(
            pl.BlockSpec((2, 3, 2, 64, 1024), lambda i: (0, 0, i, 0, 0)),
            pl.BlockSpec(block, lambda i: (0, i, 0, 0, 0, 0)),
            pl.BlockSpec((1, 8, 128), lambda i: (i, 0, 0)),
        ),
        scratch_shapes=[pltpu.VMEM((8, 384, 256), F32), pltpu.VMEM((8, 384, 256), F32)],
        compiler_params=pltpu.CompilerParams(vmem_limit_bytes=VMEM_LIMIT),
    )(meta, received, forward_x, inverse_x)
    received = exchange(sent)
    velocity, edge = call(
        gather_kernel,
        (shape(8, 24, 128), shape(24, 1024)),
        [SMEM, VMEM, VMEM, VMEM, VMEM],
        [pltpu.VMEM((3, 1040, 512), BF16), pltpu.VMEM((3, 1040, 512), BF16), pltpu.VMEM((8, 256, 768), F32)],
    )(meta, points, depth, received, inverse_y)
    edge = shifted(edge, "row", -1)
    velocity = call(
        border_kernel, shape(8, 24, 128), [SMEM, VMEM, VMEM, VMEM, VMEM], [pltpu.VMEM((24, 1152), F32)]
    )(meta, points, depth, edge, velocity)
    velocity = jnp.sum(lax.all_to_all(velocity, "col", 0, 0, tiled=True), axis=0)
    velocity = velocity.reshape(3, 1024) * live[None]
    sums = jnp.stack([jnp.sum(norm), jnp.sum(velocity * velocity)])
    sums = jnp.sum(spread_out(sums, "row"), axis=0)
    sums = jnp.sum(spread_out(sums, "col"), axis=0)
    step_length = sums[0] / sums[1]
    vorticity = spectrum * (step_length * (1.0 / math.sqrt(CELLS)))
    return vorticity, residual - step_length * velocity


def solution(mesh):
    in_specs = (
        P(None, ("row", "col")),
        P(None, ("row", "col")),
        P(("row", "col")),
        P(("row", "col")),
    )
    out_specs = (P(None, None, "col", "row", None), P(None, ("row", "col")))
    return jax.shard_map(body, mesh=mesh, in_specs=in_specs, out_specs=out_specs, check_vma=False)
```

time: 1100 us -> 322 us (0.29); the launches traced: 1080 us -> 324 us
  local copies, waits for them, and re-layouts: 385 us -> 4.37 us
  other arithmetic: 295 us -> 13.5 us
  waiting for transfers between devices: 209 us -> 24.6 us
  Pallas kernels: 0 us -> 95.2 us
  matrix products: 58.3 us -> 0 us
  blocking collectives: 105 us -> 162 us
  between operations: 17.3 us -> 1.94 us
    scatter-add x1 -> x0, other arithmetic: 188 us -> none  [spread(): jnp.zeros((channels, (planes + 1) * NY), jnp.float32).at[:, columns]]
    all_to_all x0 -> x3, blocking collectives: none -> 162 us  [the longest x2 152 us: exchange(): return lax.all_to_all(value, 'row', 0, 0, tiled=True)]
    all_to_all x2 -> x3, waiting for transfers between devices: 154 us -> 15.3 us  [the longest x2 11 us: spread_out(): lax.all_to_all(jnp.broadcast_to(value[None], (count,) + value.shape), axi...]
    gather x1 -> x0, local copies, waits for them, and re-layouts: 119 us -> none  [interpolate(): picked = extended[:, columns] * across[None]]
    pallas_call x0 -> x5, Pallas kernels: none -> 95.2 us  [the longest x1 26.9 us: body(): pl.pallas_call(spectrum_kernel, grid=(2,), out_shape=(shape(2, 3, 4, 64,...]
    unnamed x72 -> x12, local copies, waits for them, and re-layouts: 92.1 us -> 1.29 us
    reshape x8 -> x1, local copies, waits for them, and re-layouts: 69 us -> 0.01 us  [body(): velocity = velocity.reshape(3, 1024) * live[None]]
    psum x1 -> x0, blocking collectives: 67.3 us -> none  [total(): return lax.psum(value, ('row', 'col'))]
  transfers between devices with their start and end apart: 5 -> 5, of which waited for: 3 -> 5; matrix products, arithmetic and copies ran while one was open for 4% -> 0% of each run, Pallas kernels for 0% -> 0%
where the time goes in v1:
time: 322 us; the launch traced here: 324 us
  blocking collectives  162 us (50%)
  Pallas kernels  95.2 us (30%)
  waiting for transfers between devices  24.6 us (8%)
  starting transfers between devices  22.2 us (7%)
  other arithmetic  13.5 us (4%)
  local copies, waits for them, and re-layouts  4.37 us (1%)
    all_to_all x2, blocking collectives, exchange(): return lax.all_to_all(value, 'row', 0, 0, tiled=True)  152 us
    pallas_call x1, Pallas kernels, body(): pl.pallas_call(spectrum_kernel, grid=(2,), out_shape=(shape(2, 3, 4, 64,...  26.9 us
    pallas_call x1, Pallas kernels, body(): call(spread_kernel, shape(16, 2, 3, 2, 64, 128), [SMEM, VMEM, VMEM, VMEM,...  23.8 us
    pallas_call x1, Pallas kernels, body(): call(gather_kernel, (shape(8, 24, 128), shape(24, 1024)), [SMEM, VMEM, VM...  22.3 us
    all_to_all x2, starting transfers between devices, spread_out(): lax.all_to_all(jnp.broadcast_to(value[None], (count,) + value.shape), axi...  12.3 us
    pallas_call x1, Pallas kernels, body(): call(edge_kernel, (shape(64, 8, 128), shape(24, 1152)), [SMEM, VMEM])  11.4 us
    all_to_all x2, waiting for transfers between devices, spread_out(): lax.all_to_all(jnp.broadcast_to(value[None], (count,) + value.shape), axi...  11 us
    pallas_call x1, Pallas kernels, body(): call(border_kernel, shape(8, 24, 128), [SMEM, VMEM, VMEM, VMEM, VMEM], [p...  10.8 us
  transfers between devices with their start and end apart: 5, of which 5 were waited for; matrix products, arithmetic and copies ran while one was open for 0% of the time, Pallas kernels for 0%

profile of v1, /device:TPU:1, one launch (start us, length us, event | category | flops | bytes accessed | tf_op | source)
XLA Modules:
  0.0 324.4 jit_solution(5733594731216003423)
XLA Ops:
  0.6 0.7 convert_element_type.31
  1.3 0.7 fusion.11
  2.0 0.7 broadcast_multiply_fusion.1
  2.7 0.1 broadcast_in_dim.11
  2.8 0.7 pad_maximum_fusion
  3.5 0.7 broadcast_in_dim.12
  4.3 6.8 %all-to-all-start = ((f32[8,8,1024]{2,1,0:T(8,128)}), f32[8,8,1024]{2,1,0:T(8,128)S(1)}, u32[]{:S(2)}, u32[]{:S(2)}) async-start(f32[8,8,1024]{2,1,0:T(8,128)} %broadcast_in_dim.12), calls=%async_computation | async-start | bytes 524288 | tf_op jit(solution)/shard_map/all_to_all | solution.py:436
  11.1 6.5 %all-to-all-done.points = f32[8,8,1024]{2,1,0:T(8,128)S(1)} async-done(((f32[8,8,1024]{2,1,0:T(8,128)}), f32[8,8,1024]{2,1,0:T(8,128)S(1)}, u32[]{:S(2)}, u32[]{:S(2)}) %all-to-all-start) | async-done | bytes 262176 | tf_op jit(solution)/shard_map/all_to_all | solution.py:436
  17.6 0.0 copy-start
  17.6 0.1 slice.12
  17.7 0.1 convert_element_type.34
  17.8 0.6 pad_add_fusion.meta
  18.4 0.0 copy-done
  18.4 11.4 %shard_map.95 = (f32[64,8,128]{2,1,0:T(8,128)}, f32[24,1152]{1,0:T(8,128)}) custom-call(s32[66]{0:T(128)} %pad_add_fusion.meta, f32[8,8,1024]{2,1,0:T(8,128)} %copy-done), custom_call_target="tpu_custom_call" | custom-call | tf_op jit(solution)/shard_map/pallas_call | solution.py:460
  29.8 0.9 slice.13
  30.7 0.0 collective-permute-start
  30.7 6.8 %collective-permute-done.edge = f32[24,1024]{1,0:T(8,128)S(1)} collective-permute-done((f32[24,1024]{1,0:T(8,128)S(1)}, f32[24,1024]{1,0:T(8,128)S(1)}, u32[]{:S(2)}, u32[]{:S(2)}) %collective-permute-start) | collective-permute-done | bytes 98336 | tf_op jit(solution)/shard_map/ppermute | solution.py:431
  37.5 0.0 copy-start.1
  37.5 0.6 copy-done.1
  38.1 23.8 %shard_map.96 = f32[16,2,3,2,64,128]{5,4,3,2,1,0:T(8,128)} custom-call(s32[66]{0:T(128)} %pad_add_fusion.meta, f32[8,8,1024]{2,1,0:T(8,128)} %copy-done, f32[64,8,128]{2,1,0:T(8,128)} %get-tuple-element.9.depth, f32[24,1024]{1,0:T(8,128)} %copy-done.1, bf16[2,8,256,256]{3,2,1,0:T(8,128)(2,1)} %constant.38.clone.table), custom_call_target="tpu_custom_call" | custom-call | tf_op jit(solution)/shard_map/pallas_call | solution.py:462
  61.9 77.1 %all_to_all.32.received = f32[16,2,3,2,64,128]{5,4,3,2,1,0:T(8,128)} all-to-all(f32[16,2,3,2,64,128]{5,4,3,2,1,0:T(8,128)} %shard_map.96), channel_id=1, replica_groups=mesh['row'=16,'col'=8] {'row'}, dimensions={0} | all-to-all | bytes 12582912 | tf_op jit(solution)/shard_map/all_to_all | solution.py:440
  139.0 26.9 %shard_map.97 = (f32[2,3,4,64,1024]{4,3,2,1,0:T(8,128)}, f32[16,2,3,2,64,128]{5,4,3,2,1,0:T(8,128)}, f32[2,8,128]{2,1,0:T(8,128)}) custom-call(s32[66]{0:T(128)} %pad_add_fusion.meta, f32[16,2,3,2,64,128]{5,4,3,2,1,0:T(8,128)} %all_to_all.32.received, bf16[2,8,256,256]{3,2,1,0:T(8,128)(2,1)} %constant.40.clone.table, ...), custom_call_target="tpu_custom_call" | custom-call | tf_op jit(solution)/shard_map/pallas_call | solution.py:470
  165.9 75.1 %all_to_all.33.received = f32[16,2,3,2,64,128]{5,4,3,2,1,0:T(8,128)} all-to-all(f32[16,2,3,2,64,128]{5,4,3,2,1,0:T(8,128)} %get-tuple-element.13), channel_id=1, replica_groups=mesh['row'=16,'col'=8] {'row'}, dimensions={0} | all-to-all | bytes 12582912 | tf_op jit(solution)/shard_map/all_to_all | solution.py:440
  241.1 0.0 copy-start.5
  241.1 0.0 copy-start.4
  241.1 0.0 copy-start.3
  241.1 22.3 %shard_map.98 = (f32[8,24,128]{2,1,0:T(8,128)}, f32[24,1024]{1,0:T(8,128)}) custom-call(s32[66]{0:T(128)} %pad_add_fusion.meta, f32[8,8,1024]{2,1,0:T(8,128)} %copy-done, f32[64,8,128]{2,1,0:T(8,128)} %get-tuple-element.9.depth, f32[16,2,3,2,64,128]{5,4,3,2,1,0:T(8,128)} %all_to_all.33.received, bf16[2,8,256,256]{3,2,1,0:T(8,128)(2,1)} %constant.39.clone.table), custom_call_target="tpu_custom_call" | custom-call | tf_op jit(solution)/shard_map/pallas_call | solution.py:489
  263.4 1.2 collective-permute-start.1
  264.6 2.5 collective-permute-done.1.edge
  267.1 0.0 copy-start.2
  267.1 0.6 copy-done.2
  267.7 10.8 %shard_map.99 = f32[8,24,128]{2,1,0:T(8,128)} custom-call(s32[66]{0:T(128)} %pad_add_fusion.meta, f32[8,8,1024]{2,1,0:T(8,128)} %copy-done, f32[64,8,128]{2,1,0:T(8,128)} %get-tuple-element.9.depth, f32[24,1024]{1,0:T(8,128)} %copy-done.2, f32[8,24,128]{2,1,0:T(8,128)} %get-tuple-element.15.velocity), custom_call_target="tpu_custom_call" | custom-call | tf_op jit(solution)/shard_map/pallas_call | solution.py:496
  278.5 8.7 %all-to-all-start.3 = ((f32[8,24,128]{2,1,0:T(8,128)}), f32[8,24,128]{2,1,0:T(8,128)S(1)}, u32[]{:S(2)}, u32[]{:S(2)}) async-start(f32[8,24,128]{2,1,0:T(8,128)} %shard_map.99), calls=%async_computation.3 | async-start | bytes 196608 | tf_op jit(solution)/shard_map/all_to_all | solution.py:499
  287.3 0.0 copy-done.5
  287.3 0.1 fusion.9
  287.3 0.0 copy-done.4
  287.3 0.6 reduce_sum.47
  287.9 4.3 %all-to-all-done.3 = f32[8,24,128]{2,1,0:T(8,128)S(1)} async-done(((f32[8,24,128]{2,1,0:T(8,128)}), f32[8,24,128]{2,1,0:T(8,128)S(1)}, u32[]{:S(2)}, u32[]{:S(2)}) %all-to-all-start.3) | async-done | bytes 98336 | tf_op jit(solution)/shard_map/all_to_all | solution.py:499
  292.3 0.6 fusion.1
  292.9 1.3 pad_maximum_fusion.1
  294.2 10.2 %all_to_all.34 = f32[16,1,2]{2,1,0:T(1,128)S(1)} all-to-all(f32[16,1,2]{2,1,0:T(1,128)S(1)} %broadcast_in_dim.13), channel_id=1, replica_groups=mesh['row'=16,'col'=8] {'row'}, dimensions={0} | all-to-all | bytes 256 | tf_op jit(solution)/shard_map/all_to_all | solution.py:436
  304.5 0.6 broadcast_in_dim.14
  305.1 5.5 %all-to-all-start.5 = ((f32[8,1,2]{2,1,0:T(1,128)}), f32[8,1,2]{2,1,0:T(1,128)S(1)}, u32[]{:S(2)}, u32[]{:S(2)}) async-start(f32[8,1,2]{2,1,0:T(1,128)} %broadcast_in_dim.14), calls=%async_computation.5 | async-start | bytes 8192 | tf_op jit(solution)/shard_map/all_to_all | solution.py:436
  310.5 4.5 %all-to-all-done.5 = f32[8,1,2]{2,1,0:T(1,128)S(1)} async-done(((f32[8,1,2]{2,1,0:T(1,128)}), f32[8,1,2]{2,1,0:T(1,128)S(1)}, u32[]{:S(2)}, u32[]{:S(2)}) %all-to-all-start.5) | async-done | bytes 96 | tf_op jit(solution)/shard_map/all_to_all | solution.py:436
  315.1 0.6 fusion.12
  316.9 0.0 copy-done.3
  316.9 0.6 multiply_subtract_fusion
  317.5 6.9 %broadcast_multiply_fusion = f32[2,3,4,64,1024]{4,3,2,1,0:T(8,128)} fusion(f32[2,3,4,64,1024]{4,3,2,1,0:T(8,128)} %get-tuple-element.11, f32[]{:T(128)S(6)} %mul.49), kind=kLoop, calls=%fused_computation | loop fusion | flops 1572864 | bytes 12582916 | tf_op jit(solution)/shard_map/mul | solution.py:505
  (6 shorter events, 0.1 us)
Async XLA Ops:
  4.3 13.3 %all-to-all-start = ((f32[8,8,1024]{2,1,0:T(8,128)}), f32[8,8,1024]{2,1,0:T(8,128)S(1)}, u32[]{:S(2)}, u32[]{:S(2)}) async-start(f32[8,8,1024]{2,1,0:T(8,128)} %broadcast_in_dim.12), calls=%async_computation | async-start | bytes 524288 | tf_op jit(solution)/shard_map/all_to_all | solution.py:436
  17.6 0.8 copy-start
  30.7 6.8 %collective-permute-start = (f32[24,1024]{1,0:T(8,128)S(1)}, f32[24,1024]{1,0:T(8,128)S(1)}, u32[]{:S(2)}, u32[]{:S(2)}) collective-permute-start(f32[24,1024]{1,0:T(8,128)S(1)} %slice.13), channel_id=1, source_target_pairs={{0,8},{8,16},{16,24},{24,32},{32,40},{40,48},{48,56},{56,64},{64,7... | collective-permute-start | bytes 294920 | tf_op jit(solution)/shard_map/ppermute | solution.py:431
  37.5 0.6 copy-start.1
  241.1 46.2 %copy-start.5 = (s32[8]{0:T(128)S(1)}, s32[8]{0:T(128)}, u32[]{:S(2)}) copy-start(s32[8]{0:T(128)} %param.11) | copy-start | bytes 100
  241.1 46.3 %copy-start.4 = (f32[2,8,128]{2,1,0:T(8,128)S(1)}, f32[2,8,128]{2,1,0:T(8,128)}, u32[]{:S(2)}) copy-start(f32[2,8,128]{2,1,0:T(8,128)} %get-tuple-element.12) | copy-start | bytes 24580
  241.1 75.8 %copy-start.3 = (f32[3,1024]{1,0:T(4,128)S(1)}, f32[3,1024]{1,0:T(4,128)}, u32[]{:S(2)}) copy-start(f32[3,1024]{1,0:T(4,128)} %param.9) | copy-start | bytes 36868
  263.4 3.7 %collective-permute-start.1 = (f32[24,1024]{1,0:T(8,128)}, f32[24,1024]{1,0:T(8,128)S(1)}, u32[]{:S(2)}, u32[]{:S(2)}) collective-permute-start(f32[24,1024]{1,0:T(8,128)} %get-tuple-element.14), channel_id=1, source_target_pairs={{0,120},{8,0},{16,8},{24,16},{32,24},{40,32},{48,40},{56,48},{64,5... | collective-permute-start | bytes 294920 | tf_op jit(solution)/shard_map/ppermute | solution.py:431
  267.1 0.6 copy-start.2
  278.5 13.7 %all-to-all-start.3 = ((f32[8,24,128]{2,1,0:T(8,128)}), f32[8,24,128]{2,1,0:T(8,128)S(1)}, u32[]{:S(2)}, u32[]{:S(2)}) async-start(f32[8,24,128]{2,1,0:T(8,128)} %shard_map.99), calls=%async_computation.3 | async-start | bytes 196608 | tf_op jit(solution)/shard_map/all_to_all | solution.py:499
  305.1 10.0 %all-to-all-start.5 = ((f32[8,1,2]{2,1,0:T(1,128)}), f32[8,1,2]{2,1,0:T(1,128)S(1)}, u32[]{:S(2)}, u32[]{:S(2)}) async-start(f32[8,1,2]{2,1,0:T(1,128)} %broadcast_in_dim.14), calls=%async_computation.5 | async-start | bytes 8192 | tf_op jit(solution)/shard_map/all_to_all | solution.py:436

commit v2 on v1

v2 whole, which is shorter than its diff:
```python
import functools
import math

import jax
import jax.numpy as jnp
import ml_dtypes
import numpy as np
from jax import lax
from jax.experimental import pallas as pl
from jax.experimental.pallas import tpu as pltpu
from jax.sharding import PartitionSpec as P

NX = 1024
NY = 1024
NZ = 64
CELLS = float(NX * NY * NZ)
TWO_PI = 2.0 * math.pi
F32 = jnp.float32
BF16 = jnp.bfloat16
VMEM_LIMIT = 56 * 1024 * 1024
VMEM = pl.BlockSpec(memory_space=pltpu.VMEM)
SMEM = pl.BlockSpec(memory_space=pltpu.SMEM)


def halves(table):
    table = table.astype(np.float32)
    high = table.astype(ml_dtypes.bfloat16)
    low = (table - high.astype(np.float32)).astype(ml_dtypes.bfloat16)
    return np.stack([high, low])


def table_y():
    first = np.arange(8)[:, None, None]
    angle = TWO_PI * ((np.arange(128)[None, :, None] * 8 + first) * np.arange(128)[None, None, :] % 1024) / 1024
    cosine, sine = np.cos(angle), np.sin(angle)
    return np.concatenate([np.concatenate([cosine, sine], 2), np.concatenate([-sine, cosine], 2)], 1)


def table_x():
    result = np.zeros((8, 2, 2, 64, 2, 64, 2))
    inner = np.arange(64)
    for first in range(8):
        for upper in range(2):
            wave = 16 * np.arange(64) + first + 8 * upper
            angle = TWO_PI * (inner[:, None] * wave[None, :] % 1024) / 1024
            result[first, upper, 0, :, 0, :, upper] = np.cos(angle)
            result[first, upper, 1, :, 0, :, upper] = np.sin(angle)
            result[first, upper, 0, :, 1, :, upper] = -np.sin(angle)
            result[first, upper, 1, :, 1, :, upper] = np.cos(angle)
    return result.reshape(8, 256, 256)


def split(value):
    high = value.astype(BF16)
    return high, (value - high.astype(F32)).astype(BF16)


def mul(left, right):
    return jnp.dot(left, right, preferred_element_type=F32)


def mul_t(left, right):
    return lax.dot_general(left, right, (((1,), (1,)), ((), ())), preferred_element_type=F32)


def small_dft(values, sign):
    count = len(values)
    if count == 1:
        return values
    even = small_dft(values[0::2], sign)
    odd = small_dft(values[1::2], sign)
    low, high = [], []
    for k in range(count // 2):
        real, imag = odd[k]
        if k > 0:
            if 4 * k == count:
                real, imag = (-imag, real) if sign > 0 else (imag, -real)
            elif 8 * k == count:
                root = math.sqrt(0.5)
                if sign > 0:
                    real, imag = (real - imag) * root, (real + imag) * root
                else:
                    real, imag = (real + imag) * root, (imag - real) * root
            elif 8 * k == 3 * count:
                root = math.sqrt(0.5)
                if sign > 0:
                    real, imag = (real + imag) * -root, (real - imag) * root
                else:
                    real, imag = (imag - real) * root, (real + imag) * -root
            else:
                cosine = math.cos(TWO_PI * k / count)
                sine = sign * math.sin(TWO_PI * k / count)
                real, imag = real * cosine - imag * sine, real * sine + imag * cosine
        low.append((even[k][0] + real, even[k][1] + imag))
        high.append((even[k][0] - real, even[k][1] - imag))
    return low + high


def hat(distance):
    return jnp.maximum(1.0 - jnp.abs(distance), 0.0)


def ramp(shape, axis):
    return lax.broadcasted_iota(jnp.int32, shape, axis).astype(F32)


def brick_place(brick):
    return brick // 64, brick // 2 % 32, brick % 2


def block_points(points, block):
    lane = pl.multiple_of(block % 8 * 128, 128)
    return points[block // 8, :, pl.ds(lane, 128)]


def depth_wave(points, meta, depth):
    index = lax.broadcasted_iota(jnp.int32, (8, 128), 0)
    mode = 4 * meta[65] + 2 * (index // 4) + index % 2
    turn = 16 * (index // 2 % 2)

    def wave(cell):
        angle = (mode * cell + turn) & 63
        value = (jnp.abs(angle - 32) - 16).astype(F32) * (math.pi / 32.0)
        square = value * value
        total = -1.0 / 39916800.0
        for factor in (1.0 / 362880.0, -1.0 / 5040.0, 1.0 / 120.0, -1.0 / 6.0, 1.0):
            total = total * square + factor
        return total * value

    def step(block, carry):
        height = block_points(points, block)[2:3]
        lower = jnp.floor(height)
        part = height - lower
        cell = lower.astype(jnp.int32) + 32 * (meta[block] % 2)
        depth[block] = (1.0 - part) * wave(cell) + part * wave(cell + 1)
        return carry

    lax.fori_loop(0, 64, step, 0, unroll=4)


def edge_weights(point):
    weight = hat(ramp((40, 128), 0) - point[1:2])
    return jnp.concatenate([weight, jnp.zeros((88, 128), F32)], 0)


def edge_waves(point, waves, place_x):
    return waves * jnp.maximum(point[0:1] - (63 - 32 * place_x).astype(F32), 0.0)


def lower_lanes(rows):
    return lax.broadcasted_iota(jnp.int32, (rows, 128), 1) < 64


def joined(first, second):
    lower = lower_lanes(first.shape[0])
    return (
        jnp.where(lower, first, pltpu.roll(second, 64, 1)),
        jnp.where(lower, pltpu.roll(first, 64, 1), second),
    )


def pack_kernel(offsets, measured, bricks, counts, out, residual):
    lane = lax.broadcasted_iota(jnp.int32, (3, 128), 1)
    for i in range(8):
        at = slice(128 * i, 128 * i + 128)
        residual[:, at] = jnp.where(lane < counts[i], measured[:, at], 0.0)
        brick = jnp.zeros((2, 128), F32) + bricks[i].astype(F32)
        block = jnp.concatenate([offsets[:, at], residual[:, at], brick], 0)
        for dest in range(8):
            out[dest, :, at] = block


def slab_weights(point, waves, place_x):
    across = hat(ramp((64, 128), 0) - (32 * place_x).astype(F32) - point[0:1])
    return jnp.concatenate([waves[i : i + 1] * across for i in range(4)], 0)


def first_spread_kernel(meta, points, table, out, depth, field, parts, windows):
    depth_wave(points, meta, depth)
    spread_kernel(0, meta, points, table, depth, out, field, parts, windows)


def spread_kernel(pair, meta, points, table, depth, out, field, parts, windows):
    field[...] = jnp.zeros_like(field)
    windows[...] = jnp.zeros_like(windows)

    def step(block, carry):
        place_x, place_y, _ = brick_place(meta[block])
        point = block_points(points, block)
        waves = depth[block][4 * pair : 4 * pair + 4]
        weight_high, weight_low = split(slab_weights(point, waves, place_x))
        along = hat(ramp((40, 128), 0) - point[1:2])
        source = jnp.concatenate([along * point[3 + c : 4 + c] for c in range(3)], 0)
        source_high, source_low = split(source)
        both = mul_t(jnp.concatenate([source_high, source_low], 0), weight_high)
        value = both[:120] + both[120:] + mul_t(source_high, weight_low)
        row = pl.multiple_of(place_y * 32, 32)
        for c in range(3):
            field[c, pl.ds(row, 40), :] += value[40 * c : 40 * c + 40]
        waves = edge_waves(point, waves, place_x)
        source_high, source_low = split(jnp.concatenate([waves[i : i + 1] * point[3:6] for i in range(4)], 0))
        weight_high, weight_low = split(edge_weights(point))
        value = mul_t(source_high, weight_high) + mul_t(source_low, weight_high) + mul_t(source_high, weight_low)
        lane = pl.multiple_of(place_y // 4 * 128, 128)
        windows[place_y % 4, :, pl.ds(lane, 128)] += value
        return carry

    lax.fori_loop(0, 64, step, 0, unroll=4)
    for c in range(3):
        field[c, 0:1, :] += field[c, 1024:1025, :]

    def outer(tile, carry):
        row = pl.multiple_of(tile * 8, 8)
        for c in range(3):
            values = [
                (field[c, pl.ds(128 * a + row, 8), 0:128], field[c, pl.ds(128 * a + row, 8), 128:256])
                for a in range(8)
            ]
            for k, (real, imag) in enumerate(small_dft(values, -1)):
                parts[k, pl.ds(row, 8), 128 * c : 128 * c + 128] = real
                parts[k, pl.ds(128 + row, 8), 128 * c : 128 * c + 128] = imag
        return carry

    lax.fori_loop(0, 16, outer, 0, unroll=2)
    total = windows[0]
    for j in range(1, 4):
        total = total + pltpu.roll(windows[j], 32 * j, 1)
    values = [(total[0:6, 128 * a : 128 * a + 128], total[6:12, 128 * a : 128 * a + 128]) for a in range(8)]
    for k, pieces in enumerate(small_dft(values, -1)):
        windows[k // 2, 0:6, 256 * (k % 2) : 256 * (k % 2) + 256] = jnp.concatenate(pieces, 1)

    def inner(k, carry):
        high, low = split(parts[k])
        value = mul(table[0, k], high) + mul(table[1, k], high) + mul(table[0, k], low)
        high, low = split(windows[k // 2, 0:6, pl.ds(pl.multiple_of(256 * (k % 2), 256), 256)])
        edge = mul_t(high, table[0, k]) + mul_t(high, table[1, k]) + mul_t(low, table[0, k])
        edge_real = joined(edge[0:3, 0:128], edge[3:6, 0:128])
        edge_imag = joined(edge[0:3, 128:256], edge[3:6, 128:256])
        for half in range(2):
            for c in range(3):
                for part in range(2):
                    row = 128 * part + 64 * half
                    to = 64 * (2 * c + part)
                    out[2 * k + half, to : to + 64] = value[row : row + 64, 128 * c : 128 * c + 128]
            out[2 * k + half, 384:392] = jnp.concatenate(
                [edge_real[half], edge_imag[half], jnp.zeros((2, 128), F32)], 0
            )
        return carry

    lax.fori_loop(0, 8, inner, 0, unroll=2)


def spectrum_kernel(pair, meta, received, table, table_back, spectrum, out, norm, parts, back, edge):
    row = meta[64]
    lane = lax.broadcasted_iota(jnp.int32, (8, 128), 1)
    edge[...] = jnp.concatenate([received[s, 384:392] for s in range(16)], 0).T

    def placed(tile, s, j):
        at = 8 * ((s + 15) % 16) + j
        first = edge[pl.ds(tile, 8), at : at + 1]
        second = edge[pl.ds(64 + tile, 8), at : at + 1]
        return received[s, pl.ds(64 * (j % 3 * 2 + j // 3) + tile, 8)] + jnp.where(
            lane == 0, first, jnp.where(lane == 64, second, 0.0)
        )

    def outer(tile, carry):
        at = pl.multiple_of(tile * 8, 8)
        for c in range(3):
            values = [(placed(at, s, c), placed(at, s, 3 + c)) for s in range(16)]
            for k, (real, imag) in enumerate(small_dft(values, -1)):
                to = 128 * (k // 8)
                first, second = joined(real, imag)
                parts[k % 8, pl.ds(128 * c + at, 8), to : to + 128] = first
                parts[k % 8, pl.ds(128 * c + 64 + at, 8), to : to + 128] = second
        return carry

    lax.fori_loop(0, 8, outer, 0)

    index_y = 8 * (64 * (row % 2) + lax.broadcasted_iota(jnp.int32, (64, 128), 0)) + row // 2
    lane_x = lax.broadcasted_iota(jnp.int32, (64, 128), 1)
    wave_y = jnp.where(index_y < NY // 2, index_y, index_y - NY).astype(F32) * (TWO_PI / NY)

    def inner(k, total):
        high, low = split(parts[k])
        value = mul(high, table[0, k]) + mul(low, table[0, k]) + mul(high, table[1, k])
        index_x = 8 * lane_x + k
        wave_x = jnp.where(index_x < NX // 2, index_x, index_x - NX).astype(F32) * (TWO_PI / NX)
        flat = wave_x * wave_x + wave_y * wave_y
        valid = (index_y != NY // 2) & (index_x != NX // 2)
        to = pl.multiple_of(k * 128, 128)
        rows = [[None, None] for _ in range(3)]
        for h in range(2):
            index_z = 4 * meta[65] + 2 * pair + h
            wave_z = index_z.astype(F32) * (TWO_PI / NZ)
            weight = jnp.where(index_z == 0, 1.0, 2.0).astype(F32) / CELLS
            squared = flat + wave_z * wave_z
            keep = valid & (squared > 0.0)
            inverse = jnp.where(keep, 1.0 / jnp.where(keep, squared, 1.0), 0.0)

            def crossed(vector, scale):
                return [
                    (wave_y * vector[2] - wave_z * vector[1]) * scale,
                    (wave_z * vector[0] - wave_x * vector[2]) * scale,
                    (wave_x * vector[1] - wave_y * vector[0]) * scale,
                ]

            start = [128 * c + 64 * h for c in range(3)]
            real = [value[s : s + 64, 0:128] for s in start]
            imag = [value[s : s + 64, 128:256] for s in start]
            grad_real = crossed(imag, -inverse)
            grad_imag = crossed(real, inverse)
            square = 0.0
            for c in range(3):
                spectrum[0, c, h, :, pl.ds(to, 128)] = grad_real[c]
                spectrum[1, c, h, :, pl.ds(to, 128)] = grad_imag[c]
                square = square + grad_real[c] * grad_real[c] + grad_imag[c] * grad_imag[c]
            total = total + weight * square
            scale = inverse * weight
            back_real = crossed(grad_imag, -scale)
            back_imag = crossed(grad_real, scale)
            for c in range(3):
                rows[c][h] = jnp.concatenate([back_real[c], back_imag[c]], 1)
        high, low = split(jnp.concatenate([rows[c][h] for c in range(3) for h in range(2)], 0))
        back[k] = mul(high, table_back[0, k]) + mul(low, table_back[0, k]) + mul(high, table_back[1, k])
        return total

    total = lax.fori_loop(0, 8, inner, jnp.zeros((64, 128), F32))
    norm[...] = jnp.sum(total.reshape(8, 8, 128), axis=0)

    def last(tile, carry):
        at = pl.multiple_of(tile * 8, 8)
        columns = [jnp.zeros((8, 128), F32), jnp.zeros((8, 128), F32)]
        for c in range(3):
            values = []
            for k in range(16):
                to = 128 * (k // 8)
                first = back[k % 8, pl.ds(128 * c + at, 8), to : to + 128]
                second = back[k % 8, pl.ds(128 * c + 64 + at, 8), to : to + 128]
                values.append(joined(first, second))
            for s, pieces in enumerate(small_dft(values, 1)):
                for part in range(2):
                    piece = pieces[part]
                    out[s, pl.ds(64 * (2 * c + part) + at, 8)] = piece
                    place = lane == 8 * ((s + 15) % 16) + 3 * part + c
                    for h in range(2):
                        columns[h] = jnp.where(place, piece[:, 64 * h : 64 * h + 1], columns[h])
        for h in range(2):
            edge[pl.ds(64 * h + at, 8), :] = columns[h]
        return carry

    lax.fori_loop(0, 8, last, 0)
    turned = edge[...].T
    for s in range(16):
        out[s, 384:392] = turned[8 * s : 8 * s + 8]


def gather_kernel(pair, meta, points, depth, received, table, out, field_high, field_low, parts, edge, windows):
    def inner(k, carry):
        columns = [
            jnp.concatenate(
                [
                    received[2 * k + half, 64 * (2 * c + part) : 64 * (2 * c + part) + 64]
                    for part in range(2)
                    for half in range(2)
                ],
                0,
            )
            for c in range(3)
        ]
        high, low = split(jnp.concatenate(columns, 1))
        parts[k] = mul(table[0, k], high) + mul(table[1, k], high) + mul(table[0, k], low)
        first, second = joined(received[2 * k, 384:392], received[2 * k + 1, 384:392])
        real = jnp.concatenate([first[0:3], second[0:3]], 0)
        imag = jnp.concatenate([first[3:6], second[3:6]], 0)
        high, low = split(jnp.concatenate([real, imag], 1))
        edge[k] = mul_t(high, table[0, k]) + mul_t(high, table[1, k]) + mul_t(low, table[0, k])
        return carry

    lax.fori_loop(0, 8, inner, 0, unroll=2)
    values = [(edge[k, :, 0:128], edge[k, :, 128:256]) for k in range(8)]
    plane = jnp.concatenate([jnp.concatenate(pieces, 0) for pieces in small_dft(values, 1)], 1)
    for j in range(4):
        windows[j] = plane if j == 0 else pltpu.roll(plane, 1024 - 32 * j, 1)

    def outer(tile, carry):
        row = pl.multiple_of(tile * 16, 16)
        for c in range(3):
            at = 128 * c
            values = [
                (parts[k, pl.ds(row, 16), at : at + 128], parts[k, pl.ds(128 + row, 16), at : at + 128])
                for k in range(8)
            ]
            for a, pieces in enumerate(small_dft(values, 1)):
                for part in range(2):
                    high, low = split(pieces[part])
                    lane = 128 * part
                    field_high[c, pl.ds(128 * a + row, 16), lane : lane + 128] = high
                    field_low[c, pl.ds(128 * a + row, 16), lane : lane + 128] = low
        return carry

    lax.fori_loop(0, 8, outer, 0)
    for c in range(3):
        field_high[c, 1024:1040, :] = field_high[c, 0:16, :]
        field_low[c, 1024:1040, :] = field_low[c, 0:16, :]

    def step(block, carry):
        place_x, place_y, _ = brick_place(meta[block])
        point = block_points(points, block)
        waves = depth[block][4 * pair : 4 * pair + 4]
        weight_high, weight_low = split(slab_weights(point, waves, place_x))
        weights = jnp.concatenate([weight_high, weight_low], 1)
        along = hat(ramp((48, 128), 0) - point[1:2])
        row = pl.multiple_of(place_y * 32, 32)
        high = jnp.concatenate([field_high[c, pl.ds(row, 48), :] for c in range(3)], 0)
        low = jnp.concatenate([field_low[c, pl.ds(row, 48), :] for c in range(3)], 0)
        both = mul(high, weights)
        value = both[:, :128] + both[:, 128:] + mul(low, weight_high)
        velocity = [jnp.sum(along * value[48 * c : 48 * c + 48], axis=0, keepdims=True) for c in range(3)]
        waves = edge_waves(point, waves, place_x)
        weight_high, weight_low = split(edge_weights(point))
        lane = pl.multiple_of(place_y // 4 * 128, 128)
        high, low = split(windows[place_y % 4, :, pl.ds(lane, 128)])
        value = mul(high, weight_high) + mul(low, weight_high) + mul(high, weight_low)
        more = sum(waves[i : i + 1] * value[3 * i : 3 * i + 3] for i in range(4))
        for c in range(3):
            out[block // 8, pl.ds(8 * c + block % 8, 1), :] = velocity[c] + more[c : c + 1]
        return carry

    lax.fori_loop(0, 64, step, 0, unroll=4)


def sums_kernel(counts, received, first_norm, second_norm, velocity, out):
    row = lax.broadcasted_iota(jnp.int32, (8, 128), 0)
    count = jnp.zeros((8, 128), jnp.int32)
    for i in range(8):
        count = jnp.where(row == i, counts[i], count)
    live = lax.broadcasted_iota(jnp.int32, (8, 128), 1) < count
    square = jnp.zeros((8, 128), F32)
    for c in range(3):
        total = received[0, 8 * c : 8 * c + 8]
        for source in range(1, 8):
            total = total + received[source, 8 * c : 8 * c + 8]
        total = jnp.where(live, total, 0.0)
        square = square + total * total
        for i in range(8):
            velocity[c : c + 1, 128 * i : 128 * i + 128] = total[i : i + 1]
    norm = jnp.sum(first_norm[...] + second_norm[...], axis=0, keepdims=True)
    square = jnp.sum(square, axis=0, keepdims=True)
    tile = jnp.where(row == 0, norm, jnp.where(row == 1, square, 0.0))
    for dest in range(16):
        out[dest] = tile


def final_kernel(sums, residual, velocity, first, second, spectrum, out):
    total = jnp.sum(jnp.sum(sums[...], axis=0), axis=1, keepdims=True)
    length = total[0:1] / total[1:2]
    part, c = pl.program_id(0), pl.program_id(1)
    scale = length * (1.0 / math.sqrt(CELLS))
    spectrum[0, 0, 0:2] = first[part, c] * scale
    spectrum[0, 0, 2:4] = second[part, c] * scale
    out[...] = residual[...] - length * velocity[...]


def call(kernel, outs, specs, scratch=(), traffic=0):
    return pl.pallas_call(
        kernel,
        out_shape=outs,
        in_specs=specs,
        scratch_shapes=list(scratch),
        cost_estimate=pl.CostEstimate(flops=0, bytes_accessed=int(traffic), transcendentals=0),
        compiler_params=pltpu.CompilerParams(vmem_limit_bytes=VMEM_LIMIT),
    )


def shape(*dims):
    return jax.ShapeDtypeStruct(dims, F32)


def spread_out(value, axis):
    count = lax.axis_size(axis)
    return lax.all_to_all(jnp.broadcast_to(value[None], (count,) + value.shape), axis, 0, 0, tiled=True)


def exchange(value):
    return lax.all_to_all(value, "row", 0, 0, tiled=True)


def body(offsets, measured, block_brick, block_count):
    row = lax.axis_index("row")
    col = lax.axis_index("col")
    packed, residual = call(
        pack_kernel, (shape(8, 8, 1024), shape(3, 1024)), [VMEM, VMEM, SMEM, SMEM], traffic=1e6
    )(offsets, measured, block_brick, block_count)
    points = lax.all_to_all(packed, "col", 0, 0, tiled=True)
    bricks = points[:, 6, ::128].reshape(64).astype(jnp.int32)
    meta = jnp.concatenate([bricks, jnp.stack([row, col]).astype(jnp.int32)])
    y_table = table_y()
    x_table = table_x()
    forward_y = jnp.asarray(halves(y_table))
    inverse_y = jnp.asarray(halves(y_table.transpose(0, 2, 1)))
    forward_x = jnp.asarray(halves(x_table))
    inverse_x = jnp.asarray(halves(x_table.transpose(0, 2, 1)))

    scratch = [pltpu.VMEM((3, 1032, 256), F32), pltpu.VMEM((8, 256, 384), F32), pltpu.VMEM((4, 12, 1024), F32)]
    sent, depth = call(
        first_spread_kernel, (shape(16, 392, 128), shape(64, 8, 128)), [SMEM, VMEM, VMEM], scratch, 40e6
    )(meta, points, forward_y)
    received = [exchange(sent)]
    sent = call(
        functools.partial(spread_kernel, 1), shape(16, 392, 128), [SMEM, VMEM, VMEM, VMEM], scratch, 40e6
    )(meta, points, forward_y, depth)
    received.append(exchange(sent))
    spectra = []
    norms = []
    for pair in range(2):
        spectrum, sent, norm = call(
            functools.partial(spectrum_kernel, pair),
            (shape(2, 3, 2, 64, 1024), shape(16, 392, 128), shape(8, 128)),
            [SMEM, VMEM, VMEM, VMEM],
            [pltpu.VMEM((8, 384, 256), F32), pltpu.VMEM((8, 384, 256), F32), pltpu.VMEM((128, 128), F32)],
            40e6,
        )(meta, received[pair], forward_x, inverse_x)
        spectra.append(spectrum)
        norms.append(norm)
        received[pair] = exchange(sent)
    velocities = [
        call(
            functools.partial(gather_kernel, pair),
            shape(8, 24, 128),
            [SMEM, VMEM, VMEM, VMEM, VMEM],
            [
                pltpu.VMEM((3, 1040, 256), BF16),
                pltpu.VMEM((3, 1040, 256), BF16),
                pltpu.VMEM((8, 256, 384), F32),
                pltpu.VMEM((8, 6, 256), F32),
                pltpu.VMEM((4, 12, 1024), F32),
            ],
            40e6,
        )(meta, points, depth, received[pair], inverse_y)
        for pair in range(2)
    ]
    velocity = lax.all_to_all(velocities[0] + velocities[1], "col", 0, 0, tiled=True)
    velocity, sums = call(sums_kernel, (shape(3, 1024), shape(16, 8, 128)), [SMEM] + [VMEM] * 3, traffic=1e6)(
        block_count, velocity, *norms
    )
    sums = lax.all_to_all(sums, "row", 0, 0, tiled=True)
    sums = spread_out(jnp.sum(sums, axis=0), "col")
    return pl.pallas_call(
        final_kernel,
        grid=(2, 3),
        out_shape=(shape(2, 3, 4, 64, 1024), shape(3, 1024)),
        in_specs=[VMEM] * 5,
        out_specs=(pl.BlockSpec((1, 1, 4, 64, 1024), lambda i, j: (i, j, 0, 0, 0)), VMEM),
        cost_estimate=pl.CostEstimate(flops=0, bytes_accessed=13_000_000, transcendentals=0),
        compiler_params=pltpu.CompilerParams(vmem_limit_bytes=VMEM_LIMIT),
    )(sums, residual, velocity, *spectra)


def solution(mesh):
    in_specs = (
        P(None, ("row", "col")),
        P(None, ("row", "col")),
        P(("row", "col")),
        P(("row", "col")),
    )
    out_specs = (P(None, None, "col", "row", None), P(None, ("row", "col")))
    return jax.shard_map(body, mesh=mesh, in_specs=in_specs, out_specs=out_specs, check_vma=False)
```

time: 322 us -> 292 us (0.907)
  blocking collectives: 162 us -> 34.7 us
  waiting for transfers between devices: 24.6 us -> 103 us
  Pallas kernels: 95.2 us -> 119 us
  other arithmetic: 13.5 us -> 1.53 us
  starting transfers between devices: 22.2 us -> 27.1 us
    all_to_all x2, blocking collectives: 152 us -> 24.6 us  [the longest x1 14.4 us: body(): lax.all_to_all(velocities[0] + velocities[1], 'col', 0, 0, tiled=True)]
    all_to_all x3 -> x5, waiting for transfers between devices: 15.3 us -> 103 us  [the longest x4 96.7 us: exchange(): return lax.all_to_all(value, 'row', 0, 0, tiled=True)]
    pallas_call x5 -> x9, Pallas kernels: 95.2 us -> 119 us  [the longest x2 47.5 us: body(): call(functools.partial(spectrum_kernel, pair), (shape(2, 3, 2, 64, 1024),...]
    ppermute x2 -> x0, waiting for transfers between devices: 9.28 us -> none  [shifted(): lax.ppermute(value, axis, [(source, (source + steps) % count) for source...]
    mul x2 -> x0, other arithmetic: 7.58 us -> none  [the longest x1 6.86 us: body(): vorticity = spectrum * (step_length * (1.0 / math.sqrt(CELLS)))]
    all_to_all x3 -> x5, starting transfers between devices: 21 us -> 27.1 us  [the longest x4 20.2 us: exchange(): return lax.all_to_all(value, 'row', 0, 0, tiled=True)]
    unnamed x12 -> x10, local copies, waits for them, and re-layouts: 1.29 us -> 5.06 us
  transfers between devices with their start and end apart: 5 -> 5, of which waited for: 5 -> 5; matrix products, arithmetic and copies ran while one was open for 0% -> 0% of each run, Pallas kernels for 0% -> 27%
where the time goes in v2:
time: 292 us
  Pallas kernels  119 us (41%)
  waiting for transfers between devices  103 us (35%)
  blocking collectives  34.7 us (12%)
  starting transfers between devices  27.1 us (9%)
  local copies, waits for them, and re-layouts  5.26 us (2%)
    all_to_all x4, waiting for transfers between devices, exchange(): return lax.all_to_all(value, 'row', 0, 0, tiled=True)  96.7 us
    pallas_call x2, Pallas kernels, body(): call(functools.partial(spectrum_kernel, pair), (shape(2, 3, 2, 64, 1024),...  47.5 us
    pallas_call x2, Pallas kernels, body(): call(functools.partial(gather_kernel, pair), shape(8, 24, 128), [SMEM, VM...  27.7 us
    all_to_all x4, starting transfers between devices, exchange(): return lax.all_to_all(value, 'row', 0, 0, tiled=True)  20.2 us
    pallas_call x1, Pallas kernels, body(): call(first_spread_kernel, (shape(16, 392, 128), shape(64, 8, 128)), [SMEM...  17.7 us
    pallas_call x1, Pallas kernels, body(): call(functools.partial(spread_kernel, 1), shape(16, 392, 128), [SMEM, VME...  16.5 us
    all_to_all x1, blocking collectives, body(): lax.all_to_all(velocities[0] + velocities[1], 'col', 0, 0, tiled=True)  14.4 us
    all_to_all x1, blocking collectives, body(): sums = lax.all_to_all(sums, 'row', 0, 0, tiled=True)  10.2 us
  transfers between devices with their start and end apart: 5, of which 5 were waited for; matrix products, arithmetic and copies ran while one was open for 0% of the time, Pallas kernels for 27%

profile of v2, /device:TPU:1, one launch (start us, length us, event | category | flops | bytes accessed | tf_op | source)
XLA Modules:
  0.0 291.6 jit_solution(14146433386968547432)
XLA Ops:
  0.6 1.5 shard_map.95
  2.2 6.8 %all-to-all-start = ((f32[8,8,1024]{2,1,0:T(8,128)}), f32[8,8,1024]{2,1,0:T(8,128)S(1)}, u32[]{:S(2)}, u32[]{:S(2)}) async-start(f32[8,8,1024]{2,1,0:T(8,128)} %get-tuple-element.14), calls=%async_computation | async-start | bytes 524288 | tf_op jit(solution)/shard_map/all_to_all | solution.py:494
  9.0 6.5 %all-to-all-done.points = f32[8,8,1024]{2,1,0:T(8,128)S(1)} async-done(((f32[8,8,1024]{2,1,0:T(8,128)}), f32[8,8,1024]{2,1,0:T(8,128)S(1)}, u32[]{:S(2)}, u32[]{:S(2)}) %all-to-all-start) | async-done | bytes 262176 | tf_op jit(solution)/shard_map/all_to_all | solution.py:494
  15.5 0.0 copy-start.3
  15.5 0.1 slice.3
  15.6 0.1 convert_element_type.7
  15.7 0.6 pad_add_fusion.meta
  16.3 0.0 copy-done.3
  16.3 17.7 %shard_map.96 = (f32[16,392,128]{2,1,0:T(8,128)}, f32[64,8,128]{2,1,0:T(8,128)}) custom-call(s32[66]{0:T(128)} %pad_add_fusion.meta, f32[8,8,1024]{2,1,0:T(8,128)} %copy-done.3, bf16[2,8,256,256]{3,2,1,0:T(8,128)(2,1)} %constant.19.clone.table), custom_call_target="tpu_custom_call" | custom-call | bytes 40000000 | tf_op jit(solution)/shard_map/pallas_call | solution.py:505
  34.0 6.8 %all-to-all-start.1 = ((f32[16,392,128]{2,1,0:T(8,128)}), f32[16,392,128]{2,1,0:T(8,128)S(1)}, u32[]{:S(2)}, u32[]{:S(2)}) async-start(f32[16,392,128]{2,1,0:T(8,128)} %get-tuple-element.16), calls=%async_computation.1 | async-start | bytes 6422528 | tf_op jit(solution)/shard_map/all_to_all | solution.py:485
  40.7 16.5 %shard_map.99 = f32[16,392,128]{2,1,0:T(8,128)} custom-call(s32[66]{0:T(128)} %pad_add_fusion.meta, f32[8,8,1024]{2,1,0:T(8,128)} %copy-done.3, bf16[2,8,256,256]{3,2,1,0:T(8,128)(2,1)} %constant.19.clone.table, f32[64,8,128]{2,1,0:T(8,128)} %get-tuple-element.15.depth), custom_call_target="tpu_custom_call" | custom-call | bytes 40000000 | tf_op jit(solution)/shard_map/pallas_call | solution.py:509
  57.2 30.1 %all-to-all-done.1.received = f32[16,392,128]{2,1,0:T(8,128)S(1)} async-done(((f32[16,392,128]{2,1,0:T(8,128)}), f32[16,392,128]{2,1,0:T(8,128)S(1)}, u32[]{:S(2)}, u32[]{:S(2)}) %all-to-all-start.1) | async-done | bytes 3211296 | tf_op jit(solution)/shard_map/all_to_all | solution.py:485
  87.4 0.0 copy-start.2
  87.4 1.7 copy-done.2
  89.1 3.7 %all-to-all-start.3 = ((f32[16,392,128]{2,1,0:T(8,128)}), f32[16,392,128]{2,1,0:T(8,128)S(1)}, u32[]{:S(2)}, u32[]{:S(2)}) async-start(f32[16,392,128]{2,1,0:T(8,128)} %shard_map.99), calls=%async_computation.3 | async-start | bytes 6422528 | tf_op jit(solution)/shard_map/all_to_all | solution.py:485
  92.8 23.8 %shard_map.97 = (f32[2,3,2,64,1024]{4,3,2,1,0:T(8,128)}, f32[16,392,128]{2,1,0:T(8,128)}, f32[8,128]{1,0:T(8,128)}) custom-call(s32[66]{0:T(128)} %pad_add_fusion.meta, f32[16,392,128]{2,1,0:T(8,128)} %copy-done.2, bf16[2,8,256,256]{3,2,1,0:T(8,128)(2,1)} %constant.21.clone.table, bf16[2,8,256,256]{3,2,1,0:T(8,128)(2,1)} %constant.22.clone.table_back), custom_call_target="tpu_custom_call" | custom-call | bytes 40000000 | tf_op jit(solution)/shard_map/pallas_call | solution.py:516
  116.6 19.4 %all-to-all-done.3.received = f32[16,392,128]{2,1,0:T(8,128)S(1)} async-done(((f32[16,392,128]{2,1,0:T(8,128)}), f32[16,392,128]{2,1,0:T(8,128)S(1)}, u32[]{:S(2)}, u32[]{:S(2)}) %all-to-all-start.3) | async-done | bytes 3211296 | tf_op jit(solution)/shard_map/all_to_all | solution.py:485
  136.0 0.0 copy-start.1
  136.0 1.7 copy-done.1
  137.7 5.2 %all-to-all-start.2 = ((f32[16,392,128]{2,1,0:T(8,128)}), f32[16,392,128]{2,1,0:T(8,128)S(1)}, u32[]{:S(2)}, u32[]{:S(2)}) async-start(f32[16,392,128]{2,1,0:T(8,128)} %get-tuple-element.17), calls=%async_computation.2 | async-start | bytes 6422528 | tf_op jit(solution)/shard_map/all_to_all | solution.py:485
  142.9 23.7 %shard_map.100 = (f32[2,3,2,64,1024]{4,3,2,1,0:T(8,128)}, f32[16,392,128]{2,1,0:T(8,128)}, f32[8,128]{1,0:T(8,128)}) custom-call(s32[66]{0:T(128)} %pad_add_fusion.meta, f32[16,392,128]{2,1,0:T(8,128)} %copy-done.1, bf16[2,8,256,256]{3,2,1,0:T(8,128)(2,1)} %constant.21.clone.table, bf16[2,8,256,256]{3,2,1,0:T(8,128)(2,1)} %constant.22.clone.table_back), custom_call_target="tpu_custom_call" | custom-call | bytes 40000000 | tf_op jit(solution)/shard_map/pallas_call | solution.py:516
  166.7 20.6 %all-to-all-done.2.received = f32[16,392,128]{2,1,0:T(8,128)S(1)} async-done(((f32[16,392,128]{2,1,0:T(8,128)}), f32[16,392,128]{2,1,0:T(8,128)S(1)}, u32[]{:S(2)}, u32[]{:S(2)}) %all-to-all-start.2) | async-done | bytes 3211296 | tf_op jit(solution)/shard_map/all_to_all | solution.py:485
  187.3 0.0 copy-start
  187.3 1.7 copy-done
  189.0 4.5 %all-to-all-start.4 = ((f32[16,392,128]{2,1,0:T(8,128)}), f32[16,392,128]{2,1,0:T(8,128)}, u32[]{:S(2)}, u32[]{:S(2)}) async-start(f32[16,392,128]{2,1,0:T(8,128)} %get-tuple-element.18), calls=%async_computation.4 | async-start | bytes 6422528 | tf_op jit(solution)/shard_map/all_to_all | solution.py:485
  193.5 13.9 %shard_map.98 = f32[8,24,128]{2,1,0:T(8,128)} custom-call(s32[66]{0:T(128)} %pad_add_fusion.meta, f32[8,8,1024]{2,1,0:T(8,128)} %copy-done.3, f32[64,8,128]{2,1,0:T(8,128)} %get-tuple-element.15.depth, f32[16,392,128]{2,1,0:T(8,128)} %copy-done, bf16[2,8,256,256]{3,2,1,0:T(8,128)(2,1)} %constant.20.clone.table), custom_call_target="tpu_custom_call" | custom-call | bytes 40000000 | tf_op jit(solution)/shard_map/pallas_call | solution.py:527
  207.4 0.0 copy-start.4
  207.4 26.5 %all-to-all-done.4.received = f32[16,392,128]{2,1,0:T(8,128)} async-done(((f32[16,392,128]{2,1,0:T(8,128)}), f32[16,392,128]{2,1,0:T(8,128)}, u32[]{:S(2)}, u32[]{:S(2)}) %all-to-all-start.4) | async-done | bytes 3211296 | tf_op jit(solution)/shard_map/all_to_all | solution.py:485
  233.9 13.9 %shard_map.101 = f32[8,24,128]{2,1,0:T(8,128)} custom-call(s32[66]{0:T(128)} %pad_add_fusion.meta, f32[8,8,1024]{2,1,0:T(8,128)} %copy-done.3, f32[64,8,128]{2,1,0:T(8,128)} %get-tuple-element.15.depth, f32[16,392,128]{2,1,0:T(8,128)} %all-to-all-done.4.received, bf16[2,8,256,256]{3,2,1,0:T(8,128)(2,1)} %constant.20.clone.table), custom_call_target="tpu_custom_call" | custom-call | bytes 40000000 | tf_op jit(solution)/shard_map/pallas_call | solution.py:527
  247.7 0.0 copy-done.4
  247.7 0.9 add.3
  248.7 14.4 %all_to_all.40.received = f32[8,24,128]{2,1,0:T(8,128)} all-to-all(f32[8,24,128]{2,1,0:T(8,128)S(1)} %add.3), channel_id=1, replica_groups=mesh['row'=16,'col'=8] {'col'}, dimensions={0} | all-to-all | bytes 196608 | tf_op jit(solution)/shard_map/all_to_all | solution.py:542
  263.1 1.6 shard_map.102
  264.7 10.2 %all_to_all.41 = f32[16,8,128]{2,1,0:T(8,128)S(1)} all-to-all(f32[16,8,128]{2,1,0:T(8,128)} %get-tuple-element.21), channel_id=1, replica_groups=mesh['row'=16,'col'=8] {'row'}, dimensions={0} | all-to-all | bytes 131072 | tf_op jit(solution)/shard_map/all_to_all | solution.py:546
  274.9 10.0 %all_to_all.42.sums = f32[8,8,128]{2,1,0:T(8,128)} all-to-all(f32[8,8,128]{2,1,0:T(8,128)S(1)} %broadcast_in_dim.2), channel_id=1, replica_groups=mesh['row'=16,'col'=8] {'col'}, dimensions={0} | all-to-all | bytes 65536 | tf_op jit(solution)/shard_map/all_to_all | solution.py:481
  284.9 6.7 %shard_map.103 = (f32[2,3,4,64,1024]{4,3,2,1,0:T(8,128)}, f32[3,1024]{1,0:T(4,128)}) custom-call(f32[8,8,128]{2,1,0:T(8,128)} %all_to_all.42.sums, f32[3,1024]{1,0:T(4,128)} %get-tuple-element.22.residual, f32[3,1024]{1,0:T(4,128)} %get-tuple-element.23.velocity, f32[2,3,2,64,1024]{4,3,2,1,0:T(8,128)} %get-tuple-element.24.first, ...), custom_call_target="tpu_custom_call" | custom-call | bytes 13000000 | tf_op jit(solution)/shard_map/pallas_call | solution.py:548
  (3 shorter events, 0.0 us)
Async XLA Ops:
  2.2 13.3 %all-to-all-start = ((f32[8,8,1024]{2,1,0:T(8,128)}), f32[8,8,1024]{2,1,0:T(8,128)S(1)}, u32[]{:S(2)}, u32[]{:S(2)}) async-start(f32[8,8,1024]{2,1,0:T(8,128)} %get-tuple-element.14), calls=%async_computation | async-start | bytes 524288 | tf_op jit(solution)/shard_map/all_to_all | solution.py:494
  15.5 0.8 copy-start.3
  34.0 53.4 %all-to-all-start.1 = ((f32[16,392,128]{2,1,0:T(8,128)}), f32[16,392,128]{2,1,0:T(8,128)S(1)}, u32[]{:S(2)}, u32[]{:S(2)}) async-start(f32[16,392,128]{2,1,0:T(8,128)} %get-tuple-element.16), calls=%async_computation.1 | async-start | bytes 6422528 | tf_op jit(solution)/shard_map/all_to_all | solution.py:485
  87.4 1.7 copy-start.2
  89.1 46.9 %all-to-all-start.3 = ((f32[16,392,128]{2,1,0:T(8,128)}), f32[16,392,128]{2,1,0:T(8,128)S(1)}, u32[]{:S(2)}, u32[]{:S(2)}) async-start(f32[16,392,128]{2,1,0:T(8,128)} %shard_map.99), calls=%async_computation.3 | async-start | bytes 6422528 | tf_op jit(solution)/shard_map/all_to_all | solution.py:485
  136.0 1.7 copy-start.1
  137.7 49.6 %all-to-all-start.2 = ((f32[16,392,128]{2,1,0:T(8,128)}), f32[16,392,128]{2,1,0:T(8,128)S(1)}, u32[]{:S(2)}, u32[]{:S(2)}) async-start(f32[16,392,128]{2,1,0:T(8,128)} %get-tuple-element.17), calls=%async_computation.2 | async-start | bytes 6422528 | tf_op jit(solution)/shard_map/all_to_all | solution.py:485
  187.3 1.7 copy-start
  189.0 44.9 %all-to-all-start.4 = ((f32[16,392,128]{2,1,0:T(8,128)}), f32[16,392,128]{2,1,0:T(8,128)}, u32[]{:S(2)}, u32[]{:S(2)}) async-start(f32[16,392,128]{2,1,0:T(8,128)} %get-tuple-element.18), calls=%async_computation.4 | async-start | bytes 6422528 | tf_op jit(solution)/shard_map/all_to_all | solution.py:485
  207.4 40.4 %copy-start.4 = (f32[8,24,128]{2,1,0:T(8,128)S(1)}, f32[8,24,128]{2,1,0:T(8,128)}, u32[]{:S(2)}) copy-start(f32[8,24,128]{2,1,0:T(8,128)} %shard_map.98) | copy-start | bytes 294916

commit v3 on v2

--- a/solution.py
+++ b/solution.py
@@ -17,16 +17,19 @@
 TWO_PI = 2.0 * math.pi
 F32 = jnp.float32
 BF16 = jnp.bfloat16
-VMEM_LIMIT = 56 * 1024 * 1024
+VMEM_LIMIT = 64 * 1024 * 1024
 VMEM = pl.BlockSpec(memory_space=pltpu.VMEM)
 SMEM = pl.BlockSpec(memory_space=pltpu.SMEM)
+ANY = pl.BlockSpec(memory_space=pl.ANY)
+TABLE = pltpu.VMEM((8, 2, 256, 256), BF16)
+BLOCKS = pltpu.VMEM((16, 392, 128), F32)
 
 
 def halves(table):
     table = table.astype(np.float32)
     high = table.astype(ml_dtypes.bfloat16)
     low = (table - high.astype(np.float32)).astype(ml_dtypes.bfloat16)
-    return np.stack([high, low])
+    return np.stack([high, low], 1)
 
 
 def table_y():
@@ -61,6 +64,12 @@
 
 def mul_t(left, right):
     return lax.dot_general(left, right, (((1,), (1,)), ((), ())), preferred_element_type=F32)
+
+
+def doubled(high, low):
+    return jnp.concatenate(
+        [jnp.concatenate([high, high], 1), jnp.concatenate([low, jnp.zeros_like(low)], 1)], 0
+    )
 
 
 def small_dft(values, sign):
@@ -135,12 +144,11 @@
         depth[block] = (1.0 - part) * wave(cell) + part * wave(cell + 1)
         return carry
 
-    lax.fori_loop(0, 64, step, 0, unroll=4)
-
-
-def edge_weights(point):
-    weight = hat(ramp((40, 128), 0) - point[1:2])
-    return jnp.concatenate([weight, jnp.zeros((88, 128), F32)], 0)
+    lax.fori_loop(0, 64, step, 0, unroll=32)
+
+
+def edge_weights(along):
+    return jnp.concatenate([along[:40], jnp.zeros((88, 128), F32)], 0)
 
 
 def edge_waves(point, waves, place_x):
@@ -175,12 +183,23 @@
     return jnp.concatenate([waves[i : i + 1] * across for i in range(4)], 0)
 
 
-def first_spread_kernel(meta, points, table, out, depth, field, parts, windows):
+def first_spread_kernel(meta, points, table, out, depth, *scratch):
     depth_wave(points, meta, depth)
-    spread_kernel(0, meta, points, table, depth, out, field, parts, windows)
-
-
-def spread_kernel(pair, meta, points, table, depth, out, field, parts, windows):
+    spread_kernel(0, meta, points, table, depth, out, *scratch)
+
+
+def spread_kernel(
+    pair, meta, points, far_table, depth, far_out, field, parts, windows, table, out, table_done, out_done
+):
+    def table_copy(k):
+        return pltpu.make_async_copy(far_table.at[k], table.at[k], table_done.at[k])
+
+    def out_copy(k):
+        at = pl.ds(2 * k, 2)
+        return pltpu.make_async_copy(out.at[at], far_out.at[at], out_done.at[k])
+
+    for k in range(8):
+        table_copy(k).start()
     field[...] = jnp.zeros_like(field)
     windows[...] = jnp.zeros_like(windows)
 
@@ -192,20 +211,21 @@
         along = hat(ramp((40, 128), 0) - point[1:2])
         source = jnp.concatenate([along * point[3 + c : 4 + c] for c in range(3)], 0)
         source_high, source_low = split(source)
-        both = mul_t(jnp.concatenate([source_high, source_low], 0), weight_high)
-        value = both[:120] + both[120:] + mul_t(source_high, weight_low)
+        both = mul_t(doubled(source_high, source_low), jnp.concatenate([weight_high, weight_low], 1))
+        value = both[:120] + both[120:]
         row = pl.multiple_of(place_y * 32, 32)
         for c in range(3):
             field[c, pl.ds(row, 40), :] += value[40 * c : 40 * c + 40]
         waves = edge_waves(point, waves, place_x)
         source_high, source_low = split(jnp.concatenate([waves[i : i + 1] * point[3:6] for i in range(4)], 0))
-        weight_high, weight_low = split(edge_weights(point))
-        value = mul_t(source_high, weight_high) + mul_t(source_low, weight_high) + mul_t(source_high, weight_low)
+        weight_high, weight_low = split(edge_weights(along))
+        both = mul_t(doubled(source_high, source_low), jnp.concatenate([weight_high, weight_low], 1))
+        value = both[:12] + both[12:]
         lane = pl.multiple_of(place_y // 4 * 128, 128)
         windows[place_y % 4, :, pl.ds(lane, 128)] += value
         return carry
 
-    lax.fori_loop(0, 64, step, 0, unroll=4)
+    lax.fori_loop(0, 64, step, 0, unroll=32)
     for c in range(3):
         field[c, 0:1, :] += field[c, 1024:1025, :]
 
@@ -230,10 +250,11 @@
         windows[k // 2, 0:6, 256 * (k % 2) : 256 * (k % 2) + 256] = jnp.concatenate(pieces, 1)
 
     def inner(k, carry):
+        table_copy(k).wait()
         high, low = split(parts[k])
-        value = mul(table[0, k], high) + mul(table[1, k], high) + mul(table[0, k], low)
+        value = mul(table[k, 0], high) + mul(table[k, 1], high) + mul(table[k, 0], low)
         high, low = split(windows[k // 2, 0:6, pl.ds(pl.multiple_of(256 * (k % 2), 256), 256)])
-        edge = mul_t(high, table[0, k]) + mul_t(high, table[1, k]) + mul_t(low, table[0, k])
+        edge = mul_t(high, table[k, 0]) + mul_t(high, table[k, 1]) + mul_t(low, table[k, 0])
         edge_real = joined(edge[0:3, 0:128], edge[3:6, 0:128])
         edge_imag = joined(edge[0:3, 128:256], edge[3:6, 128:256])
         for half in range(2):
@@ -245,12 +266,24 @@
             out[2 * k + half, 384:392] = jnp.concatenate(
                 [edge_real[half], edge_imag[half], jnp.zeros((2, 128), F32)], 0
             )
-        return carry
-
-    lax.fori_loop(0, 8, inner, 0, unroll=2)
-
-
-def spectrum_kernel(pair, meta, received, table, table_back, spectrum, out, norm, parts, back, edge):
+        out_copy(k).start()
+        return carry
+
+    lax.fori_loop(0, 8, inner, 0)
+    for k in range(8):
+        out_copy(k).wait()
+
+
+def spectrum_kernel(
+    pair, meta, far_received, table, table_back, spectrum, out, norm, parts, back, edge, received, done
+):
+    def copy(c):
+        at = pl.ds(128 * c, 128 if c < 3 else 8)
+        return pltpu.make_async_copy(far_received.at[:, at], received.at[:, at], done.at[c])
+
+    for c in (3, 0, 1, 2):
+        copy(c).start()
+    copy(3).wait()
     row = meta[64]
     lane = lax.broadcasted_iota(jnp.int32, (8, 128), 1)
     edge[...] = jnp.concatenate([received[s, 384:392] for s in range(16)], 0).T
@@ -263,18 +296,19 @@
             lane == 0, first, jnp.where(lane == 64, second, 0.0)
         )
 
-    def outer(tile, carry):
+    def outer(c, tile, carry):
         at = pl.multiple_of(tile * 8, 8)
-        for c in range(3):
-            values = [(placed(at, s, c), placed(at, s, 3 + c)) for s in range(16)]
-            for k, (real, imag) in enumerate(small_dft(values, -1)):
-                to = 128 * (k // 8)
-                first, second = joined(real, imag)
-                parts[k % 8, pl.ds(128 * c + at, 8), to : to + 128] = first
-                parts[k % 8, pl.ds(128 * c + 64 + at, 8), to : to + 128] = second
-        return carry
-
-    lax.fori_loop(0, 8, outer, 0)
+        values = [(placed(at, s, c), placed(at, s, 3 + c)) for s in range(16)]
+        for k, (real, imag) in enumerate(small_dft(values, -1)):
+            to = 128 * (k // 8)
+            first, second = joined(real, imag)
+            parts[k % 8, pl.ds(128 * c + at, 8), to : to + 128] = first
+            parts[k % 8, pl.ds(128 * c + 64 + at, 8), to : to + 128] = second
+        return carry
+
+    for c in range(3):
+        copy(c).wait()
+        lax.fori_loop(0, 8, functools.partial(outer, c), 0)
 
     index_y = 8 * (64 * (row % 2) + lax.broadcasted_iota(jnp.int32, (64, 128), 0)) + row // 2
     lane_x = lax.broadcasted_iota(jnp.int32, (64, 128), 1)
@@ -282,7 +316,7 @@
 
     def inner(k, total):
         high, low = split(parts[k])
-        value = mul(high, table[0, k]) + mul(low, table[0, k]) + mul(high, table[1, k])
+        value = mul(high, table[k, 0]) + mul(low, table[k, 0]) + mul(high, table[k, 1])
         index_x = 8 * lane_x + k
         wave_x = jnp.where(index_x < NX // 2, index_x, index_x - NX).astype(F32) * (TWO_PI / NX)
         flat = wave_x * wave_x + wave_y * wave_y
@@ -321,7 +355,7 @@
             for c in range(3):
                 rows[c][h] = jnp.concatenate([back_real[c], back_imag[c]], 1)
         high, low = split(jnp.concatenate([rows[c][h] for c in range(3) for h in range(2)], 0))
-        back[k] = mul(high, table_back[0, k]) + mul(low, table_back[0, k]) + mul(high, table_back[1, k])
+        back[k] = mul(high, table_back[k, 0]) + mul(low, table_back[k, 0]) + mul(high, table_back[k, 1])
         return total
 
     total = lax.fori_loop(0, 8, inner, jnp.zeros((64, 128), F32))
@@ -354,8 +388,28 @@
         out[s, 384:392] = turned[8 * s : 8 * s + 8]
 
 
-def gather_kernel(pair, meta, points, depth, received, table, out, field_high, field_low, parts, edge, windows):
+def first_gather_kernel(meta, points, depth, received, table, out, *scratch):
+    gather_kernel(0, meta, points, depth, None, received, table, out, *scratch)
+
+
+def gather_kernel(
+    pair, meta, points, depth, earlier, far_received, far_table, out,
+    field_high, field_low, parts, edge, windows, table, received, table_done, received_done,
+):
+    def table_copy(k):
+        return pltpu.make_async_copy(far_table.at[k], table.at[k], table_done.at[k])
+
+    def received_copy(k):
+        at = pl.ds(2 * k, 2)
+        return pltpu.make_async_copy(far_received.at[at], received.at[at], received_done.at[k])
+
+    for k in range(8):
+        table_copy(k).start()
+        received_copy(k).start()
+
     def inner(k, carry):
+        table_copy(k).wait()
+        received_copy(k).wait()
         columns = [
             jnp.concatenate(
                 [
@@ -368,15 +422,15 @@
             for c in range(3)
         ]
         high, low = split(jnp.concatenate(columns, 1))
-        parts[k] = mul(table[0, k], high) + mul(table[1, k], high) + mul(table[0, k], low)
+        parts[k] = mul(table[k, 0], high) + mul(table[k, 1], high) + mul(table[k, 0], low)
         first, second = joined(received[2 * k, 384:392], received[2 * k + 1, 384:392])
         real = jnp.concatenate([first[0:3], second[0:3]], 0)
         imag = jnp.concatenate([first[3:6], second[3:6]], 0)
         high, low = split(jnp.concatenate([real, imag], 1))
-        edge[k] = mul_t(high, table[0, k]) + mul_t(high, table[1, k]) + mul_t(low, table[0, k])
-        return carry
-
-    lax.fori_loop(0, 8, inner, 0, unroll=2)
+        edge[k] = mul_t(high, table[k, 0]) + mul_t(high, table[k, 1]) + mul_t(low, table[k, 0])
+        return carry
+
+    lax.fori_loop(0, 8, inner, 0)
     values = [(edge[k, :, 0:128], edge[k, :, 128:256]) for k in range(8)]
     plane = jnp.concatenate([jnp.concatenate(pieces, 0) for pieces in small_dft(values, 1)], 1)
     for j in range(4):
@@ -417,16 +471,20 @@
         value = both[:, :128] + both[:, 128:] + mul(low, weight_high)
         velocity = [jnp.sum(along * value[48 * c : 48 * c + 48], axis=0, keepdims=True) for c in range(3)]
         waves = edge_waves(point, waves, place_x)
-        weight_high, weight_low = split(edge_weights(point))
+        weight_high, weight_low = split(edge_weights(along))
         lane = pl.multiple_of(place_y // 4 * 128, 128)
         high, low = split(windows[place_y % 4, :, pl.ds(lane, 128)])
         value = mul(high, weight_high) + mul(low, weight_high) + mul(high, weight_low)
         more = sum(waves[i : i + 1] * value[3 * i : 3 * i + 3] for i in range(4))
         for c in range(3):
-            out[block // 8, pl.ds(8 * c + block % 8, 1), :] = velocity[c] + more[c : c + 1]
-        return carry
-
-    lax.fori_loop(0, 64, step, 0, unroll=4)
+            at = pl.ds(8 * c + block % 8, 1)
+            total = velocity[c] + more[c : c + 1]
+            if earlier is not None:
+                total = total + earlier[block // 8, at, :]
+            out[block // 8, at, :] = total
+        return carry
+
+    lax.fori_loop(0, 64, step, 0, unroll=32)
 
 
 def sums_kernel(counts, received, first_norm, second_norm, velocity, out):
@@ -451,22 +509,40 @@
         out[dest] = tile
 
 
-def final_kernel(sums, residual, velocity, first, second, spectrum, out):
+def final_kernel(sums, residual, velocity, first, second, spectrum, out, values, loaded, stored):
+    def load(i):
+        source = (first, second)[i % 2]
+        return pltpu.make_async_copy(source.at[i // 6, i // 2 % 3], values.at[i], loaded.at[i])
+
+    def store(i):
+        place = spectrum.at[i // 6, i // 2 % 3, pl.ds(i % 2 * 2, 2)]
+        return pltpu.make_async_copy(values.at[i], place, stored.at[i])
+
+    for i in range(12):
+        load(i).start()
     total = jnp.sum(jnp.sum(sums[...], axis=0), axis=1, keepdims=True)
     length = total[0:1] / total[1:2]
-    part, c = pl.program_id(0), pl.program_id(1)
     scale = length * (1.0 / math.sqrt(CELLS))
-    spectrum[0, 0, 0:2] = first[part, c] * scale
-    spectrum[0, 0, 2:4] = second[part, c] * scale
+    for i in range(12):
+        load(i).wait()
+        values[i] = values[i] * scale
+        store(i).start()
     out[...] = residual[...] - length * velocity[...]
-
-
-def call(kernel, outs, specs, scratch=(), traffic=0):
+    for i in range(12):
+        store(i).wait()
+
+
+def filled(kernel):
+    return lambda *refs: kernel(*refs[:-1])
+
+
+def call(kernel, outs, specs, scratch=(), traffic=0, out_specs=VMEM, fill=1):
     return pl.pallas_call(
-        kernel,
+        filled(kernel),
         out_shape=outs,
         in_specs=specs,
-        scratch_shapes=list(scratch),
+        out_specs=out_specs,
+        scratch_shapes=list(scratch) + [pltpu.VMEM((fill * 2048, 128), F32)],
         cost_estimate=pl.CostEstimate(flops=0, bytes_accessed=int(traffic), transcendentals=0),
         compiler_params=pltpu.CompilerParams(vmem_limit_bytes=VMEM_LIMIT),
     )
@@ -489,7 +565,7 @@
     row = lax.axis_index("row")
     col = lax.axis_index("col")
     packed, residual = call(
-        pack_kernel, (shape(8, 8, 1024), shape(3, 1024)), [VMEM, VMEM, SMEM, SMEM], traffic=1e6
+        pack_kernel, (shape(8, 8, 1024), shape(3, 1024)), [VMEM, VMEM, SMEM, SMEM], traffic=1e6, out_specs=(VMEM, VMEM)
     )(offsets, measured, block_brick, block_count)
     points = lax.all_to_all(packed, "col", 0, 0, tiled=True)
     bricks = points[:, 6, ::128].reshape(64).astype(jnp.int32)
@@ -501,13 +577,27 @@
     forward_x = jnp.asarray(halves(x_table))
     inverse_x = jnp.asarray(halves(x_table.transpose(0, 2, 1)))
 
-    scratch = [pltpu.VMEM((3, 1032, 256), F32), pltpu.VMEM((8, 256, 384), F32), pltpu.VMEM((4, 12, 1024), F32)]
+    eight = pltpu.SemaphoreType.DMA((8,))
+    scratch = [
+        pltpu.VMEM((3, 1032, 256), F32),
+        pltpu.VMEM((8, 256, 384), F32),
+        pltpu.VMEM((4, 12, 1024), F32),
+        TABLE,
+        BLOCKS,
+        eight,
+        eight,
+    ]
     sent, depth = call(
-        first_spread_kernel, (shape(16, 392, 128), shape(64, 8, 128)), [SMEM, VMEM, VMEM], scratch, 40e6
+        first_spread_kernel,
+        (shape(16, 392, 128), shape(64, 8, 128)),
+        [SMEM, VMEM, ANY],
+        scratch,
+        40e6,
+        (ANY, VMEM),
     )(meta, points, forward_y)
     received = [exchange(sent)]
     sent = call(
-        functools.partial(spread_kernel, 1), shape(16, 392, 128), [SMEM, VMEM, VMEM, VMEM], scratch, 40e6
+        functools.partial(spread_kernel, 1), shape(16, 392, 128), [SMEM, VMEM, ANY, VMEM], scratch, 40e6, ANY, 48
     )(meta, points, forward_y, depth)
     received.append(exchange(sent))
     spectra = []
@@ -516,43 +606,52 @@
         spectrum, sent, norm = call(
             functools.partial(spectrum_kernel, pair),
             (shape(2, 3, 2, 64, 1024), shape(16, 392, 128), shape(8, 128)),
-            [SMEM, VMEM, VMEM, VMEM],
-            [pltpu.VMEM((8, 384, 256), F32), pltpu.VMEM((8, 384, 256), F32), pltpu.VMEM((128, 128), F32)],
+            [SMEM, ANY, VMEM, VMEM],
+            [
+                pltpu.VMEM((8, 384, 256), F32),
+                pltpu.VMEM((8, 384, 256), F32),
+                pltpu.VMEM((128, 128), F32),
+                BLOCKS,
+                pltpu.SemaphoreType.DMA((4,)),
+            ],
             40e6,
+            (VMEM, VMEM, VMEM),
+            40,
         )(meta, received[pair], forward_x, inverse_x)
         spectra.append(spectrum)
         norms.append(norm)
         received[pair] = exchange(sent)
-    velocities = [
-        call(
-            functools.partial(gather_kernel, pair),
-            shape(8, 24, 128),
-            [SMEM, VMEM, VMEM, VMEM, VMEM],
-            [
-                pltpu.VMEM((3, 1040, 256), BF16),
-                pltpu.VMEM((3, 1040, 256), BF16),
-                pltpu.VMEM((8, 256, 384), F32),
-                pltpu.VMEM((8, 6, 256), F32),
-                pltpu.VMEM((4, 12, 1024), F32),
-            ],
-            40e6,
-        )(meta, points, depth, received[pair], inverse_y)
-        for pair in range(2)
+    scratch = [
+        pltpu.VMEM((3, 1040, 256), BF16),
+        pltpu.VMEM((3, 1040, 256), BF16),
+        pltpu.VMEM((8, 256, 384), F32),
+        pltpu.VMEM((8, 6, 256), F32),
+        pltpu.VMEM((4, 12, 1024), F32),
+        TABLE,
+        BLOCKS,
+        eight,
+        eight,
     ]
-    velocity = lax.all_to_all(velocities[0] + velocities[1], "col", 0, 0, tiled=True)
-    velocity, sums = call(sums_kernel, (shape(3, 1024), shape(16, 8, 128)), [SMEM] + [VMEM] * 3, traffic=1e6)(
+    velocity = call(first_gather_kernel, shape(8, 24, 128), [SMEM, VMEM, VMEM, ANY, ANY], scratch, 40e6, VMEM, 48)(
+        meta, points, depth, received[0], inverse_y
+    )
+    velocity = call(
+        functools.partial(gather_kernel, 1), shape(8, 24, 128), [SMEM, VMEM, VMEM, VMEM, ANY, ANY], scratch, 40e6
+    )(meta, points, depth, velocity, received[1], inverse_y)
+    velocity = lax.all_to_all(velocity, "col", 0, 0, tiled=True)
+    velocity, sums = call(sums_kernel, (shape(3, 1024), shape(16, 8, 128)), [SMEM] + [VMEM] * 3, traffic=1e6, out_specs=(VMEM, VMEM))(
         block_count, velocity, *norms
     )
     sums = lax.all_to_all(sums, "row", 0, 0, tiled=True)
     sums = spread_out(jnp.sum(sums, axis=0), "col")
-    return pl.pallas_call(
+    twelve = pltpu.SemaphoreType.DMA((12,))
+    return call(
         final_kernel,
-        grid=(2, 3),
-        out_shape=(shape(2, 3, 4, 64, 1024), shape(3, 1024)),
-        in_specs=[VMEM] * 5,
-        out_specs=(pl.BlockSpec((1, 1, 4, 64, 1024), lambda i, j: (i, j, 0, 0, 0)), VMEM),
-        cost_estimate=pl.CostEstimate(flops=0, bytes_accessed=13_000_000, transcendentals=0),
-        compiler_params=pltpu.CompilerParams(vmem_limit_bytes=VMEM_LIMIT),
+        (shape(2, 3, 4, 64, 1024), shape(3, 1024)),
+        [VMEM, VMEM, VMEM, ANY, ANY],
+        [pltpu.VMEM((12, 2, 64, 1024), F32), twelve, twelve],
+        13e6,
+        (ANY, VMEM),
     )(sums, residual, velocity, *spectra)
 
 

time: 292 us -> 282 us (0.966)
  Pallas kernels: 119 us -> 108 us
  waiting for transfers between devices: 103 us -> 109 us
  local copies, waits for them, and re-layouts: 5.26 us -> 0.9 us
    all_to_all x4, waiting for transfers between devices: 96.7 us -> 103 us  [exchange(): return lax.all_to_all(value, 'row', 0, 0, tiled=True)]
    pallas_call x1, Pallas kernels: 16.5 us -> 11.6 us  [body(): call(functools.partial(spread_kernel, 1), shape(16, 392, 128), [SMEM, VME...]
    pallas_call x1, Pallas kernels: 17.7 us -> 12.9 us  [body(): call(first_spread_kernel, (shape(16, 392, 128), shape(64, 8, 128)), [SMEM...]
    pallas_call x3, Pallas kernels: 34.5 us -> 30.1 us  [the longest x1 11.6 us: body(): call(functools.partial(gather_kernel, 1), shape(8, 24, 128), [SMEM, VMEM,...]
    unnamed x10 -> x2, local copies, waits for them, and re-layouts: 5.06 us -> 0.7 us
  transfers between devices with their start and end apart: 5 -> 5, of which waited for: 5 -> 5; matrix products, arithmetic and copies ran while one was open for 0% -> 0% of each run, Pallas kernels for 27% -> 26%
where the time goes in v3:
time: 282 us; the launch traced here: 281 us
  waiting for transfers between devices  109 us (39%)
  Pallas kernels  108 us (38%)
  blocking collectives  32.2 us (11%)
  starting transfers between devices  29.4 us (10%)
    all_to_all x4, waiting for transfers between devices, exchange(): return lax.all_to_all(value, 'row', 0, 0, tiled=True)  103 us
    pallas_call x2, Pallas kernels, body(): call(functools.partial(spectrum_kernel, pair), (shape(2, 3, 2, 64, 1024),...  50 us
    all_to_all x4, starting transfers between devices, exchange(): return lax.all_to_all(value, 'row', 0, 0, tiled=True)  22.6 us
    pallas_call x1, Pallas kernels, body(): call(first_spread_kernel, (shape(16, 392, 128), shape(64, 8, 128)), [SMEM...  12.9 us
    all_to_all x1, blocking collectives, body(): velocity = lax.all_to_all(velocity, 'col', 0, 0, tiled=True)  12.3 us
    pallas_call x1, Pallas kernels, body(): call(functools.partial(gather_kernel, 1), shape(8, 24, 128), [SMEM, VMEM,...  11.6 us
    pallas_call x1, Pallas kernels, body(): call(first_gather_kernel, shape(8, 24, 128), [SMEM, VMEM, VMEM, ANY, ANY]...  11.6 us
    pallas_call x1, Pallas kernels, body(): call(functools.partial(spread_kernel, 1), shape(16, 392, 128), [SMEM, VME...  11.6 us
  transfers between devices with their start and end apart: 5, of which 5 were waited for; matrix products, arithmetic and copies ran while one was open for 0% of the time, Pallas kernels for 26%

profile of v3, /device:TPU:1, one launch (start us, length us, event | category | flops | bytes accessed | tf_op | source)
XLA Modules:
  0.0 280.9 jit_solution(10322826313040174904)
XLA Ops:
  0.6 1.5 shard_map.95
  2.2 6.8 %all-to-all-start = ((f32[8,8,1024]{2,1,0:T(8,128)}), f32[8,8,1024]{2,1,0:T(8,128)S(1)}, u32[]{:S(2)}, u32[]{:S(2)}) async-start(f32[8,8,1024]{2,1,0:T(8,128)} %get-tuple-element.14), calls=%async_computation | async-start | bytes 524288 | tf_op jit(solution)/shard_map/all_to_all | solution.py:570
  9.0 6.5 %all-to-all-done.refs_1_ = f32[8,8,1024]{2,1,0:T(8,128)S(1)} async-done(((f32[8,8,1024]{2,1,0:T(8,128)}), f32[8,8,1024]{2,1,0:T(8,128)S(1)}, u32[]{:S(2)}, u32[]{:S(2)}) %all-to-all-start) | async-done | bytes 262176 | tf_op jit(solution)/shard_map/all_to_all | solution.py:570
  15.5 0.0 copy-start
  15.5 0.7 copy-done
  16.2 0.1 slice.3
  16.3 0.1 convert_element_type.7
  16.4 0.7 pad_add_fusion.refs_0_
  17.1 12.9 %shard_map.96 = (f32[16,392,128]{2,1,0:T(8,128)}, f32[64,8,128]{2,1,0:T(8,128)}) custom-call(s32[66]{0:T(128)} %pad_add_fusion.refs_0_, f32[8,8,1024]{2,1,0:T(8,128)} %copy-done, bf16[8,2,256,256]{3,2,1,0:T(8,128)(2,1)} %constant.19.clone.refs_2_), custom_call_target="tpu_custom_call" | custom-call | bytes 40000000 | tf_op jit(solution)/shard_map/pallas_call | solution.py:590
  30.0 6.8 %all-to-all-start.1 = ((f32[16,392,128]{2,1,0:T(8,128)}), f32[16,392,128]{2,1,0:T(8,128)}, u32[]{:S(2)}, u32[]{:S(2)}) async-start(f32[16,392,128]{2,1,0:T(8,128)} %get-tuple-element.16), calls=%async_computation.1 | async-start | bytes 6422528 | tf_op jit(solution)/shard_map/all_to_all | solution.py:561
  36.8 11.6 %shard_map.99 = f32[16,392,128]{2,1,0:T(8,128)} custom-call(s32[66]{0:T(128)} %pad_add_fusion.refs_0_, f32[8,8,1024]{2,1,0:T(8,128)} %copy-done, bf16[8,2,256,256]{3,2,1,0:T(8,128)(2,1)} %constant.19.clone.refs_2_, f32[64,8,128]{2,1,0:T(8,128)} %get-tuple-element.15.refs_2_.refs_3_), custom_call_target="tpu_custom_call" | custom-call | bytes 40000000 | tf_op jit(solution)/shard_map/pallas_call | solution.py:599
  48.4 35.2 %all-to-all-done.1.refs_1_ = f32[16,392,128]{2,1,0:T(8,128)} async-done(((f32[16,392,128]{2,1,0:T(8,128)}), f32[16,392,128]{2,1,0:T(8,128)}, u32[]{:S(2)}, u32[]{:S(2)}) %all-to-all-start.1) | async-done | bytes 3211296 | tf_op jit(solution)/shard_map/all_to_all | solution.py:561
  83.5 4.5 %all-to-all-start.3 = ((f32[16,392,128]{2,1,0:T(8,128)}), f32[16,392,128]{2,1,0:T(8,128)}, u32[]{:S(2)}, u32[]{:S(2)}) async-start(f32[16,392,128]{2,1,0:T(8,128)} %shard_map.99), calls=%async_computation.3 | async-start | bytes 6422528 | tf_op jit(solution)/shard_map/all_to_all | solution.py:561
  88.0 25.0 %shard_map.97 = (f32[2,3,2,64,1024]{4,3,2,1,0:T(8,128)}, f32[16,392,128]{2,1,0:T(8,128)}, f32[8,128]{1,0:T(8,128)}) custom-call(s32[66]{0:T(128)} %pad_add_fusion.refs_0_, f32[16,392,128]{2,1,0:T(8,128)} %all-to-all-done.1.refs_1_, bf16[8,2,256,256]{3,2,1,0:T(8,128)(2,1)} %constant.21.clone.refs_2_, bf16[8,2,256,256]{3,2,1,0:T(8,128)(2,1)} %constant.22.clone.refs_3_), custom_call_target="tpu_custom_call" | custom-call | bytes 40000000 | tf_op jit(solution)/shard_map/pallas_call | solution.py:606
  113.1 18.5 %all-to-all-done.3.refs_1_ = f32[16,392,128]{2,1,0:T(8,128)} async-done(((f32[16,392,128]{2,1,0:T(8,128)}), f32[16,392,128]{2,1,0:T(8,128)}, u32[]{:S(2)}, u32[]{:S(2)}) %all-to-all-start.3) | async-done | bytes 3211296 | tf_op jit(solution)/shard_map/all_to_all | solution.py:561
  131.6 5.1 %all-to-all-start.2 = ((f32[16,392,128]{2,1,0:T(8,128)}), f32[16,392,128]{2,1,0:T(8,128)}, u32[]{:S(2)}, u32[]{:S(2)}) async-start(f32[16,392,128]{2,1,0:T(8,128)} %get-tuple-element.17), calls=%async_computation.2 | async-start | bytes 6422528 | tf_op jit(solution)/shard_map/all_to_all | solution.py:561
  136.7 25.0 %shard_map.100 = (f32[2,3,2,64,1024]{4,3,2,1,0:T(8,128)}, f32[16,392,128]{2,1,0:T(8,128)}, f32[8,128]{1,0:T(8,128)}) custom-call(s32[66]{0:T(128)} %pad_add_fusion.refs_0_, f32[16,392,128]{2,1,0:T(8,128)} %all-to-all-done.3.refs_1_, bf16[8,2,256,256]{3,2,1,0:T(8,128)(2,1)} %constant.21.clone.refs_2_, bf16[8,2,256,256]{3,2,1,0:T(8,128)(2,1)} %constant.22.clone.refs_3_), custom_call_target="tpu_custom_call" | custom-call | bytes 40000000 | tf_op jit(solution)/shard_map/pallas_call | solution.py:606
  161.7 16.9 %all-to-all-done.2.refs_3_ = f32[16,392,128]{2,1,0:T(8,128)} async-done(((f32[16,392,128]{2,1,0:T(8,128)}), f32[16,392,128]{2,1,0:T(8,128)}, u32[]{:S(2)}, u32[]{:S(2)}) %all-to-all-start.2) | async-done | bytes 3211296 | tf_op jit(solution)/shard_map/all_to_all | solution.py:561
  178.6 6.2 %all-to-all-start.4 = ((f32[16,392,128]{2,1,0:T(8,128)}), f32[16,392,128]{2,1,0:T(8,128)}, u32[]{:S(2)}, u32[]{:S(2)}) async-start(f32[16,392,128]{2,1,0:T(8,128)} %get-tuple-element.18), calls=%async_computation.4 | async-start | bytes 6422528 | tf_op jit(solution)/shard_map/all_to_all | solution.py:561
  184.8 11.6 %shard_map.98.refs_3_ = f32[8,24,128]{2,1,0:T(8,128)} custom-call(s32[66]{0:T(128)} %pad_add_fusion.refs_0_, f32[8,8,1024]{2,1,0:T(8,128)} %copy-done, f32[64,8,128]{2,1,0:T(8,128)} %get-tuple-element.15.refs_2_.refs_3_, f32[16,392,128]{2,1,0:T(8,128)} %all-to-all-done.2.refs_3_, bf16[8,2,256,256]{3,2,1,0:T(8,128)(2,1)} %constant.20.clone.refs_4_.refs_5_), custom_call_target="tpu_custom_call" | custom-call | bytes 40000000 | tf_op jit(solution)/shard_map/pallas_call | solution.py:635
  196.4 32.0 %all-to-all-done.4.refs_4_ = f32[16,392,128]{2,1,0:T(8,128)} async-done(((f32[16,392,128]{2,1,0:T(8,128)}), f32[16,392,128]{2,1,0:T(8,128)}, u32[]{:S(2)}, u32[]{:S(2)}) %all-to-all-start.4) | async-done | bytes 3211296 | tf_op jit(solution)/shard_map/all_to_all | solution.py:561
  228.4 11.6 %shard_map.101 = f32[8,24,128]{2,1,0:T(8,128)} custom-call(s32[66]{0:T(128)} %pad_add_fusion.refs_0_, f32[8,8,1024]{2,1,0:T(8,128)} %copy-done, f32[64,8,128]{2,1,0:T(8,128)} %get-tuple-element.15.refs_2_.refs_3_, f32[8,24,128]{2,1,0:T(8,128)} %shard_map.98.refs_3_, f32[16,392,128]{2,1,0:T(8,128)} %all-to-all-done.4.refs_4_, ...), custom_call_target="tpu_custom_call" | custom-call | bytes 40000000 | tf_op jit(solution)/shard_map/pallas_call | solution.py:638
  240.0 12.3 %all_to_all.40.refs_1_ = f32[8,24,128]{2,1,0:T(8,128)} all-to-all(f32[8,24,128]{2,1,0:T(8,128)} %shard_map.101), channel_id=1, replica_groups=mesh['row'=16,'col'=8] {'col'}, dimensions={0} | all-to-all | bytes 196608 | tf_op jit(solution)/shard_map/all_to_all | solution.py:641
  252.3 1.6 shard_map.102
  253.9 9.9 %all_to_all.41 = f32[16,8,128]{2,1,0:T(8,128)S(1)} all-to-all(f32[16,8,128]{2,1,0:T(8,128)} %get-tuple-element.21), channel_id=1, replica_groups=mesh['row'=16,'col'=8] {'row'}, dimensions={0} | all-to-all | bytes 131072 | tf_op jit(solution)/shard_map/all_to_all | solution.py:645
  263.9 10.0 %all_to_all.42.refs_0_ = f32[8,8,128]{2,1,0:T(8,128)} all-to-all(f32[8,8,128]{2,1,0:T(8,128)S(1)} %broadcast_in_dim.2), channel_id=1, replica_groups=mesh['row'=16,'col'=8] {'col'}, dimensions={0} | all-to-all | bytes 65536 | tf_op jit(solution)/shard_map/all_to_all | solution.py:557
  273.9 6.9 %shard_map.103 = (f32[2,3,4,64,1024]{4,3,2,1,0:T(8,128)}, f32[3,1024]{1,0:T(4,128)}) custom-call(f32[8,8,128]{2,1,0:T(8,128)} %all_to_all.42.refs_0_, f32[3,1024]{1,0:T(4,128)} %get-tuple-element.22.refs_1_, f32[3,1024]{1,0:T(4,128)} %get-tuple-element.23.refs_2_, f32[2,3,2,64,1024]{4,3,2,1,0:T(8,128)} %get-tuple-element.24.refs_3_, ...), custom_call_target="tpu_custom_call" | custom-call | bytes 13000000 | tf_op jit(solution)/shard_map/pallas_call | solution.py:648
  (3 shorter events, 0.0 us)
Async XLA Ops:
  2.2 13.3 %all-to-all-start = ((f32[8,8,1024]{2,1,0:T(8,128)}), f32[8,8,1024]{2,1,0:T(8,128)S(1)}, u32[]{:S(2)}, u32[]{:S(2)}) async-start(f32[8,8,1024]{2,1,0:T(8,128)} %get-tuple-element.14), calls=%async_computation | async-start | bytes 524288 | tf_op jit(solution)/shard_map/all_to_all | solution.py:570
  15.5 0.7 copy-start
  30.0 53.5 %all-to-all-start.1 = ((f32[16,392,128]{2,1,0:T(8,128)}), f32[16,392,128]{2,1,0:T(8,128)}, u32[]{:S(2)}, u32[]{:S(2)}) async-start(f32[16,392,128]{2,1,0:T(8,128)} %get-tuple-element.16), calls=%async_computation.1 | async-start | bytes 6422528 | tf_op jit(solution)/shard_map/all_to_all | solution.py:561
  83.5 48.1 %all-to-all-start.3 = ((f32[16,392,128]{2,1,0:T(8,128)}), f32[16,392,128]{2,1,0:T(8,128)}, u32[]{:S(2)}, u32[]{:S(2)}) async-start(f32[16,392,128]{2,1,0:T(8,128)} %shard_map.99), calls=%async_computation.3 | async-start | bytes 6422528 | tf_op jit(solution)/shard_map/all_to_all | solution.py:561
  131.6 47.0 %all-to-all-start.2 = ((f32[16,392,128]{2,1,0:T(8,128)}), f32[16,392,128]{2,1,0:T(8,128)}, u32[]{:S(2)}, u32[]{:S(2)}) async-start(f32[16,392,128]{2,1,0:T(8,128)} %get-tuple-element.17), calls=%async_computation.2 | async-start | bytes 6422528 | tf_op jit(solution)/shard_map/all_to_all | solution.py:561
  178.6 49.7 %all-to-all-start.4 = ((f32[16,392,128]{2,1,0:T(8,128)}), f32[16,392,128]{2,1,0:T(8,128)}, u32[]{:S(2)}, u32[]{:S(2)}) async-start(f32[16,392,128]{2,1,0:T(8,128)} %get-tuple-element.18), calls=%async_computation.4 | async-start | bytes 6422528 | tf_op jit(solution)/shard_map/all_to_all | solution.py:561

commit v4 on v3

v4 whole, which is shorter than its diff:
```python
import functools
import math

import jax
import jax.numpy as jnp
import ml_dtypes
import numpy as np
from jax import lax
from jax.experimental import pallas as pl
from jax.experimental.pallas import tpu as pltpu
from jax.sharding import PartitionSpec as P

NX = 1024
NY = 1024
NZ = 64
CELLS = float(NX * NY * NZ)
TWO_PI = 2.0 * math.pi
F32 = jnp.float32
BF16 = jnp.bfloat16
VMEM_LIMIT = 64 * 1024 * 1024
VMEM = pl.BlockSpec(memory_space=pltpu.VMEM)
SMEM = pl.BlockSpec(memory_space=pltpu.SMEM)
ANY = pl.BlockSpec(memory_space=pl.ANY)
TABLE = pltpu.VMEM((8, 2, 256, 256), BF16)
BLOCKS = pltpu.VMEM((16, 784, 128), F32)


def halves(table):
    table = table.astype(np.float32)
    high = table.astype(ml_dtypes.bfloat16)
    low = (table - high.astype(np.float32)).astype(ml_dtypes.bfloat16)
    return np.stack([high, low], 1)


def table_y():
    first = np.arange(8)[:, None, None]
    angle = TWO_PI * ((np.arange(128)[None, :, None] * 8 + first) * np.arange(128)[None, None, :] % 1024) / 1024
    cosine, sine = np.cos(angle), np.sin(angle)
    return np.concatenate([np.concatenate([cosine, sine], 2), np.concatenate([-sine, cosine], 2)], 1)


def table_x():
    result = np.zeros((8, 2, 2, 64, 2, 64, 2))
    inner = np.arange(64)
    for first in range(8):
        for upper in range(2):
            wave = 16 * np.arange(64) + first + 8 * upper
            angle = TWO_PI * (inner[:, None] * wave[None, :] % 1024) / 1024
            result[first, upper, 0, :, 0, :, upper] = np.cos(angle)
            result[first, upper, 1, :, 0, :, upper] = np.sin(angle)
            result[first, upper, 0, :, 1, :, upper] = -np.sin(angle)
            result[first, upper, 1, :, 1, :, upper] = np.cos(angle)
    return result.reshape(8, 256, 256)


def table_edge():
    place = np.arange(128)
    result = np.zeros((8, 128, 2, 128))
    for first in range(8):
        for source in range(16):
            angle = TWO_PI * ((source + 1) * (first + 8 * (place % 2)) % 16) / 16
            result[first, 2 * source, 0] = np.cos(angle)
            result[first, 2 * source, 1] = -np.sin(angle)
            result[first, 2 * source + 1, 0] = np.sin(angle)
            result[first, 2 * source + 1, 1] = np.cos(angle)
    return result.reshape(8, 128, 256)


def stacked(table):
    high, low = table[:, 0, :32], table[:, 1, :32]
    return np.concatenate([high, high, low, np.zeros_like(low)], 1)


def split(value):
    high = value.astype(BF16)
    return high, (value - high.astype(F32)).astype(BF16)


def mul(left, right):
    return jnp.dot(left, right, preferred_element_type=F32)


def mul_t(left, right):
    return lax.dot_general(left, right, (((1,), (1,)), ((), ())), preferred_element_type=F32)


def doubled(high, low):
    return jnp.concatenate(
        [jnp.concatenate([high, high], 1), jnp.concatenate([low, jnp.zeros_like(low)], 1)], 0
    )


def small_dft(values, sign):
    count = len(values)
    if count == 1:
        return values
    even = small_dft(values[0::2], sign)
    odd = small_dft(values[1::2], sign)
    low, high = [], []
    for k in range(count // 2):
        real, imag = odd[k]
        if k > 0:
            if 4 * k == count:
                real, imag = (-imag, real) if sign > 0 else (imag, -real)
            elif 8 * k == count:
                root = math.sqrt(0.5)
                if sign > 0:
                    real, imag = (real - imag) * root, (real + imag) * root
                else:
                    real, imag = (real + imag) * root, (imag - real) * root
            elif 8 * k == 3 * count:
                root = math.sqrt(0.5)
                if sign > 0:
                    real, imag = (real + imag) * -root, (real - imag) * root
                else:
                    real, imag = (imag - real) * root, (real + imag) * -root
            else:
                cosine = math.cos(TWO_PI * k / count)
                sine = sign * math.sin(TWO_PI * k / count)
                real, imag = real * cosine - imag * sine, real * sine + imag * cosine
        low.append((even[k][0] + real, even[k][1] + imag))
        high.append((even[k][0] - real, even[k][1] - imag))
    return low + high


def hat(distance):
    return jnp.maximum(1.0 - jnp.abs(distance), 0.0)


def ramp(shape, axis):
    return lax.broadcasted_iota(jnp.int32, shape, axis).astype(F32)


def brick_place(brick):
    return brick // 64, brick // 2 % 32, brick % 2


def block_points(points, block):
    lane = pl.multiple_of(block % 8 * 128, 128)
    return points[block // 8, :, pl.ds(lane, 128)]


def depth_waves(meta, block, point):
    index = lax.broadcasted_iota(jnp.int32, (8, 128), 0)
    mode = 4 * meta[65] + 2 * (index // 4) + index % 2
    turn = 16 * (index // 2 % 2)

    def wave(cell):
        angle = (mode * cell + turn) & 63
        value = (jnp.abs(angle - 32) - 16).astype(F32) * (math.pi / 32.0)
        square = value * value
        total = -1.0 / 39916800.0
        for factor in (1.0 / 362880.0, -1.0 / 5040.0, 1.0 / 120.0, -1.0 / 6.0, 1.0):
            total = total * square + factor
        return total * value

    lower = jnp.floor(point[2:3])
    part = point[2:3] - lower
    cell = lower.astype(jnp.int32) + 32 * (meta[block] % 2)
    return (1.0 - part) * wave(cell) + part * wave(cell + 1)


def edge_weights(along):
    return jnp.concatenate([along[:40], jnp.zeros((88, 128), F32)], 0)


def edge_waves(point, waves, place_x):
    return waves * jnp.maximum(point[0:1] - (63 - 32 * place_x).astype(F32), 0.0)


def lower_lanes(rows):
    return lax.broadcasted_iota(jnp.int32, (rows, 128), 1) < 64


def joined(first, second):
    lower = lower_lanes(first.shape[0])
    return (
        jnp.where(lower, first, pltpu.roll(second, 64, 1)),
        jnp.where(lower, pltpu.roll(first, 64, 1), second),
    )


def pack_kernel(offsets, measured, bricks, counts, out, residual):
    lane = lax.broadcasted_iota(jnp.int32, (3, 128), 1)
    for i in range(8):
        at = slice(128 * i, 128 * i + 128)
        residual[:, at] = jnp.where(lane < counts[i], measured[:, at], 0.0)
        brick = jnp.zeros((2, 128), F32) + bricks[i].astype(F32)
        block = jnp.concatenate([offsets[:, at], residual[:, at], brick], 0)
        for dest in range(8):
            out[dest, :, at] = block


def slab_weights(point, waves, place_x):
    across = hat(ramp((64, 128), 0) - (32 * place_x).astype(F32) - point[0:1])
    return jnp.concatenate([waves[i : i + 1] * across for i in range(8)], 0)


def spread_kernel(
    meta, points, far_table, far_out, depth, field, parts, windows, table, out, table_done, out_done
):
    def table_copy(k):
        return pltpu.make_async_copy(far_table.at[k], table.at[k], table_done.at[k])

    def out_copy(k):
        at = pl.ds(2 * k, 2)
        return pltpu.make_async_copy(out.at[at], far_out.at[at], out_done.at[k])

    for k in range(8):
        table_copy(k).start()
    field[...] = jnp.zeros_like(field)
    windows[...] = jnp.zeros_like(windows)

    def step(block, carry):
        place_x, place_y, _ = brick_place(meta[block])
        point = block_points(points, block)
        waves = depth_waves(meta, block, point)
        depth[block] = waves
        weight_high, weight_low = split(slab_weights(point, waves, place_x))
        along = hat(ramp((40, 128), 0) - point[1:2])
        source = jnp.concatenate([along * point[3 + c : 4 + c] for c in range(3)], 0)
        both = mul_t(doubled(*split(source)), jnp.concatenate([weight_high, weight_low], 1))
        value = both[:120] + both[120:]
        row = pl.multiple_of(place_y * 32, 32)
        for c in range(3):
            field[c, pl.ds(row, 40), :] += value[40 * c : 40 * c + 40]
        waves = edge_waves(point, waves, place_x)
        source = jnp.concatenate([waves[i : i + 1] * point[3:6] for i in range(8)], 0)
        both = mul_t(doubled(*split(source)), jnp.concatenate(split(edge_weights(along)), 1))
        lane = pl.multiple_of(place_y // 4 * 128, 128)
        windows[place_y % 4, :, pl.ds(lane, 128)] += both[:24] + both[24:]
        return carry

    lax.fori_loop(0, 64, step, 0, unroll=32)
    for c in range(3):
        field[c, 0:1, :] += field[c, 1024:1025, :]

    def outer(tile, carry):
        row = pl.multiple_of(tile * 8, 8)
        for c in range(3):
            for p in range(2):
                lane = 256 * p
                values = [
                    (
                        field[c, pl.ds(128 * a + row, 8), lane : lane + 128],
                        field[c, pl.ds(128 * a + row, 8), lane + 128 : lane + 256],
                    )
                    for a in range(8)
                ]
                to = 128 * (3 * p + c)
                for k, (real, imag) in enumerate(small_dft(values, -1)):
                    parts[k, pl.ds(row, 8), to : to + 128] = real
                    parts[k, pl.ds(128 + row, 8), to : to + 128] = imag
        return carry

    lax.fori_loop(0, 16, outer, 0, unroll=4)
    total = windows[0]
    for j in range(1, 4):
        total = total + pltpu.roll(windows[j], 32 * j, 1)
    real = jnp.concatenate([total[0:6], total[12:18]], 0)
    imag = jnp.concatenate([total[6:12], total[18:24]], 0)
    values = [(real[:, 128 * a : 128 * a + 128], imag[:, 128 * a : 128 * a + 128]) for a in range(8)]
    for k, pieces in enumerate(small_dft(values, -1)):
        windows[k // 2, 0:12, 256 * (k % 2) : 256 * (k % 2) + 256] = jnp.concatenate(pieces, 1)

    def inner(k, carry):
        table_copy(k).wait()
        high, low = split(parts[k])
        value = mul(table[k, 0], high) + mul(table[k, 1], high) + mul(table[k, 0], low)
        high, low = split(windows[k // 2, 0:12, pl.ds(pl.multiple_of(256 * (k % 2), 256), 256)])
        edge = mul_t(high, table[k, 0]) + mul_t(high, table[k, 1]) + mul_t(low, table[k, 0])
        for p in range(2):
            rows = edge[6 * p : 6 * p + 6]
            sides = [joined(rows[0:3, at : at + 128], rows[3:6, at : at + 128]) for at in (0, 128)]
            for half in range(2):
                for c in range(3):
                    for part in range(2):
                        row = 128 * part + 64 * half
                        to = 392 * p + 64 * (2 * c + part)
                        at = 128 * (3 * p + c)
                        out[2 * k + half, to : to + 64] = value[row : row + 64, at : at + 128]
                out[2 * k + half, 392 * p + 384 : 392 * p + 392] = jnp.concatenate(
                    [sides[part][half][c : c + 1] for c in range(3) for part in range(2)]
                    + [jnp.zeros((2, 128), F32)],
                    0,
                )
        out_copy(k).start()
        return carry

    lax.fori_loop(0, 8, inner, 0)
    for k in range(8):
        out_copy(k).wait()


def spectrum_kernel(
    meta, far_received, far_table, far_back, edge_table, edge_stack, far_spectrum, far_out, norm,
    received, out, spectrum, parts, back, edge_sum, table, table_back,
    received_done, out_done, spectrum_done, table_done, back_done,
):
    row = meta[64]

    def place(p, c):
        return pl.ds(392 * p + 128 * c, 128 if c < 3 else 8)

    def received_copy(p, c):
        at = place(p, c)
        return pltpu.make_async_copy(far_received.at[:, at], received.at[:, at], received_done.at[4 * p + c])

    def out_copy(p, c):
        at = place(p, c)
        return pltpu.make_async_copy(out.at[:, at], far_out.at[:, at], out_done.at[4 * p + c])

    def spectrum_copy(p, part):
        to = far_spectrum.at[part, :, pl.ds(2 * p, 2)]
        return pltpu.make_async_copy(spectrum.at[p, part], to, spectrum_done.at[2 * p + part])

    def table_copy(k):
        return pltpu.make_async_copy(far_table.at[k], table.at[k], table_done.at[k])

    def back_copy(k):
        return pltpu.make_async_copy(far_back.at[k], table_back.at[k], back_done.at[k])

    for c in (3, 0, 1, 2):
        received_copy(0, c).start()
    for k in range(8):
        table_copy(k).start()
        back_copy(k).start()
    for c in (3, 0, 1, 2):
        received_copy(1, c).start()

    index_y = 8 * (64 * (row % 2) + lax.broadcasted_iota(jnp.int32, (64, 128), 0)) + row // 2
    lane_x = lax.broadcasted_iota(jnp.int32, (64, 128), 1)
    wave_y = jnp.where(index_y < NY // 2, index_y, index_y - NY).astype(F32) * (TWO_PI / NY)
    sums = jnp.zeros((64, 128), F32)
    for p in range(2):
        base = 392 * p

        def outer(c, tile, carry):
            at = pl.multiple_of(tile * 8, 8)
            first = base + 128 * c
            values = [
                (received[s, pl.ds(first + at, 8)], received[s, pl.ds(first + 64 + at, 8)]) for s in range(16)
            ]
            for k, (real, imag) in enumerate(small_dft(values, -1)):
                to = 128 * (k // 8)
                first, second = joined(real, imag)
                parts[k % 8, pl.ds(128 * c + at, 8), to : to + 128] = first
                parts[k % 8, pl.ds(128 * c + 64 + at, 8), to : to + 128] = second
            return carry

        for c in range(3):
            received_copy(p, c).wait()
            lax.fori_loop(0, 8, functools.partial(outer, c), 0, unroll=8)
        received_copy(p, 3).wait()
        columns = []
        for c in range(3):
            at = base + 384 + 2 * c
            rows = jnp.concatenate([received[s, at : at + 2] for s in range(16)], 0)
            high = rows.astype(BF16).astype(F32)
            columns.append(jnp.concatenate([high, rows - high, high, jnp.zeros((32, 128), F32)], 0).T.astype(BF16))
        edge = jnp.concatenate(columns, 0)
        edge_sum[...] = jnp.zeros_like(edge_sum)

        def inner(k, total):
            if p == 0:
                table_copy(k).wait()
                back_copy(k).wait()
            high, low = split(parts[k])
            value = mul(high, table[k, 0]) + mul(low, table[k, 0]) + mul(high, table[k, 1])
            value = value + mul(edge, edge_stack[k])
            index_x = 8 * lane_x + k
            wave_x = jnp.where(index_x < NX // 2, index_x, index_x - NX).astype(F32) * (TWO_PI / NX)
            flat = wave_x * wave_x + wave_y * wave_y
            valid = (index_y != NY // 2) & (index_x != NX // 2)
            to = pl.multiple_of(k * 128, 128)
            rows = [[None, None] for _ in range(3)]
            for h in range(2):
                index_z = 4 * meta[65] + 2 * p + h
                wave_z = index_z.astype(F32) * (TWO_PI / NZ)
                weight = jnp.where(index_z == 0, 1.0, 2.0).astype(F32) / CELLS
                squared = flat + wave_z * wave_z
                keep = valid & (squared > 0.0)
                inverse = jnp.where(keep, 1.0 / jnp.where(keep, squared, 1.0), 0.0)

                def crossed(vector, scale):
                    return [
                        (wave_y * vector[2] - wave_z * vector[1]) * scale,
                        (wave_z * vector[0] - wave_x * vector[2]) * scale,
                        (wave_x * vector[1] - wave_y * vector[0]) * scale,
                    ]

                start = [128 * c + 64 * h for c in range(3)]
                real = [value[s : s + 64, 0:128] for s in start]
                imag = [value[s : s + 64, 128:256] for s in start]
                grad_real = crossed(imag, -inverse)
                grad_imag = crossed(real, inverse)
                square = 0.0
                for c in range(3):
                    spectrum[p, 0, c, h, :, pl.ds(to, 128)] = grad_real[c]
                    spectrum[p, 1, c, h, :, pl.ds(to, 128)] = grad_imag[c]
                    square = square + grad_real[c] * grad_real[c] + grad_imag[c] * grad_imag[c]
                total = total + weight * square
                scale = inverse * weight
                back_real = crossed(grad_imag, -scale)
                back_imag = crossed(grad_real, scale)
                for c in range(3):
                    rows[c][h] = jnp.concatenate([back_real[c], back_imag[c]], 1)
            high, low = split(jnp.concatenate([rows[c][h] for c in range(3) for h in range(2)], 0))
            back[k] = mul(high, table_back[k, 0]) + mul(low, table_back[k, 0]) + mul(high, table_back[k, 1])
            edge_sum[...] += (
                mul_t(high, edge_table[k, 0]) + mul_t(high, edge_table[k, 1]) + mul_t(low, edge_table[k, 0])
            )
            return total

        sums = lax.fori_loop(0, 8, inner, sums, unroll=8)
        for part in range(2):
            spectrum_copy(p, part).start()

        def last(c, tile, carry):
            at = pl.multiple_of(tile * 8, 8)
            values = []
            for k in range(16):
                to = 128 * (k // 8)
                first = back[k % 8, pl.ds(128 * c + at, 8), to : to + 128]
                second = back[k % 8, pl.ds(128 * c + 64 + at, 8), to : to + 128]
                values.append(joined(first, second))
            for s, pieces in enumerate(small_dft(values, 1)):
                for part in range(2):
                    out[s, pl.ds(base + 128 * c + 64 * part + at, 8)] = pieces[part]
            return carry

        turned = [edge_sum[128 * c : 128 * c + 128, :].T for c in range(3)]
        for s in range(16):
            out[s, base + 384 : base + 392] = jnp.concatenate(
                [turned[c][2 * s : 2 * s + 2] for c in range(3)] + [jnp.zeros((2, 128), F32)], 0
            )
        out_copy(p, 3).start()
        for c in range(3):
            lax.fori_loop(0, 8, functools.partial(last, c), 0, unroll=8)
            out_copy(p, c).start()
    norm[...] = jnp.sum(sums.reshape(8, 8, 128), axis=0)
    for p in range(2):
        for part in range(2):
            spectrum_copy(p, part).wait()
        for c in range(4):
            out_copy(p, c).wait()


def gather_kernel(
    meta, points, depth, far_received, far_table, out,
    field_high, field_low, parts, edge, windows, table, received, table_done, received_done,
):
    def table_copy(k):
        return pltpu.make_async_copy(far_table.at[k], table.at[k], table_done.at[k])

    def received_copy(k):
        at = pl.ds(2 * k, 2)
        return pltpu.make_async_copy(far_received.at[at], received.at[at], received_done.at[k])

    for k in range(8):
        table_copy(k).start()
        received_copy(k).start()

    def inner(k, carry):
        table_copy(k).wait()
        received_copy(k).wait()
        columns = []
        for p in range(2):
            for c in range(3):
                pieces = []
                for part in range(2):
                    for half in range(2):
                        at = 392 * p + 64 * (2 * c + part)
                        pieces.append(received[2 * k + half, at : at + 64])
                columns.append(jnp.concatenate(pieces, 0))
        high, low = split(jnp.concatenate(columns, 1))
        parts[k] = mul(table[k, 0], high) + mul(table[k, 1], high) + mul(table[k, 0], low)
        sides = []
        for p in range(2):
            at = 392 * p + 384
            sides.append(joined(received[2 * k, at : at + 8], received[2 * k + 1, at : at + 8]))
        rows = [
            jnp.concatenate(
                [sides[p][h][2 * c + part : 2 * c + part + 1] for p in range(2) for h in range(2) for c in range(3)],
                0,
            )
            for part in range(2)
        ]
        high, low = split(jnp.concatenate(rows, 1))
        edge[k] = mul_t(high, table[k, 0]) + mul_t(high, table[k, 1]) + mul_t(low, table[k, 0])
        return carry

    lax.fori_loop(0, 8, inner, 0)
    values = [(edge[k, :, 0:128], edge[k, :, 128:256]) for k in range(8)]
    planes = []
    for real, imag in small_dft(values, 1):
        planes.append(jnp.concatenate([real[0:6], imag[0:6], real[6:12], imag[6:12]], 0))
    plane = jnp.concatenate(planes, 1)
    for j in range(4):
        windows[j] = plane if j == 0 else pltpu.roll(plane, 1024 - 32 * j, 1)

    def outer(tile, carry):
        row = pl.multiple_of(tile * 16, 16)
        for c in range(3):
            for p in range(2):
                at = 128 * (3 * p + c)
                values = [
                    (parts[k, pl.ds(row, 16), at : at + 128], parts[k, pl.ds(128 + row, 16), at : at + 128])
                    for k in range(8)
                ]
                for a, pieces in enumerate(small_dft(values, 1)):
                    for part in range(2):
                        high, low = split(pieces[part])
                        lane = 256 * p + 128 * part
                        field_high[c, pl.ds(128 * a + row, 16), lane : lane + 128] = high
                        field_low[c, pl.ds(128 * a + row, 16), lane : lane + 128] = low
        return carry

    lax.fori_loop(0, 8, outer, 0)
    for c in range(3):
        field_high[c, 1024:1040, :] = field_high[c, 0:16, :]
        field_low[c, 1024:1040, :] = field_low[c, 0:16, :]

    def step(block, carry):
        place_x, place_y, _ = brick_place(meta[block])
        point = block_points(points, block)
        waves = depth[block]
        weight_high, weight_low = split(slab_weights(point, waves, place_x))
        along = hat(ramp((48, 128), 0) - point[1:2])
        row = pl.multiple_of(place_y * 32, 32)
        high = jnp.concatenate([field_high[c, pl.ds(row, 48), :] for c in range(3)], 0)
        low = jnp.concatenate([field_low[c, pl.ds(row, 48), :] for c in range(3)], 0)
        both = mul(high, jnp.concatenate([weight_high, weight_low], 1))
        value = both[:, :128] + both[:, 128:] + mul(low, weight_high)
        velocity = [jnp.sum(along * value[48 * c : 48 * c + 48], axis=0, keepdims=True) for c in range(3)]
        waves = edge_waves(point, waves, place_x)
        weight_high, weight_low = split(edge_weights(along))
        lane = pl.multiple_of(place_y // 4 * 128, 128)
        high, low = split(windows[place_y % 4, :, pl.ds(lane, 128)])
        value = mul(high, weight_high) + mul(low, weight_high) + mul(high, weight_low)
        more = sum(waves[i : i + 1] * value[3 * i : 3 * i + 3] for i in range(8))
        for c in range(3):
            out[block // 8, pl.ds(8 * c + block % 8, 1), :] = velocity[c] + more[c : c + 1]
        return carry

    lax.fori_loop(0, 64, step, 0, unroll=32)


def sums_kernel(counts, received, norms, velocity, out):
    row = lax.broadcasted_iota(jnp.int32, (8, 128), 0)
    count = jnp.zeros((8, 128), jnp.int32)
    for i in range(8):
        count = jnp.where(row == i, counts[i], count)
    live = lax.broadcasted_iota(jnp.int32, (8, 128), 1) < count
    square = jnp.zeros((8, 128), F32)
    for c in range(3):
        total = received[0, 8 * c : 8 * c + 8]
        for source in range(1, 8):
            total = total + received[source, 8 * c : 8 * c + 8]
        total = jnp.where(live, total, 0.0)
        square = square + total * total
        for i in range(8):
            velocity[c : c + 1, 128 * i : 128 * i + 128] = total[i : i + 1]
    norm = jnp.sum(norms[...], axis=0, keepdims=True)
    square = jnp.sum(square, axis=0, keepdims=True)
    tile = jnp.where(row == 0, norm, jnp.where(row == 1, square, 0.0))
    for dest in range(16):
        out[dest] = tile


def final_kernel(sums, residual, velocity, gradient, spectrum, out, values, loaded, stored):
    def load(i):
        source = gradient.at[i // 6, i // 2 % 3, pl.ds(i % 2 * 2, 2)]
        return pltpu.make_async_copy(source, values.at[i], loaded.at[i])

    def store(i):
        place = spectrum.at[i // 6, i // 2 % 3, pl.ds(i % 2 * 2, 2)]
        return pltpu.make_async_copy(values.at[i], place, stored.at[i])

    for i in range(12):
        load(i).start()
    total = jnp.sum(jnp.sum(sums[...], axis=0), axis=1, keepdims=True)
    length = total[0:1] / total[1:2]
    scale = length * (1.0 / math.sqrt(CELLS))
    for i in range(12):
        load(i).wait()
        values[i] = values[i] * scale
        store(i).start()
    out[...] = residual[...] - length * velocity[...]
    for i in range(12):
        store(i).wait()


def call(kernel, outs, specs, scratch=(), traffic=0, out_specs=VMEM):
    return pl.pallas_call(
        kernel,
        out_shape=outs,
        in_specs=specs,
        out_specs=out_specs,
        scratch_shapes=list(scratch),
        cost_estimate=pl.CostEstimate(flops=0, bytes_accessed=int(traffic), transcendentals=0),
        compiler_params=pltpu.CompilerParams(vmem_limit_bytes=VMEM_LIMIT),
    )


def near(value):
    return pltpu.with_memory_space_constraint(value, pltpu.VMEM)


def far(value):
    return pltpu.with_memory_space_constraint(value, pltpu.HBM)


def near_shape(*dims):
    return pltpu.VMEM(dims, F32)


def shape(*dims):
    return jax.ShapeDtypeStruct(dims, F32)


def spread_out(value, axis):
    count = lax.axis_size(axis)
    return lax.all_to_all(jnp.broadcast_to(value[None], (count,) + value.shape), axis, 0, 0, tiled=True)


def exchange(value):
    return lax.all_to_all(value, "row", 0, 0, tiled=True)


def body(offsets, measured, block_brick, block_count):
    row = lax.axis_index("row")
    col = lax.axis_index("col")
    packed, residual = call(
        pack_kernel, (shape(8, 8, 1024), shape(3, 1024)), [VMEM, VMEM, SMEM, SMEM], traffic=1e6, out_specs=(VMEM, VMEM)
    )(offsets, measured, block_brick, block_count)
    points = lax.all_to_all(packed, "col", 0, 0, tiled=True)
    bricks = points[:, 6, ::128].reshape(64).astype(jnp.int32)
    meta = jnp.concatenate([bricks, jnp.stack([row, col]).astype(jnp.int32)])
    y_table = table_y()
    x_table = table_x()
    forward_y = jnp.asarray(halves(y_table))
    inverse_y = jnp.asarray(halves(y_table.transpose(0, 2, 1)))
    forward_x = jnp.asarray(halves(x_table))
    inverse_x = jnp.asarray(halves(x_table.transpose(0, 2, 1)))

    edge_table = halves(table_edge())
    eight = pltpu.SemaphoreType.DMA((8,))
    sent, depth = call(
        spread_kernel,
        (shape(16, 784, 128), shape(64, 8, 128)),
        [SMEM, VMEM, ANY],
        [
            pltpu.VMEM((3, 1032, 512), F32),
            pltpu.VMEM((8, 256, 768), F32),
            pltpu.VMEM((4, 24, 1024), F32),
            TABLE,
            BLOCKS,
            eight,
            eight,
        ],
        40e6,
        (ANY, VMEM),
    )(meta, points, forward_y)
    received = exchange(sent)
    spectrum, sent, norm = call(
        spectrum_kernel,
        (shape(2, 3, 4, 64, 1024), shape(16, 784, 128), shape(8, 128)),
        [SMEM, ANY, ANY, ANY, VMEM, VMEM],
        [
            BLOCKS,
            BLOCKS,
            pltpu.VMEM((2, 2, 3, 2, 64, 1024), F32),
            pltpu.VMEM((8, 384, 256), F32),
            pltpu.VMEM((8, 384, 256), F32),
            pltpu.VMEM((384, 128), F32),
            TABLE,
            TABLE,
            eight,
            eight,
            pltpu.SemaphoreType.DMA((4,)),
            eight,
            eight,
        ],
        40e6,
        (ANY, ANY, VMEM),
    )(meta, received, forward_x, inverse_x, jnp.asarray(edge_table), jnp.asarray(stacked(edge_table)))
    received = exchange(sent)
    velocity = call(
        gather_kernel,
        shape(8, 24, 128),
        [SMEM, VMEM, VMEM, ANY, ANY],
        [
            pltpu.VMEM((3, 1040, 512), BF16),
            pltpu.VMEM((3, 1040, 512), BF16),
            pltpu.VMEM((8, 256, 768), F32),
            pltpu.VMEM((8, 12, 256), F32),
            pltpu.VMEM((4, 24, 1024), F32),
            TABLE,
            BLOCKS,
            eight,
            eight,
        ],
        40e6,
    )(meta, points, depth, received, inverse_y)
    velocity = lax.all_to_all(velocity, "col", 0, 0, tiled=True)
    velocity, sums = call(sums_kernel, (shape(3, 1024), shape(16, 8, 128)), [SMEM] + [VMEM] * 2, traffic=1e6, out_specs=(VMEM, VMEM))(
        block_count, velocity, norm
    )
    sums = lax.all_to_all(sums, "row", 0, 0, tiled=True)
    sums = spread_out(jnp.sum(sums, axis=0), "col")
    twelve = pltpu.SemaphoreType.DMA((12,))
    return call(
        final_kernel,
        (shape(2, 3, 4, 64, 1024), shape(3, 1024)),
        [VMEM, VMEM, VMEM, ANY],
        [pltpu.VMEM((12, 2, 64, 1024), F32), twelve, twelve],
        13e6,
        (ANY, VMEM),
    )(sums, residual, velocity, spectrum)


def solution(mesh):
    in_specs = (
        P(None, ("row", "col")),
        P(None, ("row", "col")),
        P(("row", "col")),
        P(("row", "col")),
    )
    out_specs = (P(None, None, "col", "row", None), P(None, ("row", "col")))
    return jax.shard_map(body, mesh=mesh, in_specs=in_specs, out_specs=out_specs, check_vma=False)
```

time: 282 us -> 274 us (0.972)
  blocking collectives: 32.2 us -> 191 us
  waiting for transfers between devices: 109 us -> 6.5 us
  Pallas kernels: 108 us -> 67 us
  starting transfers between devices: 29.4 us -> 6.81 us
    all_to_all x0 -> x2, blocking collectives: none -> 158 us  [exchange(): return lax.all_to_all(value, 'row', 0, 0, tiled=True)]
    all_to_all x4 -> x0, waiting for transfers between devices: 103 us -> none  [exchange(): return lax.all_to_all(value, 'row', 0, 0, tiled=True)]
    pallas_call x6 -> x3, Pallas kernels: 97.7 us -> 57 us  [the longest x1 24 us: body(): call(spectrum_kernel, (shape(2, 3, 4, 64, 1024), shape(16, 784, 128), sha...]
    all_to_all x4 -> x0, starting transfers between devices: 22.6 us -> none  [exchange(): return lax.all_to_all(value, 'row', 0, 0, tiled=True)]
  transfers between devices with their start and end apart: 5 -> 1, of which waited for: 5 -> 1; matrix products, arithmetic and copies ran while one was open for 0% -> 0% of each run, Pallas kernels for 26% -> 0%
where the time goes in v4:
time: 274 us
  blocking collectives  191 us (70%)
  Pallas kernels  67 us (24%)
  starting transfers between devices  6.81 us (2%)
  waiting for transfers between devices  6.5 us (2%)
    all_to_all x2, blocking collectives, exchange(): return lax.all_to_all(value, 'row', 0, 0, tiled=True)  158 us
    pallas_call x1, Pallas kernels, body(): call(spectrum_kernel, (shape(2, 3, 4, 64, 1024), shape(16, 784, 128), sha...  24 us
    pallas_call x1, Pallas kernels, body(): call(spread_kernel, (shape(16, 784, 128), shape(64, 8, 128)), [SMEM, VMEM...  16.9 us
    pallas_call x1, Pallas kernels, body(): call(gather_kernel, shape(8, 24, 128), [SMEM, VMEM, VMEM, ANY, ANY], [plt...  16.1 us
    all_to_all x1, blocking collectives, body(): velocity = lax.all_to_all(velocity, 'col', 0, 0, tiled=True)  12.4 us
    all_to_all x1, blocking collectives, body(): sums = lax.all_to_all(sums, 'row', 0, 0, tiled=True)  10.2 us
    all_to_all x1, blocking collectives, spread_out(): lax.all_to_all(jnp.broadcast_to(value[None], (count,) + value.shape), axi...  10 us
    pallas_call x1, Pallas kernels, body(): call(final_kernel, (shape(2, 3, 4, 64, 1024), shape(3, 1024)), [VMEM, VME...  6.88 us
  transfers between devices with their start and end apart: 1, of which 1 were waited for; matrix products, arithmetic and copies ran while one was open for 0% of the time, Pallas kernels for 0%

profile of v4, /device:TPU:1, one launch (start us, length us, event | category | flops | bytes accessed | tf_op | source)
XLA Modules:
  0.0 273.6 jit_solution(2237498177300038845)
XLA Ops:
  0.6 1.5 shard_map.113
  2.2 6.8 %all-to-all-start = ((f32[8,8,1024]{2,1,0:T(8,128)}), f32[8,8,1024]{2,1,0:T(8,128)S(1)}, u32[]{:S(2)}, u32[]{:S(2)}) async-start(f32[8,8,1024]{2,1,0:T(8,128)} %get-tuple-element.11), calls=%async_computation | async-start | bytes 524288 | tf_op jit(solution)/shard_map/all_to_all | solution.py:637
  9.0 6.5 %all-to-all-done.points = f32[8,8,1024]{2,1,0:T(8,128)S(1)} async-done(((f32[8,8,1024]{2,1,0:T(8,128)}), f32[8,8,1024]{2,1,0:T(8,128)S(1)}, u32[]{:S(2)}, u32[]{:S(2)}) %all-to-all-start) | async-done | bytes 262176 | tf_op jit(solution)/shard_map/all_to_all | solution.py:637
  15.5 0.0 copy-start
  15.5 0.7 copy-done
  16.2 0.1 slice.3
  16.3 0.1 convert_element_type.7
  16.4 0.6 pad_add_fusion.meta
  17.0 16.9 %shard_map.114 = (f32[16,784,128]{2,1,0:T(8,128)}, f32[64,8,128]{2,1,0:T(8,128)}) custom-call(s32[66]{0:T(128)} %pad_add_fusion.meta, f32[8,8,1024]{2,1,0:T(8,128)} %copy-done, bf16[8,2,256,256]{3,2,1,0:T(8,128)(2,1)} %constant.23.clone.far_table), custom_call_target="tpu_custom_call" | custom-call | bytes 40000000 | tf_op jit(solution)/shard_map/pallas_call | solution.py:649
  34.0 80.1 %all_to_all.30.far_received = f32[16,784,128]{2,1,0:T(8,128)} all-to-all(f32[16,784,128]{2,1,0:T(8,128)} %get-tuple-element.13), channel_id=1, replica_groups=mesh['row'=16,'col'=8] {'row'}, dimensions={0} | all-to-all | bytes 12845056 | tf_op jit(solution)/shard_map/all_to_all | solution.py:628
  114.0 24.0 %shard_map.115 = (f32[2,3,4,64,1024]{4,3,2,1,0:T(8,128)}, f32[16,784,128]{2,1,0:T(8,128)}, f32[8,128]{1,0:T(8,128)}) custom-call(s32[66]{0:T(128)} %pad_add_fusion.meta, f32[16,784,128]{2,1,0:T(8,128)} %all_to_all.30.far_received, bf16[8,2,256,256]{3,2,1,0:T(8,128)(2,1)} %constant.25.clone.far_table, bf16[8,2,256,256]{3,2,1,0:T(8,128)(2,1)} %constant.26.clone.far_back, ...), custom_call_target="tpu_custom_call" | custom-call | bytes 40000000 | tf_op jit(solution)/shard_map/pallas_call | solution.py:666
  138.0 78.3 %all_to_all.31.far_received = f32[16,784,128]{2,1,0:T(8,128)} all-to-all(f32[16,784,128]{2,1,0:T(8,128)} %get-tuple-element.14), channel_id=1, replica_groups=mesh['row'=16,'col'=8] {'row'}, dimensions={0} | all-to-all | bytes 12845056 | tf_op jit(solution)/shard_map/all_to_all | solution.py:628
  216.3 16.1 %shard_map.116 = f32[8,24,128]{2,1,0:T(8,128)} custom-call(s32[66]{0:T(128)} %pad_add_fusion.meta, f32[8,8,1024]{2,1,0:T(8,128)} %copy-done, f32[64,8,128]{2,1,0:T(8,128)} %get-tuple-element.12.depth, f32[16,784,128]{2,1,0:T(8,128)} %all_to_all.31.far_received, bf16[8,2,256,256]{3,2,1,0:T(8,128)(2,1)} %constant.24.clone.far_table), custom_call_target="tpu_custom_call" | custom-call | bytes 40000000 | tf_op jit(solution)/shard_map/pallas_call | solution.py:689
  232.4 12.4 %all_to_all.32.received = f32[8,24,128]{2,1,0:T(8,128)} all-to-all(f32[8,24,128]{2,1,0:T(8,128)} %shard_map.116), channel_id=1, replica_groups=mesh['row'=16,'col'=8] {'col'}, dimensions={0} | all-to-all | bytes 196608 | tf_op jit(solution)/shard_map/all_to_all | solution.py:706
  244.8 1.6 shard_map.117
  246.3 10.2 %all_to_all.33 = f32[16,8,128]{2,1,0:T(8,128)S(1)} all-to-all(f32[16,8,128]{2,1,0:T(8,128)} %get-tuple-element.16), channel_id=1, replica_groups=mesh['row'=16,'col'=8] {'row'}, dimensions={0} | all-to-all | bytes 131072 | tf_op jit(solution)/shard_map/all_to_all | solution.py:710
  256.5 10.0 %all_to_all.34.sums = f32[8,8,128]{2,1,0:T(8,128)} all-to-all(f32[8,8,128]{2,1,0:T(8,128)S(1)} %broadcast_in_dim.2), channel_id=1, replica_groups=mesh['row'=16,'col'=8] {'col'}, dimensions={0} | all-to-all | bytes 65536 | tf_op jit(solution)/shard_map/all_to_all | solution.py:624
  266.5 6.9 %shard_map.118 = (f32[2,3,4,64,1024]{4,3,2,1,0:T(8,128)}, f32[3,1024]{1,0:T(4,128)}) custom-call(f32[8,8,128]{2,1,0:T(8,128)} %all_to_all.34.sums, f32[3,1024]{1,0:T(4,128)} %get-tuple-element.17.residual, f32[3,1024]{1,0:T(4,128)} %get-tuple-element.18.velocity, f32[2,3,4,64,1024]{4,3,2,1,0:T(8,128)} %get-tuple-element.19.gradient), custom_call_target="tpu_custom_call" | custom-call | bytes 13000000 | tf_op jit(solution)/shard_map/pallas_call | solution.py:713
  (3 shorter events, 0.0 us)
Async XLA Ops:
  2.2 13.3 %all-to-all-start = ((f32[8,8,1024]{2,1,0:T(8,128)}), f32[8,8,1024]{2,1,0:T(8,128)S(1)}, u32[]{:S(2)}, u32[]{:S(2)}) async-start(f32[8,8,1024]{2,1,0:T(8,128)} %get-tuple-element.11), calls=%async_computation | async-start | bytes 524288 | tf_op jit(solution)/shard_map/all_to_all | solution.py:637
  15.5 0.7 copy-start

commit v5 on v4

--- a/solution.py
+++ b/solution.py
@@ -18,11 +18,12 @@
 F32 = jnp.float32
 BF16 = jnp.bfloat16
 VMEM_LIMIT = 64 * 1024 * 1024
+LIM_A = 44 * 1024 * 1024
+LIM_X = 36 * 1024 * 1024
 VMEM = pl.BlockSpec(memory_space=pltpu.VMEM)
 SMEM = pl.BlockSpec(memory_space=pltpu.SMEM)
 ANY = pl.BlockSpec(memory_space=pl.ANY)
 TABLE = pltpu.VMEM((8, 2, 256, 256), BF16)
-BLOCKS = pltpu.VMEM((16, 784, 128), F32)
 
 
 def halves(table):
@@ -197,14 +198,10 @@
 
 
 def spread_kernel(
-    meta, points, far_table, far_out, depth, field, parts, windows, table, out, table_done, out_done
+    meta, points, far_table, out, depth, field, parts, windows, table, table_done
 ):
     def table_copy(k):
         return pltpu.make_async_copy(far_table.at[k], table.at[k], table_done.at[k])
-
-    def out_copy(k):
-        at = pl.ds(2 * k, 2)
-        return pltpu.make_async_copy(out.at[at], far_out.at[at], out_done.at[k])
 
     for k in range(8):
         table_copy(k).start()
@@ -284,31 +281,17 @@
                     + [jnp.zeros((2, 128), F32)],
                     0,
                 )
-        out_copy(k).start()
         return carry
 
     lax.fori_loop(0, 8, inner, 0)
-    for k in range(8):
-        out_copy(k).wait()
 
 
 def spectrum_kernel(
-    meta, far_received, far_table, far_back, edge_table, edge_stack, far_spectrum, far_out, norm,
-    received, out, spectrum, parts, back, edge_sum, table, table_back,
-    received_done, out_done, spectrum_done, table_done, back_done,
+    meta, received, far_table, far_back, edge_table, edge_stack, far_spectrum, out, norm,
+    spectrum, parts, back, edge_sum, table, table_back,
+    spectrum_done, table_done, back_done,
 ):
     row = meta[64]
-
-    def place(p, c):
-        return pl.ds(392 * p + 128 * c, 128 if c < 3 else 8)
-
-    def received_copy(p, c):
-        at = place(p, c)
-        return pltpu.make_async_copy(far_received.at[:, at], received.at[:, at], received_done.at[4 * p + c])
-
-    def out_copy(p, c):
-        at = place(p, c)
-        return pltpu.make_async_copy(out.at[:, at], far_out.at[:, at], out_done.at[4 * p + c])
 
     def spectrum_copy(p, part):
         to = far_spectrum.at[part, :, pl.ds(2 * p, 2)]
@@ -320,13 +303,9 @@
     def back_copy(k):
         return pltpu.make_async_copy(far_back.at[k], table_back.at[k], back_done.at[k])
 
-    for c in (3, 0, 1, 2):
-        received_copy(0, c).start()
     for k in range(8):
         table_copy(k).start()
         back_copy(k).start()
-    for c in (3, 0, 1, 2):
-        received_copy(1, c).start()
 
     index_y = 8 * (64 * (row % 2) + lax.broadcasted_iota(jnp.int32, (64, 128), 0)) + row // 2
     lane_x = lax.broadcasted_iota(jnp.int32, (64, 128), 1)
@@ -349,9 +328,7 @@
             return carry
 
         for c in range(3):
-            received_copy(p, c).wait()
             lax.fori_loop(0, 8, functools.partial(outer, c), 0, unroll=8)
-        received_copy(p, 3).wait()
         columns = []
         for c in range(3):
             at = base + 384 + 2 * c
@@ -434,36 +411,25 @@
             out[s, base + 384 : base + 392] = jnp.concatenate(
                 [turned[c][2 * s : 2 * s + 2] for c in range(3)] + [jnp.zeros((2, 128), F32)], 0
             )
-        out_copy(p, 3).start()
         for c in range(3):
             lax.fori_loop(0, 8, functools.partial(last, c), 0, unroll=8)
-            out_copy(p, c).start()
     norm[...] = jnp.sum(sums.reshape(8, 8, 128), axis=0)
     for p in range(2):
         for part in range(2):
             spectrum_copy(p, part).wait()
-        for c in range(4):
-            out_copy(p, c).wait()
 
 
 def gather_kernel(
-    meta, points, depth, far_received, far_table, out,
-    field_high, field_low, parts, edge, windows, table, received, table_done, received_done,
+    meta, points, depth, received, far_table, out, field_high, field_low, parts, edge, windows, table, table_done
 ):
     def table_copy(k):
         return pltpu.make_async_copy(far_table.at[k], table.at[k], table_done.at[k])
 
-    def received_copy(k):
-        at = pl.ds(2 * k, 2)
-        return pltpu.make_async_copy(far_received.at[at], received.at[at], received_done.at[k])
-
     for k in range(8):
         table_copy(k).start()
-        received_copy(k).start()
 
     def inner(k, carry):
         table_copy(k).wait()
-        received_copy(k).wait()
         columns = []
         for p in range(2):
             for c in range(3):
@@ -591,7 +557,7 @@
         store(i).wait()
 
 
-def call(kernel, outs, specs, scratch=(), traffic=0, out_specs=VMEM):
+def call(kernel, outs, specs, scratch=(), traffic=0, out_specs=VMEM, limit=VMEM_LIMIT):
     return pl.pallas_call(
         kernel,
         out_shape=outs,
@@ -599,7 +565,7 @@
         out_specs=out_specs,
         scratch_shapes=list(scratch),
         cost_estimate=pl.CostEstimate(flops=0, bytes_accessed=int(traffic), transcendentals=0),
-        compiler_params=pltpu.CompilerParams(vmem_limit_bytes=VMEM_LIMIT),
+        compiler_params=pltpu.CompilerParams(vmem_limit_bytes=limit),
     )
 
 
@@ -648,48 +614,44 @@
     eight = pltpu.SemaphoreType.DMA((8,))
     sent, depth = call(
         spread_kernel,
-        (shape(16, 784, 128), shape(64, 8, 128)),
+        (near_shape(16, 784, 128), shape(64, 8, 128)),
         [SMEM, VMEM, ANY],
         [
             pltpu.VMEM((3, 1032, 512), F32),
             pltpu.VMEM((8, 256, 768), F32),
             pltpu.VMEM((4, 24, 1024), F32),
             TABLE,
-            BLOCKS,
-            eight,
             eight,
         ],
         40e6,
-        (ANY, VMEM),
+        (VMEM, VMEM),
+        LIM_A,
     )(meta, points, forward_y)
     received = exchange(sent)
     spectrum, sent, norm = call(
         spectrum_kernel,
-        (shape(2, 3, 4, 64, 1024), shape(16, 784, 128), shape(8, 128)),
-        [SMEM, ANY, ANY, ANY, VMEM, VMEM],
+        (shape(2, 3, 4, 64, 1024), near_shape(16, 784, 128), shape(8, 128)),
+        [SMEM, VMEM, ANY, ANY, VMEM, VMEM],
         [
-            BLOCKS,
-            BLOCKS,
             pltpu.VMEM((2, 2, 3, 2, 64, 1024), F32),
             pltpu.VMEM((8, 384, 256), F32),
             pltpu.VMEM((8, 384, 256), F32),
             pltpu.VMEM((384, 128), F32),
             TABLE,
             TABLE,
-            eight,
-            eight,
             pltpu.SemaphoreType.DMA((4,)),
             eight,
             eight,
         ],
         40e6,
-        (ANY, ANY, VMEM),
-    )(meta, received, forward_x, inverse_x, jnp.asarray(edge_table), jnp.asarray(stacked(edge_table)))
+        (ANY, VMEM, VMEM),
+        LIM_X,
+    )(meta, near(received), forward_x, inverse_x, jnp.asarray(edge_table), jnp.asarray(stacked(edge_table)))
     received = exchange(sent)
     velocity = call(
         gather_kernel,
         shape(8, 24, 128),
-        [SMEM, VMEM, VMEM, ANY, ANY],
+        [SMEM, VMEM, VMEM, VMEM, ANY],
         [
             pltpu.VMEM((3, 1040, 512), BF16),
             pltpu.VMEM((3, 1040, 512), BF16),
@@ -697,12 +659,12 @@
             pltpu.VMEM((8, 12, 256), F32),
             pltpu.VMEM((4, 24, 1024), F32),
             TABLE,
-            BLOCKS,
-            eight,
             eight,
         ],
         40e6,
-    )(meta, points, depth, received, inverse_y)
+        VMEM,
+        LIM_A,
+    )(meta, points, depth, near(received), inverse_y)
     velocity = lax.all_to_all(velocity, "col", 0, 0, tiled=True)
     velocity, sums = call(sums_kernel, (shape(3, 1024), shape(16, 8, 128)), [SMEM] + [VMEM] * 2, traffic=1e6, out_specs=(VMEM, VMEM))(
         block_count, velocity, norm

time: 274 us -> 262 us (0.956)
  Pallas kernels: 67 us -> 57.9 us
  blocking collectives: 191 us -> 187 us
    pallas_call x3, Pallas kernels: 57 us -> 47.9 us  [the longest x1 18.9 us: body(): call(spectrum_kernel, (shape(2, 3, 4, 64, 1024), near_shape(16, 784, 128)...]
where the time goes in v5:
time: 262 us; the launch traced here: 261 us
  blocking collectives  187 us (71%)
  Pallas kernels  57.9 us (22%)
  starting transfers between devices  6.81 us (3%)
  waiting for transfers between devices  6.5 us (2%)
    all_to_all x2, blocking collectives, exchange(): return lax.all_to_all(value, 'row', 0, 0, tiled=True)  156 us
    pallas_call x1, Pallas kernels, body(): call(spectrum_kernel, (shape(2, 3, 4, 64, 1024), near_shape(16, 784, 128)...  18.9 us
    pallas_call x1, Pallas kernels, body(): call(spread_kernel, (near_shape(16, 784, 128), shape(64, 8, 128)), [SMEM,...  15 us
    pallas_call x1, Pallas kernels, body(): call(gather_kernel, shape(8, 24, 128), [SMEM, VMEM, VMEM, VMEM, ANY], [pl...  13.9 us
    all_to_all x1, blocking collectives, body(): velocity = lax.all_to_all(velocity, 'col', 0, 0, tiled=True)  11.7 us
    all_to_all x1, blocking collectives, spread_out(): lax.all_to_all(jnp.broadcast_to(value[None], (count,) + value.shape), axi...  10 us
    all_to_all x1, blocking collectives, body(): sums = lax.all_to_all(sums, 'row', 0, 0, tiled=True)  9.94 us
    pallas_call x1, Pallas kernels, body(): call(final_kernel, (shape(2, 3, 4, 64, 1024), shape(3, 1024)), [VMEM, VME...  6.88 us
  transfers between devices with their start and end apart: 1, of which 1 were waited for; matrix products, arithmetic and copies ran while one was open for 0% of the time, Pallas kernels for 0%

profile of v5, /device:TPU:1, one launch (start us, length us, event | category | flops | bytes accessed | tf_op | source)
XLA Modules:
  0.0 261.3 jit_solution(13985615377552180769)
XLA Ops:
  0.6 1.5 shard_map.113
  2.2 6.8 %all-to-all-start = ((f32[8,8,1024]{2,1,0:T(8,128)}), f32[8,8,1024]{2,1,0:T(8,128)S(1)}, u32[]{:S(2)}, u32[]{:S(2)}) async-start(f32[8,8,1024]{2,1,0:T(8,128)} %get-tuple-element.11), calls=%async_computation | async-start | bytes 524288 | tf_op jit(solution)/shard_map/all_to_all | solution.py:603
  9.0 6.5 %all-to-all-done.points = f32[8,8,1024]{2,1,0:T(8,128)S(1)} async-done(((f32[8,8,1024]{2,1,0:T(8,128)}), f32[8,8,1024]{2,1,0:T(8,128)S(1)}, u32[]{:S(2)}, u32[]{:S(2)}) %all-to-all-start) | async-done | bytes 262176 | tf_op jit(solution)/shard_map/all_to_all | solution.py:603
  15.5 0.1 slice.3
  15.6 0.1 convert_element_type.7
  15.7 0.1 pad_add_fusion.meta
  15.8 0.0 copy-start
  15.8 1.6 copy-done
  17.4 15.0 %shard_map.114 = (f32[16,784,128]{2,1,0:T(8,128)S(1)}, f32[64,8,128]{2,1,0:T(8,128)S(1)}) custom-call(s32[66]{0:T(128)S(1)} %pad_add_fusion.meta, f32[8,8,1024]{2,1,0:T(8,128)S(1)} %all-to-all-done.points, bf16[8,2,256,256]{3,2,1,0:T(8,128)(2,1)S(1)} %copy-done), custom_call_target="tpu_custom_call" | custom-call | bytes 40000000 | tf_op jit(solution)/shard_map/pallas_call | solution.py:615
  32.4 0.0 copy-start.2
  32.4 0.0 copy-start.3
  32.4 0.0 copy-start.4
  32.5 0.0 copy-start.5
  32.5 80.0 %all_to_all.30.received = f32[16,784,128]{2,1,0:T(8,128)S(1)} all-to-all(f32[16,784,128]{2,1,0:T(8,128)S(1)} %get-tuple-element.13), channel_id=1, replica_groups=mesh['row'=16,'col'=8] {'row'}, dimensions={0} | all-to-all | bytes 12845056 | tf_op jit(solution)/shard_map/all_to_all | solution.py:594
  112.5 0.0 copy-done.2
  112.5 0.0 copy-done.3
  112.5 0.0 copy-done.4
  112.5 0.0 copy-done.5
  112.5 18.9 %shard_map.115 = (f32[2,3,4,64,1024]{4,3,2,1,0:T(8,128)}, f32[16,784,128]{2,1,0:T(8,128)S(1)}, f32[8,128]{1,0:T(8,128)S(1)}) custom-call(s32[66]{0:T(128)S(1)} %pad_add_fusion.meta, f32[16,784,128]{2,1,0:T(8,128)S(1)} %all_to_all.30.received, bf16[8,2,256,256]{3,2,1,0:T(8,128)(2,1)S(1)} %copy-done.3, bf16[8,2,256,256]{3,2,1,0:T(8,128)(2,1)S(1)} %copy-done.2, ...), custom_call_target="tpu_custom_call" | custom-call | bytes 40000000 | tf_op jit(solution)/shard_map/pallas_call | solution.py:631
  131.4 0.0 copy-start.6
  131.4 0.0 copy-start.1
  131.5 75.7 %all_to_all.31.received = f32[16,784,128]{2,1,0:T(8,128)S(1)} all-to-all(f32[16,784,128]{2,1,0:T(8,128)S(1)} %get-tuple-element.14), channel_id=1, replica_groups=mesh['row'=16,'col'=8] {'row'}, dimensions={0} | all-to-all | bytes 12845056 | tf_op jit(solution)/shard_map/all_to_all | solution.py:594
  207.1 0.0 copy-done.6
  207.1 0.0 copy-done.1
  207.1 13.9 %shard_map.116 = f32[8,24,128]{2,1,0:T(8,128)S(1)} custom-call(s32[66]{0:T(128)S(1)} %pad_add_fusion.meta, f32[8,8,1024]{2,1,0:T(8,128)S(1)} %all-to-all-done.points, f32[64,8,128]{2,1,0:T(8,128)S(1)} %get-tuple-element.12.depth, f32[16,784,128]{2,1,0:T(8,128)S(1)} %all_to_all.31.received, bf16[8,2,256,256]{3,2,1,0:T(8,128)(2,1)S(1)} %copy-done.1), custom_call_target="tpu_custom_call" | custom-call | bytes 40000000 | tf_op jit(solution)/shard_map/pallas_call | solution.py:651
  221.1 11.7 %all_to_all.32.received = f32[8,24,128]{2,1,0:T(8,128)} all-to-all(f32[8,24,128]{2,1,0:T(8,128)S(1)} %shard_map.116), channel_id=1, replica_groups=mesh['row'=16,'col'=8] {'col'}, dimensions={0} | all-to-all | bytes 196608 | tf_op jit(solution)/shard_map/all_to_all | solution.py:668
  232.7 1.6 shard_map.117
  234.3 9.9 %all_to_all.33 = f32[16,8,128]{2,1,0:T(8,128)S(1)} all-to-all(f32[16,8,128]{2,1,0:T(8,128)} %get-tuple-element.16), channel_id=1, replica_groups=mesh['row'=16,'col'=8] {'row'}, dimensions={0} | all-to-all | bytes 131072 | tf_op jit(solution)/shard_map/all_to_all | solution.py:672
  244.3 10.0 %all_to_all.34.sums = f32[8,8,128]{2,1,0:T(8,128)} all-to-all(f32[8,8,128]{2,1,0:T(8,128)S(1)} %broadcast_in_dim.2), channel_id=1, replica_groups=mesh['row'=16,'col'=8] {'col'}, dimensions={0} | all-to-all | bytes 65536 | tf_op jit(solution)/shard_map/all_to_all | solution.py:590
  254.3 6.9 %shard_map.118 = (f32[2,3,4,64,1024]{4,3,2,1,0:T(8,128)}, f32[3,1024]{1,0:T(4,128)}) custom-call(f32[8,8,128]{2,1,0:T(8,128)} %all_to_all.34.sums, f32[3,1024]{1,0:T(4,128)} %get-tuple-element.17.residual, f32[3,1024]{1,0:T(4,128)} %get-tuple-element.18.velocity, f32[2,3,4,64,1024]{4,3,2,1,0:T(8,128)} %get-tuple-element.19.gradient), custom_call_target="tpu_custom_call" | custom-call | bytes 13000000 | tf_op jit(solution)/shard_map/pallas_call | solution.py:675
  (3 shorter events, 0.0 us)
Async XLA Ops:
  2.2 13.3 %all-to-all-start = ((f32[8,8,1024]{2,1,0:T(8,128)}), f32[8,8,1024]{2,1,0:T(8,128)S(1)}, u32[]{:S(2)}, u32[]{:S(2)}) async-start(f32[8,8,1024]{2,1,0:T(8,128)} %get-tuple-element.11), calls=%async_computation | async-start | bytes 524288 | tf_op jit(solution)/shard_map/all_to_all | solution.py:603
  15.8 1.6 copy-start
  32.4 80.1 %copy-start.2 = (bf16[8,2,256,256]{3,2,1,0:T(8,128)(2,1)S(1)}, bf16[8,2,256,256]{3,2,1,0:T(8,128)(2,1)}, u32[]{:S(2)}) copy-start(bf16[8,2,256,256]{3,2,1,0:T(8,128)(2,1)} %constant.26.clone.far_back) | copy-start | bytes 6291460
  32.4 80.1 %copy-start.3 = (bf16[8,2,256,256]{3,2,1,0:T(8,128)(2,1)S(1)}, bf16[8,2,256,256]{3,2,1,0:T(8,128)(2,1)}, u32[]{:S(2)}) copy-start(bf16[8,2,256,256]{3,2,1,0:T(8,128)(2,1)} %constant.25.clone.far_table) | copy-start | bytes 6291460
  32.4 80.1 %copy-start.4 = (bf16[8,2,128,256]{3,2,1,0:T(8,128)(2,1)S(1)}, bf16[8,2,128,256]{3,2,1,0:T(8,128)(2,1)}, u32[]{:S(2)}) copy-start(bf16[8,2,128,256]{3,2,1,0:T(8,128)(2,1)} %constant.27.clone.edge_table) | copy-start | bytes 3145732
  32.5 80.1 %copy-start.5 = (bf16[8,128,256]{2,1,0:T(8,128)(2,1)S(1)}, bf16[8,128,256]{2,1,0:T(8,128)(2,1)}, u32[]{:S(2)}) copy-start(bf16[8,128,256]{2,1,0:T(8,128)(2,1)} %constant.28.clone.edge_stack) | copy-start | bytes 1572868
  131.4 75.7 %copy-start.6 = (f32[8,128]{1,0:T(8,128)}, f32[8,128]{1,0:T(8,128)S(1)}, u32[]{:S(2)}) copy-start(f32[8,128]{1,0:T(8,128)S(1)} %get-tuple-element.15.norms) | copy-start | bytes 12292
  131.4 75.7 %copy-start.1 = (bf16[8,2,256,256]{3,2,1,0:T(8,128)(2,1)S(1)}, bf16[8,2,256,256]{3,2,1,0:T(8,128)(2,1)}, u32[]{:S(2)}) copy-start(bf16[8,2,256,256]{3,2,1,0:T(8,128)(2,1)} %constant.24.clone.far_table) | copy-start | bytes 6291460
